TPU v7x, 128 devices: a whole 4x4x4 slice. The times are simulated.
128 devices in a mesh: crest: 16 (over x, y), section: 8 (over z, core).
Axes of the slice: x: 4, y: 4, z: 4, core: 2. Of those that a mesh axis runs over, the one named last changes fastest.
Arguments:
- pressure_head: float32 [64, 256, 256], P('crest', 'section'), may hold values from -12 to 12
- zone_ids: int32 [64, 256, 256], P('crest', 'section'), may hold values from 0 to 7
- retention_alpha: float32 [8], replicated, may hold values from 0.5 to 4
- retention_exponent: float32 [8], replicated, may hold values from 1.4 to 2.6
- conductivity: float32 [8], replicated, may hold values from 0.1 to 1
- sent_columns: int32 [128, 128, 64], P(('crest', 'section')), may hold values from 0 to 127
- displacement: float32 [3, 131072], P(None, ('crest', 'section')), may hold values from -0.12 to 0.12
- stress_old: float32 [8, 6, 131072], P(None, None, ('crest', 'section')), may hold values from -6 to 6
- connectivity: int32 [8, 131072], P(None, ('crest', 'section')), may hold values from 0 to 1535, as said below
- shared_nodes: int32 [65536], P(('crest', 'section')), may hold values from 0 to 1023, as said below
- element_zone: int32 [131072], P(('crest', 'section')), may hold values from 0 to 7
- element_slot: int32 [131072], P(('crest', 'section')), may hold values from 0 to 8191
- element_depth: int32 [131072], P(('crest', 'section')), may hold values from 0 to 15
- cohesion: float32 [8], replicated, may hold values from 0.2 to 2
- friction: float32 [8], replicated, may hold values from 0.3 to 0.9
Outputs:
- head_out: float32 [64, 256, 256], P('crest', 'section')
- stress_new: float32 [8, 6, 131072], P(None, None, ('crest', 'section'))
- plastic_release: float32 [8, 131072], P(None, ('crest', 'section'))
- node_forces: float32 [3, 131072], P(None, ('crest', 'section'))
Inputs may be any that keep to these rules, and one draw needn't show every extreme that they name: `connectivity`: entries below 1024 are the partition's own nodes; entry 1024 + g names ghost g, the g-th entry of the next partition's shared list; the last partition uses no ghosts. `shared_nodes`: the 512 entries of a partition are distinct nodes of it.
All inputs are finite; a program needn't handle non-finite values.
Results may differ from a plain program's by a relative error of at most 0.0003.
Values sent between devices are 32-bit elements; how exact they have to be, the bound alone decides.
No kernel may reach another device: no remote copies, remote signals or barrier semaphores. Data moves between devices by JAX's collectives and lax.ppermute only.
A program may use at most 64 MiB of HBM per device.

v0:
```python
import jax
import jax.numpy as jnp
import numpy as np
from jax import lax
from jax.sharding import PartitionSpec as P

BAND = 16
SWEEPS = 3


STORAGE = 0.5
THETA_GAP = 0.35
TIME_STEP = 0.05
REDUCTION = 1.4
YOUNG = 200.0
POISSON = 0.3
NEIGHBOURS = (
    (1, 0, 0, 0.0),
    (-1, 0, 0, 0.0),
    (0, 1, 0, 0.0),
    (0, -1, 0, 0.0),
    (0, 0, 1, 1.0),
    (0, 0, -1, -1.0),
)


def extended_2(block, sides, width):
    for axis, dim in sides:
        count = lax.axis_size(axis)
        forward = [(i, i + 1) for i in range(count - 1)]
        backward = [(target, source) for source, target in forward]
        low = lax.ppermute(
            lax.slice_in_dim(block, block.shape[dim] - width, None, axis=dim), axis, forward
        )
        high = lax.ppermute(lax.slice_in_dim(block, 0, width, axis=dim), axis, backward)
        block = jnp.concatenate([low, block, high], axis=dim)
    return block


def from_behind(shard, axis, by):
    devices = lax.axis_size(axis)
    pairs = [(i, i + by) for i in range(devices) if 0 <= i + by < devices]
    return lax.ppermute(shard, axis, pairs)


def corner_signs(index):
    return (2 * (index & 1) - 1, 2 * (index >> 1 & 1) - 1, 2 * (index >> 2 & 1) - 1)


def strain_matrix():
    matrix = np.zeros((48, 24))
    inv_root = 1.0 / np.sqrt(3.0)
    for gauss_point in range(8):
        gauss = [value * inv_root for value in corner_signs(gauss_point)]
        row_start = 6 * gauss_point
        for node_corner in range(8):
            sign_x, sign_y, sign_z = corner_signs(node_corner)
            grad_x = 0.25 * sign_x * (1 + gauss[1] * sign_y) * (1 + gauss[2] * sign_z)
            grad_y = 0.25 * sign_y * (1 + gauss[0] * sign_x) * (1 + gauss[2] * sign_z)
            grad_z = 0.25 * sign_z * (1 + gauss[0] * sign_x) * (1 + gauss[1] * sign_y)
            matrix[row_start + 0, node_corner] = grad_x
            matrix[row_start + 1, 8 + node_corner] = grad_y
            matrix[row_start + 2, 16 + node_corner] = grad_z
            matrix[row_start + 3, node_corner] = grad_y
            matrix[row_start + 3, 8 + node_corner] = grad_x
            matrix[row_start + 4, 8 + node_corner] = grad_z
            matrix[row_start + 4, 16 + node_corner] = grad_y
            matrix[row_start + 5, 16 + node_corner] = grad_x
            matrix[row_start + 5, node_corner] = grad_z
    return matrix


def zone_field(zones, values):
    result = jnp.zeros(zones.shape, jnp.float32)
    for zone in range(values.shape[0]):
        result = jnp.where(zones == zone, values[zone], result)
    return result


def van_genuchten(head_now, alpha, expo, cond_sat):
    expo_safe = jnp.where(expo > 0, expo, 2.0)
    m_expo = 1.0 - 1.0 / expo_safe
    scaled = alpha * jnp.maximum(-head_now, 0.0)
    power_n = scaled**expo_safe
    saturation = (1.0 + power_n) ** (-m_expo)
    inner = 1.0 - (1.0 - saturation ** (1.0 / m_expo)) ** m_expo
    cond = cond_sat * jnp.sqrt(saturation) * inner * inner
    capacity = STORAGE + THETA_GAP * alpha * expo_safe * m_expo * scaled ** (expo_safe - 1.0) * (
        1.0 + power_n
    ) ** (-m_expo - 1.0)
    return (saturation, cond, capacity)


def sweep_update(head_pad, cond_pad, capacity):
    head_z = jnp.pad(head_pad, ((0, 0), (0, 0), (1, 1)))
    cond_z = jnp.pad(cond_pad, ((0, 0), (0, 0), (1, 1)))
    size_x = head_pad.shape[0] - 2
    size_y = head_pad.shape[1] - 2
    size_z = head_pad.shape[2]
    head_here = head_z[1 : 1 + size_x, 1 : 1 + size_y, 1 : 1 + size_z]
    cond_here = cond_z[1 : 1 + size_x, 1 : 1 + size_y, 1 : 1 + size_z]
    inflow = jnp.zeros_like(head_here)
    for shift_x, shift_y, shift_z, lift in NEIGHBOURS:
        head_there = head_z[
            1 + shift_x : 1 + shift_x + size_x,
            1 + shift_y : 1 + shift_y + size_y,
            1 + shift_z : 1 + shift_z + size_z,
        ]
        cond_there = cond_z[
            1 + shift_x : 1 + shift_x + size_x,
            1 + shift_y : 1 + shift_y + size_y,
            1 + shift_z : 1 + shift_z + size_z,
        ]
        inflow = inflow + jnp.sqrt(cond_here * cond_there) * (head_there - head_here + lift)
    return head_here + TIME_STEP * inflow / capacity


def return_map(strain, stress_old, pore, cohesion_e, friction_e):
    lame_first = YOUNG * POISSON / ((1.0 + POISSON) * (1.0 - 2.0 * POISSON))
    modulus = YOUNG / (2.0 * (1.0 + POISSON))
    volume = strain[:, 0] + strain[:, 1] + strain[:, 2]
    normals = [
        stress_old[:, i] + lame_first * volume + 2.0 * modulus * strain[:, i] + pore
        for i in range(3)
    ]
    shears = [stress_old[:, i] + modulus * strain[:, i] for i in range(3, 6)]
    mean_stress = (normals[0] + normals[1] + normals[2]) / 3.0
    devs = [value - mean_stress for value in normals]
    deviator = jnp.sqrt(
        0.5 * (devs[0] ** 2 + devs[1] ** 2 + devs[2] ** 2)
        + shears[0] ** 2
        + shears[1] ** 2
        + shears[2] ** 2
    )
    tan_red = friction_e / REDUCTION
    cos_red = 1.0 / jnp.sqrt(1.0 + tan_red * tan_red)
    sin_red = tan_red * cos_red
    denom = jnp.sqrt(3.0) * (3.0 - sin_red)
    slope = 6.0 * sin_red / denom
    bound_value = 6.0 * (cohesion_e / REDUCTION) * cos_red / denom
    allow = jnp.maximum(bound_value - slope * mean_stress, 0.0)
    yielded = deviator > allow
    scale = jnp.where(yielded, allow / jnp.where(yielded, deviator, 1.0), 1.0)
    new_parts = [mean_stress + scale * devs[i] - pore for i in range(3)] + [
        scale * shears[i] for i in range(3)
    ]
    return (jnp.stack(new_parts, axis=1), (1.0 - scale) * deviator)


def per_device(
    pressure_head,
    zone_ids,
    retention_alpha,
    retention_exponent,
    conductivity,
    sent_columns,
    displacement,
    stress_old,
    connectivity,
    shared_nodes,
    element_zone,
    element_slot,
    element_depth,
    cohesion,
    friction,
):
    alpha_field = zone_field(zone_ids, retention_alpha)
    expo_field = zone_field(zone_ids, retention_exponent)
    sat_field = zone_field(zone_ids, conductivity)
    head_now = pressure_head
    for sweep in range(SWEEPS):
        saturation, cond, capacity = van_genuchten(head_now, alpha_field, expo_field, sat_field)
        padded = extended_2(jnp.stack([head_now, cond]), (("crest", 1), ("section", 2)), 1)
        head_now = sweep_update(padded[0], padded[1], capacity)
    saturation = van_genuchten(head_now, alpha_field, expo_field, sat_field)[0]
    size_x, size_y, depth = head_now.shape
    band_count = depth // BAND
    band_rows = (saturation * head_now).reshape(size_x * size_y, band_count, BAND)
    wanted = sent_columns[0]
    npart = wanted.shape[0]
    slots = wanted.shape[1]
    band_index = (jnp.arange(npart, dtype=jnp.int32) % band_count)[:, None]
    outgoing = band_rows[wanted, band_index]
    incoming = lax.all_to_all(
        outgoing, ("crest", "section"), split_axis=0, concat_axis=0, tiled=True
    )
    received = incoming.reshape(npart * slots * BAND)
    pore = received[element_slot * BAND + element_depth]
    nodes_dev = displacement.shape[1]
    ghost_count = shared_nodes.shape[0]
    elem_count = connectivity.shape[1]
    node_rows = displacement.T
    ghost_values = from_behind(node_rows[shared_nodes], ("crest", "section"), -1)
    extended = jnp.concatenate([node_rows, ghost_values], axis=0)
    strain_rows = jnp.asarray(strain_matrix(), jnp.float32)
    force_rows = jnp.asarray(strain_matrix().T * 0.125, jnp.float32)
    corner_rows = extended[connectivity]
    elem_disp = jnp.transpose(corner_rows, (2, 0, 1)).reshape(24, elem_count)
    strain = jnp.dot(strain_rows, elem_disp, precision=lax.Precision.HIGHEST).reshape(
        8, 6, elem_count
    )
    cohesion_e = zone_field(element_zone, cohesion)
    friction_e = zone_field(element_zone, friction)
    stress_new, release = return_map(strain, stress_old, pore, cohesion_e, friction_e)
    elem_force = jnp.dot(
        force_rows, stress_new.reshape(48, elem_count), precision=lax.Precision.HIGHEST
    ).reshape(3, 8 * elem_count)
    flat_index = connectivity.reshape(-1)
    local_sum = jax.ops.segment_sum(elem_force.T, flat_index, num_segments=nodes_dev + ghost_count)
    returned = from_behind(local_sum[nodes_dev:], ("crest", "section"), 1)
    node_forces = local_sum[:nodes_dev].at[shared_nodes].add(returned)
    return (head_now, stress_new, release, node_forces.T)


def solution(mesh):
    return jax.shard_map(
        per_device,
        mesh=mesh,
        in_specs=(
            P("crest", "section", None),
            P("crest", "section", None),
            P(),
            P(),
            P(),
            P(("crest", "section"), None, None),
            P(None, ("crest", "section")),
            P(None, None, ("crest", "section")),
            P(None, ("crest", "section")),
            P(("crest", "section")),
            P(("crest", "section")),
            P(("crest", "section")),
            P(("crest", "section")),
            P(),
            P(),
        ),
        out_specs=(
            P("crest", "section", None),
            P(None, None, ("crest", "section")),
            P(None, ("crest", "section")),
            P(None, ("crest", "section")),
        ),
        check_vma=False,
    )
```

profile of v0, /device:TPU:2, one launch (start us, length us, event | category | flops | bytes accessed | tf_op | source)
XLA Modules:
  0.0 306.4 jit_solution(2419758170193778723)
XLA Ops:
  0.7 1.1 broadcast_compare_fusion
  1.8 1.6 fusion.106
  3.4 1.6 fusion.108
  5.0 1.6 fusion.107
  6.6 16.9 %fusion.3 = (f32[1,4,32,256]{3,2,1,0:T(8,128)S(1)}, f32[4,32,256]{2,1,0:T(8,128)S(1)}, f32[4,32,256]{2,1,0:T(8,128)S(1)}, f32[4,32,256]{2,1,0:T(8,128)S(1)}) fusion(f32[4,32,256]{2,1,0:T(8,128)} %param.17, pred[4,32,256]{2,1,0:T(8,128)(4,1)S(1)} %get-tuple-element.79, pred[4,32,256]{2,1,0:T(8,128)(4,1)S(1)} %get-tuple-element.78, ...), kind=kLoop, calls=%fused_computation.35 | loop fusion | flops 1277952 | bytes 917600 | tf_op jit(solution)/shard_map/stack | solution.py:173
  23.5 0.8 pad_maximum_fusion.9
  24.3 3.5 %collective-permute-start = (f32[2,1,32,256]{3,2,1,0:T(8,128)S(1)}, f32[2,1,32,256]{3,2,1,0:T(8,128)S(1)}, u32[]{:S(2)}, u32[]{:S(2)}) collective-permute-start(f32[2,1,32,256]{3,2,1,0:T(8,128)S(1)} %get-tuple-element.71), channel_id=1, source_target_pairs={{0,8},{8,16},{16,24},{24,32},{32,40},{40,48},{48,56},{56,64},{64,7... | collective-permute-start | bytes 196616 | tf_op jit(solution)/shard_map/ppermute | solution.py:32
  27.8 4.5 %collective-permute-start.1 = (f32[2,1,32,256]{3,2,1,0:T(8,128)S(1)}, f32[2,1,32,256]{3,2,1,0:T(8,128)S(1)}, u32[]{:S(2)}, u32[]{:S(2)}) collective-permute-start(f32[2,1,32,256]{3,2,1,0:T(8,128)S(1)} %get-tuple-element.72), channel_id=1, source_target_pairs={{8,0},{16,8},{24,16},{32,24},{40,32},{48,40},{56,48},{64,56},{72,6... | collective-permute-start | bytes 196616 | tf_op jit(solution)/shard_map/ppermute | solution.py:35
  32.3 0.7 compare_select_fusion.4
  33.0 0.9 copy.115
  33.9 0.7 fusion.95
  34.6 1.0 gather_fusion
  35.7 5.1 %collective-permute-start.12 = (f32[512,3]{1,0:T(8,128)S(1)}, f32[512,3]{1,0:T(8,128)S(1)}, u32[]{:S(2)}, u32[]{:S(2)}) collective-permute-start(f32[512,3]{1,0:T(8,128)S(1)} %gather_fusion), channel_id=1, source_target_pairs={{1,0},{2,1},{3,2},{4,3},{5,4},{6,5},{7,6},{8,7},{9,8},{10,9},{11,1... | collective-permute-start | bytes 18440 | tf_op jit(solution)/shard_map/ppermute | solution.py:43
  41.0 1.3 collective-permute-start.2
  42.3 1.3 collective-permute-start.3
  43.6 1.7 collective-permute-done.3
  45.4 2.0 fusion.4
  47.5 3.1 collective-permute-start.4
  50.5 4.9 %collective-permute-start.5 = (f32[2,1,32,256]{3,2,1,0:T(8,128)S(1)}, f32[2,1,32,256]{3,2,1,0:T(8,128)S(1)}, u32[]{:S(2)}, u32[]{:S(2)}) collective-permute-start(f32[2,1,32,256]{3,2,1,0:T(8,128)S(1)} %get-tuple-element.70), channel_id=1, source_target_pairs={{8,0},{16,8},{24,16},{32,24},{40,32},{48,40},{56,48},{64,56},{72,6... | collective-permute-start | bytes 196616 | tf_op jit(solution)/shard_map/ppermute | solution.py:35
  56.1 1.7 collective-permute-done.5
  57.8 2.2 collective-permute-start.6
  60.0 1.3 collective-permute-start.7
  62.0 1.2 collective-permute-done.7
  63.4 2.0 fusion.5
  65.4 1.9 collective-permute-start.8
  67.3 6.4 %collective-permute-start.9 = (f32[2,1,32,256]{3,2,1,0:T(8,128)S(1)}, f32[2,1,32,256]{3,2,1,0:T(8,128)S(1)}, u32[]{:S(2)}, u32[]{:S(2)}) collective-permute-start(f32[2,1,32,256]{3,2,1,0:T(8,128)S(1)} %get-tuple-element.68), channel_id=1, source_target_pairs={{8,0},{16,8},{24,16},{32,24},{40,32},{48,40},{56,48},{64,56},{72,6... | collective-permute-start | bytes 196616 | tf_op jit(solution)/shard_map/ppermute | solution.py:35
  73.7 10.0 %fusion.96 = (f32[1024]{0:T(1024)S(1)}, pred[1024]{0:T(1024)(128)(4,1)S(1)}, pred[1024]{0:T(1024)(128)(4,1)S(1)}, pred[1024]{0:T(1024)(128)(4,1)S(1)}, pred[1024...) fusion(f32[]{:T(128)} %bitcast.57, f32[]{:T(128)} %bitcast.56, ...), kind=kLoop, calls=%fused_computation.225 | loop fusion | flops 33792 | bytes 16448 | tf_op jit(solution)/shard_map/div | solution.py:140
  83.7 4.1 %collective-permute-start.10 = (f32[2,6,1,256]{3,2,1,0:T(1,128)S(1)}, f32[2,6,1,256]{3,2,1,0:T(1,128)S(1)}, u32[]{:S(2)}, u32[]{:S(2)}) collective-permute-start(f32[2,6,1,256]{3,2,1,0:T(1,128)S(1)} %get-tuple-element.55), channel_id=1, source_target_pairs={{0,1},{1,2},{2,3},{3,4},{4,5},{5,6},{6,7},{8,9},{9,10},{10,11},{11... | collective-permute-start | bytes 36872 | tf_op jit(solution)/shard_map/ppermute | solution.py:32
  87.8 1.3 collective-permute-start.11
  89.1 5.1 %divide_multiply_fusion = f32[1024]{0:T(1024)S(1)} fusion(pred[1024]{0:T(1024)(128)(4,1)S(1)} %get-tuple-element.40, pred[1024]{0:T(1024)(128)(4,1)S(1)} %get-tuple-element.39, pred[1024]{0:T(1024)(128)(4,1)S(1)} %get-tuple-element.38, pred[1024]{0:T(1024)(128)(4,1)S(1)} %get-tuple-element.37, pred[1024]{0:T(1024)(128)(4,1)S(1)} %get-tuple-element.36, ...), kind=kLoop, calls=%fused_computation.223 | loop fusion | flops 17408 | bytes 12320 | tf_op jit(solution)/shard_map/mul | solution.py:141
  94.5 2.1 power_multiply_fusion
  97.0 88.4 %gather_fusion.2 = f32[8192,16]{1,0:T(8,128)} fusion(f32[128,16,16]{2,1,0:T(8,128)S(1)} %reshape.295, s32[8192]{0:T(1024)S(1)} %reshape.259), kind=kCustom, calls=%fused_computation.2 | custom fusion | bytes 1114112 | tf_op jit(solution)/shard_map/gather | solution.py:183
  185.4 2.8 copy.123
  188.2 1.5 reshape.298
  189.6 9.9 %all-to-all-start = ((f32[128,1,1024]{2,1,0:T(1,128)}), f32[128,1,1024]{2,1,0:T(1,128)S(1)}, u32[]{:S(2)}, u32[]{:S(2)}) async-start(f32[128,1,1024]{2,1,0:T(1,128)} %reshape.298), calls=%async_computation | async-start | bytes 1048576 | tf_op jit(solution)/shard_map/all_to_all | solution.py:184
  199.6 27.8 %gather_fusion.1 = f32[8192,3]{1,0:T(8,128)} fusion(f32[1536,3]{1,0:T(8,128)S(1)} %pad_maximum_fusion, s32[8192]{0:T(1024)S(1)} %bitcast_clamp_fusion), kind=kCustom, calls=%fused_computation.1 | custom fusion | bytes 229376 | tf_op jit(solution)/shard_map/gather | solution.py:197
  227.3 2.9 copy.116
  231.2 1.9 reduce
  233.4 2.7 copy.124
  236.1 3.3 %reshape.237 = f32[131072]{0:T(1024)S(1)} reshape(f32[128,64,16]{2,1,0:T(8,128)} %copy.124) | data formatting | bytes 1048576 | tf_op jit(solution)/shard_map/reshape | solution.py:187
  239.4 6.2 %gather_fusion.3 = f32[1024]{0:T(1024)S(1)} fusion(f32[131072]{0:T(1024)S(1)} %reshape.237, s32[1024]{0:T(1024)S(1)} %get-tuple-element.121), kind=kCustom, calls=%fused_computation.3 | custom fusion | bytes 12288 | tf_op jit(solution)/shard_map/gather | solution.py:188
  245.6 0.7 subtract_multiply_fusion
  247.0 2.7 copy.129
  249.6 40.5 %scatter_custom_fusion = f32[1536,3]{1,0:T(8,128)S(1)} fusion(s32[8192]{0:T(1024)S(1)} %bitcast.137, f32[3,8192]{0,1:T(8,128)} %copy.129, f32[]{:T(128)} %constant.40.clone.1), kind=kCustom, calls=%fused_computation.6 | custom fusion | flops 24576 | bytes 116740 | tf_op jit(solution)/shard_map/scatter-add | solution.py:209
  290.2 2.1 collective-permute-start.13
  292.4 9.8 %collective-permute-done.13 = f32[512,3]{1,0:T(8,128)S(1)} collective-permute-done((f32[512,3]{1,0:T(8,128)S(1)}, f32[512,3]{1,0:T(8,128)S(1)}, u32[]{:S(2)}, u32[]{:S(2)}) %collective-permute-start.13) | collective-permute-done | bytes 6176 | tf_op jit(solution)/shard_map/ppermute | solution.py:43
  302.2 3.5 %scatter_fusion = f32[1024,3]{1,0:T(8,128)S(1)} fusion(f32[1024,3]{1,0:T(8,128)S(1)} %slice.539, s32[512]{0:T(512)S(1)} %compare_select_fusion.4, f32[512,3]{1,0:T(8,128)S(1)} %collective-permute-done.13), kind=kCustom, calls=%fused_computation.5 | custom fusion | flops 1536 | bytes 20480 | tf_op jit(solution)/shard_map/scatter-add | solution.py:211
  305.7 0.8 copy.130
  (70 shorter events, 4.3 us)
Async XLA Ops:
  0.6 40.3 %copy-start = (f32[4,32,256]{2,1,0:T(8,128)S(1)}, f32[4,32,256]{2,1,0:T(8,128)}, u32[]{:S(2)}) copy-start(f32[4,32,256]{2,1,0:T(8,128)} %param.17) | copy-start | bytes 393220
  0.6 40.2 %copy-start.4 = (s32[1,128,64]{1,2,0:T(8,128)S(1)}, s32[1,128,64]{1,2,0:T(8,128)}, u32[]{:S(2)}) copy-start(s32[1,128,64]{1,2,0:T(8,128)} %param.22) | copy-start | bytes 98308
  0.7 40.2 %copy-start.3 = (s32[8,1024]{1,0:T(8,128)S(1)}, s32[8,1024]{1,0:T(8,128)}, u32[]{:S(2)}) copy-start(s32[8,1024]{1,0:T(8,128)} %param.25) | copy-start | bytes 98308
  24.3 16.6 %collective-permute-start = (f32[2,1,32,256]{3,2,1,0:T(8,128)S(1)}, f32[2,1,32,256]{3,2,1,0:T(8,128)S(1)}, u32[]{:S(2)}, u32[]{:S(2)}) collective-permute-start(f32[2,1,32,256]{3,2,1,0:T(8,128)S(1)} %get-tuple-element.71), channel_id=1, source_target_pairs={{0,8},{8,16},{16,24},{24,32},{32,40},{40,48},{48,56},{56,64},{64,7... | collective-permute-start | bytes 196616 | tf_op jit(solution)/shard_map/ppermute | solution.py:32
  27.8 13.1 %collective-permute-start.1 = (f32[2,1,32,256]{3,2,1,0:T(8,128)S(1)}, f32[2,1,32,256]{3,2,1,0:T(8,128)S(1)}, u32[]{:S(2)}, u32[]{:S(2)}) collective-permute-start(f32[2,1,32,256]{3,2,1,0:T(8,128)S(1)} %get-tuple-element.72), channel_id=1, source_target_pairs={{8,0},{16,8},{24,16},{32,24},{40,32},{48,40},{56,48},{64,56},{72,6... | collective-permute-start | bytes 196616 | tf_op jit(solution)/shard_map/ppermute | solution.py:35
  33.0 22.5 %copy-start.5 = (f32[8]{0:T(128)S(1)}, f32[8]{0:T(128)}, u32[]{:S(2)}) copy-start(f32[8]{0:T(128)} %param.31) | copy-start | bytes 100
  33.9 27.4 %copy-start.6 = (f32[8]{0:T(128)S(1)}, f32[8]{0:T(128)}, u32[]{:S(2)}) copy-start(f32[8]{0:T(128)} %param.30) | copy-start | bytes 100
  35.7 163.8 %collective-permute-start.12 = (f32[512,3]{1,0:T(8,128)S(1)}, f32[512,3]{1,0:T(8,128)S(1)}, u32[]{:S(2)}, u32[]{:S(2)}) collective-permute-start(f32[512,3]{1,0:T(8,128)S(1)} %gather_fusion), channel_id=1, source_target_pairs={{1,0},{2,1},{3,2},{4,3},{5,4},{6,5},{7,6},{8,7},{9,8},{10,9},{11,1... | collective-permute-start | bytes 18440 | tf_op jit(solution)/shard_map/ppermute | solution.py:43
  41.0 2.6 collective-permute-start.2
  42.3 3.1 %collective-permute-start.3 = (f32[2,6,1,256]{3,2,1,0:T(1,128)S(1)}, f32[2,6,1,256]{3,2,1,0:T(1,128)S(1)}, u32[]{:S(2)}, u32[]{:S(2)}) collective-permute-start(f32[2,6,1,256]{3,2,1,0:T(1,128)S(1)} %get-tuple-element.60), channel_id=1, source_target_pairs={{1,0},{2,1},{3,2},{4,3},{5,4},{6,5},{7,6},{9,8},{10,9},{11,10},{12... | collective-permute-start | bytes 36872 | tf_op jit(solution)/shard_map/ppermute | solution.py:35
  45.4 28.3 %copy-start.9 = (s32[1024]{0:T(1024)S(1)}, s32[1024]{0:T(1024)}, u32[]{:S(2)}) copy-start(s32[1024]{0:T(1024)} %param.27) | copy-start | bytes 12292
  47.5 8.7 %collective-permute-start.4 = (f32[2,1,32,256]{3,2,1,0:T(8,128)S(1)}, f32[2,1,32,256]{3,2,1,0:T(8,128)S(1)}, u32[]{:S(2)}, u32[]{:S(2)}) collective-permute-start(f32[2,1,32,256]{3,2,1,0:T(8,128)S(1)} %get-tuple-element.69), channel_id=1, source_target_pairs={{0,8},{8,16},{16,24},{24,32},{32,40},{40,48},{48,56},{56,64},{64,7... | collective-permute-start | bytes 196616 | tf_op jit(solution)/shard_map/ppermute | solution.py:32
  50.5 7.2 %collective-permute-start.5 = (f32[2,1,32,256]{3,2,1,0:T(8,128)S(1)}, f32[2,1,32,256]{3,2,1,0:T(8,128)S(1)}, u32[]{:S(2)}, u32[]{:S(2)}) collective-permute-start(f32[2,1,32,256]{3,2,1,0:T(8,128)S(1)} %get-tuple-element.70), channel_id=1, source_target_pairs={{8,0},{16,8},{24,16},{32,24},{40,32},{48,40},{56,48},{64,56},{72,6... | collective-permute-start | bytes 196616 | tf_op jit(solution)/shard_map/ppermute | solution.py:35
  57.8 4.2 %collective-permute-start.6 = (f32[2,6,1,256]{3,2,1,0:T(1,128)S(1)}, f32[2,6,1,256]{3,2,1,0:T(1,128)S(1)}, u32[]{:S(2)}, u32[]{:S(2)}) collective-permute-start(f32[2,6,1,256]{3,2,1,0:T(1,128)S(1)} %get-tuple-element.57), channel_id=1, source_target_pairs={{0,1},{1,2},{2,3},{3,4},{4,5},{5,6},{6,7},{8,9},{9,10},{10,11},{11... | collective-permute-start | bytes 36872 | tf_op jit(solution)/shard_map/ppermute | solution.py:32
  60.0 3.2 %collective-permute-start.7 = (f32[2,6,1,256]{3,2,1,0:T(1,128)S(1)}, f32[2,6,1,256]{3,2,1,0:T(1,128)S(1)}, u32[]{:S(2)}, u32[]{:S(2)}) collective-permute-start(f32[2,6,1,256]{3,2,1,0:T(1,128)S(1)} %get-tuple-element.58), channel_id=1, source_target_pairs={{1,0},{2,1},{3,2},{4,3},{5,4},{6,5},{7,6},{9,8},{10,9},{11,10},{12... | collective-permute-start | bytes 36872 | tf_op jit(solution)/shard_map/ppermute | solution.py:35
  65.4 18.3 %collective-permute-start.8 = (f32[2,1,32,256]{3,2,1,0:T(8,128)S(1)}, f32[2,1,32,256]{3,2,1,0:T(8,128)S(1)}, u32[]{:S(2)}, u32[]{:S(2)}) collective-permute-start(f32[2,1,32,256]{3,2,1,0:T(8,128)S(1)} %get-tuple-element.67), channel_id=1, source_target_pairs={{0,8},{8,16},{16,24},{24,32},{32,40},{40,48},{48,56},{56,64},{64,7... | collective-permute-start | bytes 196616 | tf_op jit(solution)/shard_map/ppermute | solution.py:32
  67.3 16.4 %collective-permute-start.9 = (f32[2,1,32,256]{3,2,1,0:T(8,128)S(1)}, f32[2,1,32,256]{3,2,1,0:T(8,128)S(1)}, u32[]{:S(2)}, u32[]{:S(2)}) collective-permute-start(f32[2,1,32,256]{3,2,1,0:T(8,128)S(1)} %get-tuple-element.68), channel_id=1, source_target_pairs={{8,0},{16,8},{24,16},{32,24},{40,32},{48,40},{56,48},{64,56},{72,6... | collective-permute-start | bytes 196616 | tf_op jit(solution)/shard_map/ppermute | solution.py:35
  83.7 10.6 %collective-permute-start.10 = (f32[2,6,1,256]{3,2,1,0:T(1,128)S(1)}, f32[2,6,1,256]{3,2,1,0:T(1,128)S(1)}, u32[]{:S(2)}, u32[]{:S(2)}) collective-permute-start(f32[2,6,1,256]{3,2,1,0:T(1,128)S(1)} %get-tuple-element.55), channel_id=1, source_target_pairs={{0,1},{1,2},{2,3},{3,4},{4,5},{5,6},{6,7},{8,9},{9,10},{10,11},{11... | collective-permute-start | bytes 36872 | tf_op jit(solution)/shard_map/ppermute | solution.py:32
  87.8 6.6 %collective-permute-start.11 = (f32[2,6,1,256]{3,2,1,0:T(1,128)S(1)}, f32[2,6,1,256]{3,2,1,0:T(1,128)S(1)}, u32[]{:S(2)}, u32[]{:S(2)}) collective-permute-start(f32[2,6,1,256]{3,2,1,0:T(1,128)S(1)} %get-tuple-element.56), channel_id=1, source_target_pairs={{1,0},{2,1},{3,2},{4,3},{5,4},{6,5},{7,6},{9,8},{10,9},{11,10},{12... | collective-permute-start | bytes 36872 | tf_op jit(solution)/shard_map/ppermute | solution.py:35
  189.6 41.1 %all-to-all-start = ((f32[128,1,1024]{2,1,0:T(1,128)}), f32[128,1,1024]{2,1,0:T(1,128)S(1)}, u32[]{:S(2)}, u32[]{:S(2)}) async-start(f32[128,1,1024]{2,1,0:T(1,128)} %reshape.298), calls=%async_computation | async-start | bytes 1048576 | tf_op jit(solution)/shard_map/all_to_all | solution.py:184
  227.3 2.9 copy-start.7
  236.1 9.5 %copy-start.1 = (f32[8,6,1024]{2,0,1:T(8,128)S(1)}, f32[8,6,1024]{2,0,1:T(8,128)}, u32[]{:S(2)}) copy-start(f32[8,6,1024]{2,0,1:T(8,128)} %param.24) | copy-start | bytes 589828
  239.4 7.3 %copy-start.8 = (f32[24,48]{1,0:T(8,128)S(1)}, f32[24,48]{1,0:T(8,128)}, u32[]{:S(2)}) copy-start(f32[24,48]{1,0:T(8,128)} %constant.26.clone) | copy-start | bytes 13828
  246.5 43.7 %copy-start.2 = (f32[8,6,1024]{2,0,1:T(8,128)}, f32[8,6,1024]{2,0,1:T(8,128)S(1)}, u32[]{:S(2)}) copy-start(f32[8,6,1024]{2,0,1:T(8,128)S(1)} %multiply_dynamic-update-slice_fusion) | copy-start | bytes 589828
  290.2 11.9 %collective-permute-start.13 = (f32[512,3]{1,0:T(8,128)S(1)}, f32[512,3]{1,0:T(8,128)S(1)}, u32[]{:S(2)}, u32[]{:S(2)}) collective-permute-start(f32[512,3]{1,0:T(8,128)S(1)} %slice.540), channel_id=1, source_target_pairs={{0,1},{1,2},{2,3},{3,4},{4,5},{5,6},{6,7},{7,8},{8,9},{9,10},{10,1... | collective-permute-start | bytes 18440 | tf_op jit(solution)/shard_map/ppermute | solution.py:43
where the time goes:
time: 308 us; the launch traced here: 306 us
  local copies, waits for them, and re-layouts  149 us (48%)
  other arithmetic  88.5 us (29%)
  starting transfers between devices  52.7 us (17%)
  waiting for transfers between devices  14.5 us (5%)
    gather x2, local copies, waits for them, and re-layouts, per_device(): outgoing = band_rows[wanted, band_index]  91.2 us
    scatter-add x1, other arithmetic, per_device(): jax.ops.segment_sum(elem_force.T, flat_index, num_segments=nodes_dev + gh...  40.5 us
    gather x2, local copies, waits for them, and re-layouts, per_device(): corner_rows = extended[connectivity]  30.6 us
    another operation x3, other arithmetic, per_device(): jnp.stack([head_now, cond])  20.9 us
    ppermute x6, starting transfers between devices, extended_2(): lax.ppermute(lax.slice_in_dim(block, 0, width, axis=dim), axis, backward)  19.6 us
    ppermute x6, starting transfers between devices, extended_2(): lax.ppermute(lax.slice_in_dim(block, block.shape[dim] - width, None, axis...  16 us
    div x1, other arithmetic, return_map(): bound_value = 6.0 * (cohesion_e / REDUCTION) * cos_red / denom  9.96 us
    all_to_all x1, starting transfers between devices, per_device(): lax.all_to_all(outgoing, ('crest', 'section'), split_axis=0, concat_axis=...  9.88 us
  transfers between devices with their start and end apart: 15, of which 4 were waited for; matrix products, arithmetic and copies ran while one was open for 49% of the time, Pallas kernels for 0%

commit v1 on v0

v1 whole, which is shorter than its diff:
```python
import jax
import jax.numpy as jnp
import numpy as np
from jax import lax
from jax.experimental import pallas as pl
from jax.experimental.pallas import tpu as pltpu
from jax.sharding import PartitionSpec as P

BAND = 16
SWEEPS = 3
WIDE = 3

STORAGE = 0.5
THETA_GAP = 0.35
TIME_STEP = 0.05
REDUCTION = 1.4
YOUNG = 200.0
POISSON = 0.3

AXES = ("crest", "section")
VMEM_LIMIT = 48 * 1024 * 1024


def corner_signs(index):
    return (2 * (index & 1) - 1, 2 * (index >> 1 & 1) - 1, 2 * (index >> 2 & 1) - 1)


def strain_matrix():
    matrix = np.zeros((48, 24))
    inv_root = 1.0 / np.sqrt(3.0)
    for gauss_point in range(8):
        gauss = [value * inv_root for value in corner_signs(gauss_point)]
        row_start = 6 * gauss_point
        for node_corner in range(8):
            sign_x, sign_y, sign_z = corner_signs(node_corner)
            grad_x = 0.25 * sign_x * (1 + gauss[1] * sign_y) * (1 + gauss[2] * sign_z)
            grad_y = 0.25 * sign_y * (1 + gauss[0] * sign_x) * (1 + gauss[2] * sign_z)
            grad_z = 0.25 * sign_z * (1 + gauss[0] * sign_x) * (1 + gauss[1] * sign_y)
            matrix[row_start + 0, node_corner] = grad_x
            matrix[row_start + 1, 8 + node_corner] = grad_y
            matrix[row_start + 2, 16 + node_corner] = grad_z
            matrix[row_start + 3, node_corner] = grad_y
            matrix[row_start + 3, 8 + node_corner] = grad_x
            matrix[row_start + 4, 8 + node_corner] = grad_z
            matrix[row_start + 4, 16 + node_corner] = grad_y
            matrix[row_start + 5, 16 + node_corner] = grad_x
            matrix[row_start + 5, node_corner] = grad_z
    return matrix


def component_major():
    order = [6 * gauss_point + comp for comp in range(6) for gauss_point in range(8)]
    return strain_matrix()[order]


def take_lanes(row, lanes):
    return jnp.take_along_axis(jnp.broadcast_to(row, lanes.shape), lanes, axis=1, mode="promise_in_bounds")


def pick(values_ref, index, first=0):
    lane = lax.broadcasted_iota(jnp.int32, (8, 128), 1)
    table = jnp.zeros((8, 128), jnp.float32)
    for zone in range(values_ref.shape[0]):
        table = jnp.where(lane == first + zone, values_ref[zone], table)
    return table if index is None else take_lanes(table, index)


def pack_section(head_ref, zone_ref, disp_ref, shared_ref, forward_ref, backward_ref):
    rows = head_ref.shape[1]
    planes = head_ref.shape[0]
    for x in range(planes):
        at = WIDE * x
        forward_ref[at : at + WIDE, :] = head_ref[x, rows - WIDE : rows, :]
        backward_ref[at : at + WIDE, :] = head_ref[x, 0:WIDE, :]
        at += WIDE * planes
        forward_ref[at : at + WIDE, :] = zone_ref[x, rows - WIDE : rows, :].astype(jnp.float32) + 1.0
        backward_ref[at : at + WIDE, :] = zone_ref[x, 0:WIDE, :].astype(jnp.float32) + 1.0
    index = shared_ref[...]
    index = jnp.concatenate([index, index], axis=0)
    lanes, segment = index & 127, index >> 7
    for comp in range(3):
        found = jnp.zeros((8, 128), jnp.float32)
        for s in range(disp_ref.shape[1] // 128):
            row = disp_ref[comp : comp + 1, s * 128 : (s + 1) * 128]
            found = jnp.where(segment == s, take_lanes(row, lanes), found)
        for s in range(4):
            at = 2 * WIDE * planes + 2 * comp + s // 2
            backward_ref[at : at + 1, (s % 2) * 128 : (s % 2 + 1) * 128] = found[s : s + 1]
    backward_ref[30:32, :] = jnp.zeros((2, 256), jnp.float32)


def pack_crest(place_ref, head_ref, zone_ref, before_ref, after_ref, low_ref, high_ref):
    planes, rows = head_ref.shape[0], head_ref.shape[1]
    inside = jnp.where(place_ref[0] < place_ref[1] - 1, 1.0, 0.0)
    for x in range(planes):
        for field in range(2):
            at = field * WIDE * planes + WIDE * x
            own = head_ref[x] if field == 0 else zone_ref[x].astype(jnp.float32) + 1.0
            tail = jnp.concatenate(
                [
                    after_ref[at : at + WIDE, :] * inside,
                    jnp.zeros((2, own.shape[1]), jnp.float32),
                    before_ref[at : at + WIDE, :],
                ],
                axis=0,
            )
            if x < WIDE:
                low_ref[field, x, 0:rows, :] = own
                low_ref[field, x, rows : rows + 8, :] = tail
            if x >= planes - WIDE:
                high_ref[field, x - planes + WIDE, 0:rows, :] = own
                high_ref[field, x - planes + WIDE, rows : rows + 8, :] = tail


def seepage(
    alpha_ref,
    expo_ref,
    ks_ref,
    low_ref,
    high_ref,
    before_ref,
    after_ref,
    wanted_ref,
    head_ref,
    out_ref,
    h,
    alpha_f,
    expo_f,
    m_f,
    root_f,
    r_f,
    cap_f,
    table,
    deep,
    index,
):
    planes = head_ref.shape[0]
    rows = head_ref.shape[1]
    total = planes + 2 * WIDE
    height, depth = h.shape[1], h.shape[2]
    lane8 = lax.broadcasted_iota(jnp.int32, (8, 128), 1)
    alpha_t = pick(alpha_ref, None, 1)
    expo_t = pick(expo_ref, None, 1)
    expo_t = jnp.where(expo_t > 0, expo_t, 2.0)
    m_t = 1.0 - 1.0 / expo_t
    root_t = jnp.sqrt(pick(ks_ref, None, 1))

    def fields(x, source, plane):
        h[x] = source[0, plane]
        for row in range(0, height, 8):
            for col in range(0, depth, 128):
                zone = source[1, plane, row : row + 8, col : col + 128].astype(jnp.int32)
                alpha_f[x, row : row + 8, col : col + 128] = take_lanes(alpha_t, zone)
                expo_f[x, row : row + 8, col : col + 128] = take_lanes(expo_t, zone)
                m_f[x, row : row + 8, col : col + 128] = take_lanes(m_t, zone)
                root_f[x, row : row + 8, col : col + 128] = take_lanes(root_t, zone)

    @pl.loop(0, WIDE)
    def _(x):
        fields(x, before_ref, x)
        fields(WIDE + x, low_ref, x)
        fields(WIDE + planes + x, after_ref, x)

    fields(2 * WIDE, high_ref, WIDE - 1)

    def log_terms(x):
        scaled = alpha_f[x] * jnp.maximum(-h[x], 0.0)
        expo = expo_f[x]
        log_a = jnp.log(jnp.maximum(scaled, 1e-30))
        log_p = expo * log_a
        log_1p = jnp.log(1.0 + jnp.exp(log_p))
        return expo, log_a, log_p, log_1p

    def retention(x):
        expo, log_a, log_p, log_1p = log_terms(x)
        m = m_f[x]
        inner = 1.0 - jnp.exp(m * (log_p - log_1p))
        r_f[x] = root_f[x] * jnp.exp(-0.25 * m * log_1p) * inner
        power = jnp.exp(log_p - log_a - (m + 1.0) * log_1p)
        cap_f[x] = TIME_STEP / (STORAGE + THETA_GAP * alpha_f[x] * (expo - 1.0) * power)

    inner_z = lax.broadcasted_iota(jnp.int32, (height, depth), 1) < depth - 1

    def face(x):
        return r_f[x] * r_f[x + 1] * (h[x + 1] - h[x])

    for sweep in range(SWEEPS):

        @pl.loop(sweep, total - sweep)
        def _(x):
            retention(x)

        def update(x, came):
            here, r = h[x], r_f[x]
            goes = face(x)
            flux_y = r * pltpu.roll(r, height - 1, 0) * (pltpu.roll(here, height - 1, 0) - here)
            flux_z = r * pltpu.roll(r, depth - 1, 1) * (pltpu.roll(here, depth - 1, 1) - here + 1.0)
            flux_z = jnp.where(inner_z, flux_z, 0.0)
            inflow = goes - came + (flux_y - pltpu.roll(flux_y, 1, 0)) + (flux_z - pltpu.roll(flux_z, 1, 1))
            h[x] = here + cap_f[x] * inflow
            return goes

        lax.fori_loop(sweep + 1, total - sweep - 1, update, face(sweep))

    for x in range(planes):
        _, _, _, log_1p = log_terms(WIDE + x)
        here = h[WIDE + x][0:rows]
        head_ref[x] = here
        table[x * rows : (x + 1) * rows, :] = jnp.exp(-m_f[WIDE + x] * log_1p)[0:rows] * here
    deep[...] = table[...].T
    index[:, 0:64] = wanted_ref[...]
    index[:, 64:128] = wanted_ref[...]
    bands = depth // BAND

    @pl.loop(0, bands)
    def _(b):
        upper = deep[pl.ds(pl.multiple_of(b * BAND, 8), 8), :]
        lower = deep[pl.ds(pl.multiple_of(b * BAND + 8, 8), 8), :]
        for group in range(wanted_ref.shape[0] // bands):
            d = group * bands + b
            columns = jnp.broadcast_to(index[pl.ds(d, 1), :], (8, 128))
            out_ref[d] = jnp.where(lane8 < 64, take_lanes(upper, columns), take_lanes(lower, columns))


def trial_state(matrix_ref, disp_ref, ghost_ref, conn_ref, stress_ref, trial_ref, nodes, corners):
    for comp in range(3):
        for s in range(8):
            nodes[comp * 12 + s : comp * 12 + s + 1, :] = disp_ref[comp : comp + 1, s * 128 : (s + 1) * 128]
        for s in range(4):
            at = 24 + 2 * comp + s // 2
            nodes[comp * 12 + 8 + s : comp * 12 + 9 + s, :] = ghost_ref[at : at + 1, (s % 2) * 128 : (s % 2 + 1) * 128]
    elems = conn_ref.shape[1]

    @pl.loop(0, elems, step=128)
    def _(e):
        e = pl.multiple_of(e, 128)
        index = conn_ref[:, pl.ds(e, 128)]
        lanes, segment = index & 127, index >> 7
        found = [jnp.zeros((8, 128), jnp.float32) for _ in range(3)]
        for s in range(12):
            here = segment == s
            for comp in range(3):
                row = nodes[comp * 12 + s : comp * 12 + s + 1, :]
                found[comp] = jnp.where(here, take_lanes(row, lanes), found[comp])
        for comp in range(3):
            corners[comp * 8 : comp * 8 + 8, pl.ds(e, 128)] = found[comp]

    strain = jnp.dot(
        matrix_ref[...], corners[...], precision=lax.Precision.HIGHEST, preferred_element_type=jnp.float32
    )
    lame_first = YOUNG * POISSON / ((1.0 + POISSON) * (1.0 - 2.0 * POISSON))
    modulus = YOUNG / (2.0 * (1.0 + POISSON))
    part = [strain[8 * i : 8 * i + 8] for i in range(6)]
    volume = lame_first * (part[0] + part[1] + part[2])
    normals = [stress_ref[:, i, :] + volume + 2.0 * modulus * part[i] for i in range(3)]
    shears = [stress_ref[:, i, :] + modulus * part[i] for i in range(3, 6)]
    mean = (normals[0] + normals[1] + normals[2]) * (1.0 / 3.0)
    devs = [value - mean for value in normals]
    trial_ref[6] = mean
    trial_ref[7] = jnp.sqrt(
        0.5 * (devs[0] ** 2 + devs[1] ** 2 + devs[2] ** 2) + shears[0] ** 2 + shears[1] ** 2 + shears[2] ** 2
    )
    for i in range(3):
        trial_ref[i] = devs[i]
        trial_ref[3 + i] = shears[i]


def halves(value):
    high = value.astype(jnp.bfloat16).astype(jnp.float32)
    return high, value - high


def final_state(
    cohesion_ref,
    friction_ref,
    matrix_ref,
    band_ref,
    slot_ref,
    depth_ref,
    zone_ref,
    trial_ref,
    conn_ref,
    stress_ref,
    release_ref,
    own_ref,
    ghost_ref,
    force_h,
    force_l,
):
    slot, depth = slot_ref[...], depth_ref[...]
    wanted_row = (slot >> 6) * 8 + (depth & 7)
    wanted_lane = (depth >> 3) * 64 + (slot & 63)

    def look(at, found):
        at = pl.multiple_of(at * 8, 8)
        for row in range(8):
            value = take_lanes(band_ref[pl.ds(at + row, 1), :], wanted_lane)
            found = jnp.where(wanted_row == at + row, value, found)
        return found

    pore = lax.fori_loop(0, band_ref.shape[0] // 8, look, jnp.zeros((8, 128), jnp.float32))
    zone = zone_ref[...]
    tan_red = pick(friction_ref, zone) * (1.0 / REDUCTION)
    cos_red = 1.0 / jnp.sqrt(1.0 + tan_red * tan_red)
    sin_red = tan_red * cos_red
    common = 6.0 / (np.sqrt(3.0).astype(np.float32) * (3.0 - sin_red))
    slope = common * sin_red
    bound = common * (pick(cohesion_ref, zone) * (1.0 / REDUCTION)) * cos_red

    def spread(value):
        return jnp.concatenate([value[r : r + 1] for r in range(8)], axis=1)

    allow = jnp.maximum(spread(bound - slope * pore) - spread(slope) * trial_ref[6], 0.0)
    deviator = trial_ref[7]
    yielded = deviator > allow
    scale = jnp.where(yielded, allow / jnp.where(yielded, deviator, 1.0), 1.0)
    release_ref[...] = (1.0 - scale) * deviator
    mean = trial_ref[6]
    parts = [mean + scale * trial_ref[i] for i in range(3)] + [scale * trial_ref[3 + i] for i in range(3)]
    for i in range(6):
        stress_ref[:, i, :] = parts[i]
    force = jnp.dot(
        matrix_ref[...],
        jnp.concatenate(parts, axis=0),
        precision=lax.Precision.HIGHEST,
        preferred_element_type=jnp.float32,
    )
    high, low = halves(force)
    force_h[...] = high
    force_l[...] = low
    elems = conn_ref.shape[1]
    in_segment = lax.broadcasted_iota(jnp.int32, (16, elems), 0)
    in_lane = lax.broadcasted_iota(jnp.int32, (128, elems), 0)

    def gathered(corner, total):
        node = conn_ref[pl.ds(corner, 1), :]
        here = jnp.broadcast_to(node >> 7, in_segment.shape) == in_segment
        rows = []
        for source in (force_h, force_l):
            for comp in range(3):
                value = jnp.broadcast_to(source[pl.ds(comp * 8 + corner, 1), :], in_segment.shape)
                rows.append(jnp.where(here, value, 0.0))
        left = jnp.concatenate(rows, axis=0).astype(jnp.bfloat16)
        right = jnp.where(jnp.broadcast_to(node & 127, in_lane.shape) == in_lane, 1.0, 0.0).astype(jnp.bfloat16)
        return total + lax.dot_general(left, right, (((1,), (1,)), ((), ())), preferred_element_type=jnp.float32)

    total = lax.fori_loop(0, 8, gathered, jnp.zeros((96, 128), jnp.float32))
    total = total[0:48] + total[48:96]
    for comp in range(3):
        own_ref[comp * 8 : comp * 8 + 8, :] = total[comp * 16 : comp * 16 + 8]
        ghost_ref[comp * 4 : comp * 4 + 4, :] = total[comp * 16 + 8 : comp * 16 + 12]


def add_returned(own_ref, ghost_ref, shared_ref, out_ref):
    shared = shared_ref[...]
    in_lane = lax.broadcasted_iota(jnp.int32, (128, 128), 0)
    in_segment = lax.broadcasted_iota(jnp.int32, (8, 128), 0)
    lefts, rights = [], []
    for s in range(4):
        node = shared[s : s + 1]
        rights.append(jnp.where(jnp.broadcast_to(node & 127, in_lane.shape) == in_lane, 1.0, 0.0))
        here = jnp.broadcast_to(node >> 7, in_segment.shape) == in_segment
        rows = []
        for comp in range(3):
            value = ghost_ref[comp * 4 + s : comp * 4 + s + 1, :]
            high, low = halves(value)
            for piece in (high, low):
                rows.append(jnp.where(here, jnp.broadcast_to(piece, in_segment.shape), 0.0))
        lefts.append(jnp.concatenate(rows, axis=0))
    left = jnp.concatenate(lefts, axis=1).astype(jnp.bfloat16)
    right = jnp.concatenate(rights, axis=1).astype(jnp.bfloat16)
    added = lax.dot_general(left, right, (((1,), (1,)), ((), ())), preferred_element_type=jnp.float32)
    for comp in range(3):
        total = own_ref[comp * 8 : comp * 8 + 8, :] + added[comp * 16 : comp * 16 + 8] + added[comp * 16 + 8 : comp * 16 + 16]
        for s in range(8):
            out_ref[comp : comp + 1, s * 128 : (s + 1) * 128] = total[s : s + 1]


VM = pl.BlockSpec(memory_space=pltpu.VMEM)
SM = pl.BlockSpec(memory_space=pltpu.SMEM)


def call(body, specs, outs, scratch, name):
    return pl.pallas_call(
        body,
        in_specs=specs,
        out_specs=tuple(VM for _ in outs),
        out_shape=tuple(jax.ShapeDtypeStruct(shape, jnp.float32) for shape in outs),
        scratch_shapes=scratch,
        compiler_params=pltpu.CompilerParams(vmem_limit_bytes=VMEM_LIMIT),
        name=name,
    )


def steps(count, by):
    return [(i, i + by) for i in range(count) if 0 <= i + by < count]


def per_device(
    pressure_head,
    zone_ids,
    retention_alpha,
    retention_exponent,
    conductivity,
    sent_columns,
    displacement,
    stress_old,
    connectivity,
    shared_nodes,
    element_zone,
    element_slot,
    element_depth,
    cohesion,
    friction,
):
    crest, section = (lax.axis_size(axis) for axis in AXES)
    devices = crest * section
    planes, rows, depth = pressure_head.shape
    height = rows + 8
    elems = connectivity.shape[1]
    nodes = displacement.shape[1]
    shared = shared_nodes.reshape(4, 128)
    place = jnp.stack([lax.axis_index("section"), jnp.int32(section)])

    forward, backward = call(
        pack_section, [VM] * 4, [(2 * WIDE * planes, depth), (32, depth)], [], "pack_section"
    )(pressure_head, zone_ids, displacement, shared)
    before = lax.ppermute(forward, "section", steps(section, 1))
    after = lax.ppermute(backward, AXES, steps(devices, -1))

    edge = (2, WIDE, height, depth)
    low, high = call(pack_crest, [SM] + [VM] * 4, [edge, edge], [], "pack_crest")(
        place, pressure_head, zone_ids, before, after
    )
    west = lax.ppermute(high, "crest", steps(crest, 1))
    east = lax.ppermute(low, "crest", steps(crest, -1))

    matrix = component_major()
    (trial,) = call(
        trial_state,
        [VM] * 5,
        [(8, 8, elems)],
        [pltpu.VMEM((40, 128), jnp.float32), pltpu.VMEM((24, elems), jnp.float32)],
        "trial_state",
    )(jnp.asarray(matrix, jnp.float32), displacement, after, connectivity, stress_old)

    total = planes + 2 * WIDE
    field = pltpu.VMEM((total, height, depth), jnp.float32)
    head_out, outgoing = call(
        seepage,
        [SM] * 3 + [VM] * 5,
        [pressure_head.shape, (devices, 8, 128)],
        [field] * 7
        + [
            pltpu.VMEM((planes * rows, depth), jnp.float32),
            pltpu.VMEM((depth, planes * rows), jnp.float32),
            pltpu.VMEM((devices, 128), jnp.int32),
        ],
        "seepage",
    )(retention_alpha, retention_exponent, conductivity, low, high, west, east, sent_columns[0])
    incoming = lax.all_to_all(outgoing, AXES, split_axis=0, concat_axis=0, tiled=True)

    stress_new, release, own, ghost = call(
        final_state,
        [SM] * 2 + [VM] * 7,
        [stress_old.shape, (8, elems), (24, 128), (12, 128)],
        [pltpu.VMEM((24, elems), jnp.float32)] * 2,
        "final_state",
    )(
        cohesion,
        friction,
        jnp.asarray(matrix.T * 0.125, jnp.float32),
        incoming.reshape(devices * 8, 128),
        element_slot.reshape(8, 128),
        element_depth.reshape(8, 128),
        element_zone.reshape(8, 128),
        trial,
        connectivity,
    )
    returned = lax.ppermute(ghost, AXES, steps(devices, 1))
    (node_forces,) = call(add_returned, [VM] * 3, [(3, nodes)], [], "add_returned")(own, returned, shared)
    return (head_out, stress_new, release, node_forces)


def solution(mesh):
    return jax.shard_map(
        per_device,
        mesh=mesh,
        in_specs=(
            P("crest", "section", None),
            P("crest", "section", None),
            P(),
            P(),
            P(),
            P(("crest", "section"), None, None),
            P(None, ("crest", "section")),
            P(None, None, ("crest", "section")),
            P(None, ("crest", "section")),
            P(("crest", "section")),
            P(("crest", "section")),
            P(("crest", "section")),
            P(("crest", "section")),
            P(),
            P(),
        ),
        out_specs=(
            P("crest", "section", None),
            P(None, None, ("crest", "section")),
            P(None, ("crest", "section")),
            P(None, ("crest", "section")),
        ),
        check_vma=False,
    )
```

time: 308 us -> 84.1 us (0.27)
  local copies, waits for them, and re-layouts: 149 us -> 5.53 us
  other arithmetic: 88.5 us -> 0.08 us
  Pallas kernels: 0 us -> 24.9 us
  starting transfers between devices: 52.7 us -> 28.5 us
  waiting for transfers between devices: 14.5 us -> 23.8 us
    gather x6 -> x0, local copies, waits for them, and re-layouts: 129 us -> none  [the longest x2 91.2 us: per_device(): outgoing = band_rows[wanted, band_index]]
    scatter-add x2 -> x0, other arithmetic: 44 us -> none  [the longest x1 40.5 us: per_device(): jax.ops.segment_sum(elem_force.T, flat_index, num_segments=nodes_dev + gh...]
    pallas_call x0 -> x6, Pallas kernels: none -> 24.9 us  [the longest x1 13.4 us: per_device(): call(final_state, [SM] * 2 + [VM] * 7, [stress_old.shape, (8, elems), (24...]
    ppermute x14 -> x5, starting transfers between devices: 42.8 us -> 19.1 us  [the longest x1 7.94 us: per_device(): after = lax.ppermute(backward, AXES, steps(devices, -1))]
    another operation x4 -> x1, other arithmetic: 21 us -> 0.08 us  [per_device(): place = jnp.stack([lax.axis_index('section'), jnp.int32(section)])]
    all_to_all x1, waiting for transfers between devices: 0.01 us -> 11.3 us  [per_device(): lax.all_to_all(outgoing, AXES, split_axis=0, concat_axis=0, tiled=True)]
    div x1 -> x0, other arithmetic: 9.96 us -> none  [return_map(): bound_value = 6.0 * (cohesion_e / REDUCTION) * cos_red / denom]
    mul x3 -> x0, other arithmetic: 7.91 us -> none  [the longest x1 5.06 us: return_map(): allow = jnp.maximum(bound_value - slope * mean_stress, 0.0)]
  transfers between devices with their start and end apart: 15 -> 6, of which waited for: 4 -> 5; matrix products, arithmetic and copies ran while one was open for 49% -> 1% of each run, Pallas kernels for 0% -> 1%
where the time goes in v1:
time: 84.1 us; the launch traced here: 83.7 us
  starting transfers between devices  28.5 us (34%)
  Pallas kernels  24.9 us (30%)
  waiting for transfers between devices  23.8 us (28%)
  local copies, waits for them, and re-layouts  5.53 us (7%)
    pallas_call x1, Pallas kernels, per_device(): call(final_state, [SM] * 2 + [VM] * 7, [stress_old.shape, (8, elems), (24...  13.4 us
    all_to_all x1, waiting for transfers between devices, per_device(): lax.all_to_all(outgoing, AXES, split_axis=0, concat_axis=0, tiled=True)  11.3 us
    all_to_all x1, starting transfers between devices, per_device(): lax.all_to_all(outgoing, AXES, split_axis=0, concat_axis=0, tiled=True)  9.39 us
    pallas_call x1, Pallas kernels, per_device(): call(seepage, [SM] * 3 + [VM] * 5, [pressure_head.shape, (devices, 8, 128...  8.88 us
    ppermute x1, starting transfers between devices, per_device(): after = lax.ppermute(backward, AXES, steps(devices, -1))  7.94 us
    ppermute x1, waiting for transfers between devices, per_device(): returned = lax.ppermute(ghost, AXES, steps(devices, 1))  6.45 us
    ppermute x1, starting transfers between devices, per_device(): east = lax.ppermute(low, 'crest', steps(crest, -1))  6.03 us
    unnamed x45, local copies, waits for them, and re-layouts  5.53 us
  transfers between devices with their start and end apart: 6, of which 5 were waited for; matrix products, arithmetic and copies ran while one was open for 1% of the time, Pallas kernels for 1%

profile of v1, /device:TPU:2, one launch (start us, length us, event | category | flops | bytes accessed | tf_op | source)
XLA Modules:
  0.0 83.7 jit_solution(9815421537314968797)
XLA Ops:
  0.6 0.0 copy-start
  0.6 0.9 %copy-done = f32[4,32,256]{2,1,0:T(8,128)S(1)} copy-done((f32[4,32,256]{2,1,0:T(8,128)S(1)}, f32[4,32,256]{2,1,0:T(8,128)}, u32[]{:S(2)}) %copy-start) | copy-done | bytes 131096
  1.5 0.9 %copy-done.2 = s32[4,32,256]{2,1,0:T(8,128)S(1)} copy-done((s32[4,32,256]{2,1,0:T(8,128)S(1)}, s32[4,32,256]{2,1,0:T(8,128)}, u32[]{:S(2)}) %copy-start.2) | copy-done | bytes 131096
  2.4 0.7 copy-done.5
  3.2 0.7 copy-done.9
  3.8 0.1 pack_section.1
  3.9 7.9 %collective-permute-start.1 = (f32[32,256]{1,0:T(8,128)S(1)}, f32[32,256]{1,0:T(8,128)S(1)}, u32[]{:S(2)}, u32[]{:S(2)}) collective-permute-start(f32[32,256]{1,0:T(8,128)S(1)} %get-tuple-element.15), channel_id=1, source_target_pairs={{1,0},{2,1},{3,2},{4,3},{5,4},{6,5},{7,6},{8,7},{9,8},{10,9},{11,1... | collective-permute-start | bytes 98312 | tf_op jit(solution)/shard_map/ppermute | solution.py:429
  11.9 1.3 %collective-permute-start = (f32[24,256]{1,0:T(8,128)S(1)}, f32[24,256]{1,0:T(8,128)S(1)}, u32[]{:S(2)}, u32[]{:S(2)}) collective-permute-start(f32[24,256]{1,0:T(8,128)S(1)} %get-tuple-element.14), channel_id=1, source_target_pairs={{0,1},{1,2},{2,3},{3,4},{4,5},{5,6},{6,7},{8,9},{9,10},{10,11},{11... | collective-permute-start | bytes 73736 | tf_op jit(solution)/shard_map/ppermute | solution.py:428
  13.2 0.1 pad_add_fusion.place_ref
  13.3 0.7 collective-permute-done.before_ref
  14.0 0.0 collective-permute-done.1.after_ref.ghost_ref
  14.0 0.0 copy-done.1
  14.0 0.0 copy-done.3
  14.0 0.6 pack_crest.1
  14.6 1.9 %collective-permute-start.2 = (f32[2,3,40,256]{3,2,1,0:T(8,128)S(1)}, f32[2,3,40,256]{3,2,1,0:T(8,128)S(1)}, u32[]{:S(2)}, u32[]{:S(2)}) collective-permute-start(f32[2,3,40,256]{3,2,1,0:T(8,128)S(1)} %get-tuple-element.17.high_ref), channel_id=1, source_target_pairs={{0,8},{8,16},{16,24},{24,32},{32,40},{40,48},{48,56},{56,64},{64,7... | collective-permute-start | bytes 737288 | tf_op jit(solution)/shard_map/ppermute | solution.py:435
  16.5 6.0 %collective-permute-start.3 = (f32[2,3,40,256]{3,2,1,0:T(8,128)S(1)}, f32[2,3,40,256]{3,2,1,0:T(8,128)S(1)}, u32[]{:S(2)}, u32[]{:S(2)}) collective-permute-start(f32[2,3,40,256]{3,2,1,0:T(8,128)S(1)} %get-tuple-element.16.low_ref), channel_id=1, source_target_pairs={{8,0},{16,8},{24,16},{32,24},{40,32},{48,40},{56,48},{64,56},{72,6... | collective-permute-start | bytes 737288 | tf_op jit(solution)/shard_map/ppermute | solution.py:436
  22.6 0.0 copy-done.20
  22.6 0.1 copy.21
  22.7 0.0 copy-start.14
  22.7 0.0 copy-start.15
  22.7 0.0 copy-start.16
  22.7 4.1 %collective-permute-done.2.before_ref = f32[2,3,40,256]{3,2,1,0:T(8,128)S(1)} collective-permute-done((f32[2,3,40,256]{3,2,1,0:T(8,128)S(1)}, f32[2,3,40,256]{3,2,1,0:T(8,128)S(1)}, u32[]{:S(2)}, u32[]{:S(2)}) %collective-permute-start.2) | collective-permute-done | bytes 245792 | tf_op jit(solution)/shard_map/ppermute | solution.py:435
  26.8 1.2 %collective-permute-done.3.after_ref = f32[2,3,40,256]{3,2,1,0:T(8,128)S(1)} collective-permute-done((f32[2,3,40,256]{3,2,1,0:T(8,128)S(1)}, f32[2,3,40,256]{3,2,1,0:T(8,128)S(1)}, u32[]{:S(2)}, u32[]{:S(2)}) %collective-permute-start.3) | collective-permute-done | bytes 245792 | tf_op jit(solution)/shard_map/ppermute | solution.py:436
  28.0 0.0 copy-done.14
  28.0 0.0 copy-done.15
  28.0 0.0 copy-done.16
  28.0 8.9 %seepage.1 = (f32[4,32,256]{2,1,0:T(8,128)}, f32[128,8,128]{2,1,0:T(8,128)}) custom-call(f32[8]{0:T(128)S(1)} %copy-done.14, f32[8]{0:T(128)S(1)} %copy-done.15, f32[8]{0:T(128)S(1)} %copy-done.16, f32[2,3,40,256]{3,2,1,0:T(8,128)S(1)} %get-tuple-element.16.low_ref, f32[2,3,40,256]{3,2,1,0:T(8,128)S(1)} %get-tuple-element.17.high_ref, ...), custom_call_target="tpu_custom_call" | custom-call | tf_op jit(solution)/shard_map/seepage/pallas_call | solution.py:449
  36.9 9.4 %all-to-all-start = ((f32[128,8,128]{2,1,0:T(8,128)}), f32[128,8,128]{2,1,0:T(8,128)S(1)}, u32[]{:S(2)}, u32[]{:S(2)}) async-start(f32[128,8,128]{2,1,0:T(8,128)} %get-tuple-element.19), calls=%async_computation | async-start | bytes 1048576 | tf_op jit(solution)/shard_map/all_to_all | solution.py:461
  46.3 0.0 copy-done.19
  46.3 0.0 copy-start.4
  46.3 0.0 copy-start.6
  46.3 0.0 copy-start.7
  46.3 0.1 copy.22.stress_ref
  46.5 0.6 copy-done.4
  47.1 0.0 copy-done.6
  47.1 0.0 copy-done.7
  47.1 1.2 %trial_state.1.trial_ref = f32[8,8,1024]{2,1,0:T(8,128)S(1)} custom-call(f32[48,24]{1,0:T(8,128)S(1)} %copy-done.7, f32[3,1024]{1,0:T(4,128)S(1)} %copy-done.6, f32[32,256]{1,0:T(8,128)S(1)} %collective-permute-done.1.after_ref.ghost_ref, s32[8,1024]{1,0:T(8,128)S(1)} %copy-done.4, f32[8,6,1024]{2,1,0:T(8,128)S(1)} %copy.22.stress_ref), custom_call_target="tpu_custom_call" | custom-call | tf_op jit(solution)/shard_map/trial_state/pallas_call | solution.py:439
  48.3 0.0 copy-start.11
  48.3 11.3 %all-to-all-done = f32[128,8,128]{2,1,0:T(8,128)S(1)} async-done(((f32[128,8,128]{2,1,0:T(8,128)}), f32[128,8,128]{2,1,0:T(8,128)S(1)}, u32[]{:S(2)}, u32[]{:S(2)}) %all-to-all-start) | async-done | bytes 524320 | tf_op jit(solution)/shard_map/all_to_all | solution.py:461
  59.7 0.0 copy-done.8
  59.7 0.6 copy-done.17
  60.3 0.0 copy-done.18
  60.3 13.4 %final_state.1 = (f32[8,6,1024]{2,1,0:T(8,128)S(1)}, f32[8,1024]{1,0:T(8,128)}, f32[24,128]{1,0:T(8,128)S(1)}, f32[12,128]{1,0:T(8,128)S(1)}) custom-call(f32[8]{0:T(128)S(1)} %copy-done.17, f32[8]{0:T(128)S(1)} %copy-done.18, f32[24,48]{1,0:T(8,128)S(1)} %copy-done.8, f32[1024,128]{1,0:T(8,128)S(1)} %bitcast.7, s32[8,128]{1,0:T(8,128)S(1)} %bitcast.11, ...), custom_call_target="tpu_custom_call" | custom-call | tf_op jit(solution)/shard_map/final_state/pallas_call | solution.py:463
  73.7 1.9 %collective-permute-start.4 = (f32[12,128]{1,0:T(8,128)S(1)}, f32[12,128]{1,0:T(8,128)S(1)}, u32[]{:S(2)}, u32[]{:S(2)}) collective-permute-start(f32[12,128]{1,0:T(8,128)S(1)} %get-tuple-element.23), channel_id=1, source_target_pairs={{0,1},{1,2},{2,3},{3,4},{4,5},{5,6},{6,7},{7,8},{8,9},{9,10},{10,1... | collective-permute-start | bytes 18440 | tf_op jit(solution)/shard_map/ppermute | solution.py:480
  75.6 0.0 copy-start.10
  75.7 0.8 copy.23
  76.5 6.5 %collective-permute-done.4.ghost_ref = f32[12,128]{1,0:T(8,128)S(1)} collective-permute-done((f32[12,128]{1,0:T(8,128)S(1)}, f32[12,128]{1,0:T(8,128)S(1)}, u32[]{:S(2)}, u32[]{:S(2)}) %collective-permute-start.4) | collective-permute-done | bytes 6176 | tf_op jit(solution)/shard_map/ppermute | solution.py:480
  82.9 0.8 add_returned.1
  (16 shorter events, 0.0 us)
Async XLA Ops:
  0.6 0.9 %copy-start = (f32[4,32,256]{2,1,0:T(8,128)S(1)}, f32[4,32,256]{2,1,0:T(8,128)}, u32[]{:S(2)}) copy-start(f32[4,32,256]{2,1,0:T(8,128)} %head_ref.3) | copy-start | bytes 393220
  1.5 0.9 %copy-start.2 = (s32[4,32,256]{2,1,0:T(8,128)S(1)}, s32[4,32,256]{2,1,0:T(8,128)}, u32[]{:S(2)}) copy-start(s32[4,32,256]{2,1,0:T(8,128)} %zone_ref.3) | copy-start | bytes 393220
  2.4 0.7 copy-start.5
  3.2 0.7 copy-start.9
  3.8 10.2 %copy-start.1 = (f32[4,32,256]{2,1,0:T(8,128)S(1)}, f32[4,32,256]{2,1,0:T(8,128)}, u32[]{:S(2)}) copy-start(f32[4,32,256]{2,1,0:T(8,128)} %head_ref.3) | copy-start | bytes 393220
  3.8 10.2 %copy-start.3 = (s32[4,32,256]{2,1,0:T(8,128)S(1)}, s32[4,32,256]{2,1,0:T(8,128)}, u32[]{:S(2)}) copy-start(s32[4,32,256]{2,1,0:T(8,128)} %zone_ref.3) | copy-start | bytes 393220
  3.9 10.1 %collective-permute-start.1 = (f32[32,256]{1,0:T(8,128)S(1)}, f32[32,256]{1,0:T(8,128)S(1)}, u32[]{:S(2)}, u32[]{:S(2)}) collective-permute-start(f32[32,256]{1,0:T(8,128)S(1)} %get-tuple-element.15), channel_id=1, source_target_pairs={{1,0},{2,1},{3,2},{4,3},{5,4},{6,5},{7,6},{8,7},{9,8},{10,9},{11,1... | collective-permute-start | bytes 98312 | tf_op jit(solution)/shard_map/ppermute | solution.py:429
  11.9 2.1 %collective-permute-start = (f32[24,256]{1,0:T(8,128)S(1)}, f32[24,256]{1,0:T(8,128)S(1)}, u32[]{:S(2)}, u32[]{:S(2)}) collective-permute-start(f32[24,256]{1,0:T(8,128)S(1)} %get-tuple-element.14), channel_id=1, source_target_pairs={{0,1},{1,2},{2,3},{3,4},{4,5},{5,6},{6,7},{8,9},{9,10},{10,11},{11... | collective-permute-start | bytes 73736 | tf_op jit(solution)/shard_map/ppermute | solution.py:428
  13.3 9.3 %copy-start.20 = (s32[1,128,64]{1,2,0:T(8,128)S(1)}, s32[1,128,64]{1,2,0:T(8,128)}, u32[]{:S(2)}) copy-start(s32[1,128,64]{1,2,0:T(8,128)} %param.22) | copy-start | bytes 98308
  14.6 12.2 %collective-permute-start.2 = (f32[2,3,40,256]{3,2,1,0:T(8,128)S(1)}, f32[2,3,40,256]{3,2,1,0:T(8,128)S(1)}, u32[]{:S(2)}, u32[]{:S(2)}) collective-permute-start(f32[2,3,40,256]{3,2,1,0:T(8,128)S(1)} %get-tuple-element.17.high_ref), channel_id=1, source_target_pairs={{0,8},{8,16},{16,24},{24,32},{32,40},{40,48},{48,56},{56,64},{64,7... | collective-permute-start | bytes 737288 | tf_op jit(solution)/shard_map/ppermute | solution.py:435
  16.5 11.5 %collective-permute-start.3 = (f32[2,3,40,256]{3,2,1,0:T(8,128)S(1)}, f32[2,3,40,256]{3,2,1,0:T(8,128)S(1)}, u32[]{:S(2)}, u32[]{:S(2)}) collective-permute-start(f32[2,3,40,256]{3,2,1,0:T(8,128)S(1)} %get-tuple-element.16.low_ref), channel_id=1, source_target_pairs={{8,0},{16,8},{24,16},{32,24},{40,32},{48,40},{56,48},{64,56},{72,6... | collective-permute-start | bytes 737288 | tf_op jit(solution)/shard_map/ppermute | solution.py:436
  22.7 5.3 %copy-start.14 = (f32[8]{0:T(128)S(1)}, f32[8]{0:T(128)}, u32[]{:S(2)}) copy-start(f32[8]{0:T(128)} %alpha_ref.1) | copy-start | bytes 100
  22.7 5.3 %copy-start.15 = (f32[8]{0:T(128)S(1)}, f32[8]{0:T(128)}, u32[]{:S(2)}) copy-start(f32[8]{0:T(128)} %expo_ref.1) | copy-start | bytes 100
  22.7 5.3 %copy-start.16 = (f32[8]{0:T(128)S(1)}, f32[8]{0:T(128)}, u32[]{:S(2)}) copy-start(f32[8]{0:T(128)} %ks_ref.1) | copy-start | bytes 100
  36.9 9.4 %copy-start.19 = (f32[8,6,1024]{2,0,1:T(8,128)S(1)}, f32[8,6,1024]{2,0,1:T(8,128)}, u32[]{:S(2)}) copy-start(f32[8,6,1024]{2,0,1:T(8,128)} %param.24) | copy-start | bytes 589828
  36.9 22.8 %all-to-all-start = ((f32[128,8,128]{2,1,0:T(8,128)}), f32[128,8,128]{2,1,0:T(8,128)S(1)}, u32[]{:S(2)}, u32[]{:S(2)}) async-start(f32[128,8,128]{2,1,0:T(8,128)} %get-tuple-element.19), calls=%async_computation | async-start | bytes 1048576 | tf_op jit(solution)/shard_map/all_to_all | solution.py:461
  46.3 0.8 copy-start.4
  46.3 0.8 copy-start.6
  46.3 0.8 copy-start.7
  47.1 12.6 %copy-start.8 = (f32[24,48]{1,0:T(8,128)S(1)}, f32[24,48]{1,0:T(8,128)}, u32[]{:S(2)}) copy-start(f32[24,48]{1,0:T(8,128)} %constant.11.clone.matrix_ref) | copy-start | bytes 13828
  47.1 12.6 %copy-start.12 = (s32[1024]{0:T(1024)S(1)}, s32[1024]{0:T(1024)}, u32[]{:S(2)}) copy-start(s32[1024]{0:T(1024)} %param.29) | copy-start | bytes 12292
  47.1 12.6 %copy-start.13 = (s32[1024]{0:T(1024)S(1)}, s32[1024]{0:T(1024)}, u32[]{:S(2)}) copy-start(s32[1024]{0:T(1024)} %param.27) | copy-start | bytes 12292
  48.3 11.4 %copy-start.11 = (s32[1024]{0:T(1024)S(1)}, s32[1024]{0:T(1024)}, u32[]{:S(2)}) copy-start(s32[1024]{0:T(1024)} %param.28) | copy-start | bytes 12292
  59.7 0.7 copy-start.17
  59.7 0.7 copy-start.18
  73.7 9.2 %collective-permute-start.4 = (f32[12,128]{1,0:T(8,128)S(1)}, f32[12,128]{1,0:T(8,128)S(1)}, u32[]{:S(2)}, u32[]{:S(2)}) collective-permute-start(f32[12,128]{1,0:T(8,128)S(1)} %get-tuple-element.23), channel_id=1, source_target_pairs={{0,1},{1,2},{2,3},{3,4},{4,5},{5,6},{6,7},{7,8},{8,9},{9,10},{10,1... | collective-permute-start | bytes 18440 | tf_op jit(solution)/shard_map/ppermute | solution.py:480
  75.6 7.3 %copy-start.10 = (s32[512]{0:T(512)S(1)}, s32[512]{0:T(512)}, u32[]{:S(2)}) copy-start(s32[512]{0:T(512)} %param.26) | copy-start | bytes 6148

commit v2 on v1

--- a/solution.py
+++ b/solution.py
@@ -139,21 +139,28 @@
     total = planes + 2 * WIDE
     height, depth = h.shape[1], h.shape[2]
     lane8 = lax.broadcasted_iota(jnp.int32, (8, 128), 1)
-    alpha_t = pick(alpha_ref, None, 1)
-    expo_t = pick(expo_ref, None, 1)
-    expo_t = jnp.where(expo_t > 0, expo_t, 2.0)
-    m_t = 1.0 - 1.0 / expo_t
-    root_t = jnp.sqrt(pick(ks_ref, None, 1))
+    zones = alpha_ref.shape[0]
+    alpha_t = [jnp.full((8, depth), alpha_ref[z], jnp.float32) for z in range(zones)]
+    expo_t = [jnp.full((8, depth), expo_ref[z], jnp.float32) for z in range(zones)]
+    expo_t = [jnp.where(value > 0, value, 2.0) for value in expo_t]
+    m_t = [1.0 - 1.0 / value for value in expo_t]
+    root_t = [jnp.sqrt(jnp.full((8, depth), ks_ref[z], jnp.float32)) for z in range(zones)]
 
     def fields(x, source, plane):
         h[x] = source[0, plane]
         for row in range(0, height, 8):
-            for col in range(0, depth, 128):
-                zone = source[1, plane, row : row + 8, col : col + 128].astype(jnp.int32)
-                alpha_f[x, row : row + 8, col : col + 128] = take_lanes(alpha_t, zone)
-                expo_f[x, row : row + 8, col : col + 128] = take_lanes(expo_t, zone)
-                m_f[x, row : row + 8, col : col + 128] = take_lanes(m_t, zone)
-                root_f[x, row : row + 8, col : col + 128] = take_lanes(root_t, zone)
+            zone = source[1, plane, row : row + 8, :].astype(jnp.int32) - 1
+            bits = [(zone & (1 << bit)) != 0 for bit in range(3)]
+
+            def choose(values):
+                for bit in bits:
+                    values = [jnp.where(bit, values[i + 1], values[i]) for i in range(0, len(values), 2)]
+                return values[0]
+
+            alpha_f[x, row : row + 8, :] = choose(alpha_t)
+            expo_f[x, row : row + 8, :] = choose(expo_t)
+            m_f[x, row : row + 8, :] = choose(m_t)
+            root_f[x, row : row + 8, :] = jnp.where(zone >= 0, choose(root_t), 0.0)
 
     @pl.loop(0, WIDE)
     def _(x):
@@ -252,8 +259,8 @@
     modulus = YOUNG / (2.0 * (1.0 + POISSON))
     part = [strain[8 * i : 8 * i + 8] for i in range(6)]
     volume = lame_first * (part[0] + part[1] + part[2])
-    normals = [stress_ref[:, i, :] + volume + 2.0 * modulus * part[i] for i in range(3)]
-    shears = [stress_ref[:, i, :] + modulus * part[i] for i in range(3, 6)]
+    normals = [stress_ref[i] + volume + 2.0 * modulus * part[i] for i in range(3)]
+    shears = [stress_ref[i] + modulus * part[i] for i in range(3, 6)]
     mean = (normals[0] + normals[1] + normals[2]) * (1.0 / 3.0)
     devs = [value - mean for value in normals]
     trial_ref[6] = mean
@@ -284,21 +291,26 @@
     release_ref,
     own_ref,
     ghost_ref,
-    force_h,
-    force_l,
 ):
     slot, depth = slot_ref[...], depth_ref[...]
     wanted_row = (slot >> 6) * 8 + (depth & 7)
     wanted_lane = (depth >> 3) * 64 + (slot & 63)
 
-    def look(at, found):
-        at = pl.multiple_of(at * 8, 8)
-        for row in range(8):
-            value = take_lanes(band_ref[pl.ds(at + row, 1), :], wanted_lane)
-            found = jnp.where(wanted_row == at + row, value, found)
-        return found
-
-    pore = lax.fori_loop(0, band_ref.shape[0] // 8, look, jnp.zeros((8, 128), jnp.float32))
+    def spread(value):
+        return jnp.concatenate([value[r : r + 1] for r in range(8)], axis=1)
+
+    elems = conn_ref.shape[1]
+    found_row = lax.broadcasted_iota(jnp.int32, (band_ref.shape[0], elems), 0) == spread(wanted_row)
+    high, low = halves(band_ref[...])
+    found = lax.dot_general(
+        jnp.concatenate([high, low], axis=1).astype(jnp.bfloat16),
+        jnp.where(found_row, 1.0, 0.0).astype(jnp.bfloat16),
+        (((0,), (0,)), ((), ())),
+        preferred_element_type=jnp.float32,
+    )
+    found = found[0:128] + found[128:256]
+    in_lane = lax.broadcasted_iota(jnp.int32, (128, elems), 0)
+    pore = jnp.sum(jnp.where(in_lane == spread(wanted_lane), found, 0.0), axis=0, keepdims=True)
     zone = zone_ref[...]
     tan_red = pick(friction_ref, zone) * (1.0 / REDUCTION)
     cos_red = 1.0 / jnp.sqrt(1.0 + tan_red * tan_red)
@@ -307,10 +319,7 @@
     slope = common * sin_red
     bound = common * (pick(cohesion_ref, zone) * (1.0 / REDUCTION)) * cos_red
 
-    def spread(value):
-        return jnp.concatenate([value[r : r + 1] for r in range(8)], axis=1)
-
-    allow = jnp.maximum(spread(bound - slope * pore) - spread(slope) * trial_ref[6], 0.0)
+    allow = jnp.maximum(spread(bound) - spread(slope) * (trial_ref[6] + pore), 0.0)
     deviator = trial_ref[7]
     yielded = deviator > allow
     scale = jnp.where(yielded, allow / jnp.where(yielded, deviator, 1.0), 1.0)
@@ -318,33 +327,27 @@
     mean = trial_ref[6]
     parts = [mean + scale * trial_ref[i] for i in range(3)] + [scale * trial_ref[3 + i] for i in range(3)]
     for i in range(6):
-        stress_ref[:, i, :] = parts[i]
+        stress_ref[i] = parts[i]
     force = jnp.dot(
         matrix_ref[...],
         jnp.concatenate(parts, axis=0),
         precision=lax.Precision.HIGHEST,
         preferred_element_type=jnp.float32,
     )
+    in_segment = lax.broadcasted_iota(jnp.int32, (16, elems), 0)
     high, low = halves(force)
-    force_h[...] = high
-    force_l[...] = low
-    elems = conn_ref.shape[1]
-    in_segment = lax.broadcasted_iota(jnp.int32, (16, elems), 0)
-    in_lane = lax.broadcasted_iota(jnp.int32, (128, elems), 0)
-
-    def gathered(corner, total):
-        node = conn_ref[pl.ds(corner, 1), :]
+    total = jnp.zeros((96, 128), jnp.float32)
+    for corner in range(8):
+        node = conn_ref[corner : corner + 1, :]
         here = jnp.broadcast_to(node >> 7, in_segment.shape) == in_segment
         rows = []
-        for source in (force_h, force_l):
+        for source in (high, low):
             for comp in range(3):
-                value = jnp.broadcast_to(source[pl.ds(comp * 8 + corner, 1), :], in_segment.shape)
-                rows.append(jnp.where(here, value, 0.0))
+                value = source[comp * 8 + corner : comp * 8 + corner + 1, :]
+                rows.append(jnp.where(here, jnp.broadcast_to(value, in_segment.shape), 0.0))
         left = jnp.concatenate(rows, axis=0).astype(jnp.bfloat16)
         right = jnp.where(jnp.broadcast_to(node & 127, in_lane.shape) == in_lane, 1.0, 0.0).astype(jnp.bfloat16)
-        return total + lax.dot_general(left, right, (((1,), (1,)), ((), ())), preferred_element_type=jnp.float32)
-
-    total = lax.fori_loop(0, 8, gathered, jnp.zeros((96, 128), jnp.float32))
+        total += lax.dot_general(left, right, (((1,), (1,)), ((), ())), preferred_element_type=jnp.float32)
     total = total[0:48] + total[48:96]
     for comp in range(3):
         own_ref[comp * 8 : comp * 8 + 8, :] = total[comp * 16 : comp * 16 + 8]
@@ -442,8 +445,9 @@
         [(8, 8, elems)],
         [pltpu.VMEM((40, 128), jnp.float32), pltpu.VMEM((24, elems), jnp.float32)],
         "trial_state",
-    )(jnp.asarray(matrix, jnp.float32), displacement, after, connectivity, stress_old)
-
+    )(jnp.asarray(matrix, jnp.float32), displacement, after, connectivity, stress_old.transpose(1, 0, 2))
+
+    trial, low = lax.optimization_barrier((trial, low))
     total = planes + 2 * WIDE
     field = pltpu.VMEM((total, height, depth), jnp.float32)
     head_out, outgoing = call(
@@ -463,8 +467,8 @@
     stress_new, release, own, ghost = call(
         final_state,
         [SM] * 2 + [VM] * 7,
-        [stress_old.shape, (8, elems), (24, 128), (12, 128)],
-        [pltpu.VMEM((24, elems), jnp.float32)] * 2,
+        [(6, 8, elems), (8, elems), (24, 128), (12, 128)],
+        [],
         "final_state",
     )(
         cohesion,
@@ -479,7 +483,7 @@
     )
     returned = lax.ppermute(ghost, AXES, steps(devices, 1))
     (node_forces,) = call(add_returned, [VM] * 3, [(3, nodes)], [], "add_returned")(own, returned, shared)
-    return (head_out, stress_new, release, node_forces)
+    return (head_out, stress_new.transpose(1, 0, 2), release, node_forces)
 
 
 def solution(mesh):

time: 84.1 us -> 73.3 us (0.87)
  blocking collectives: 0 us -> 19.7 us
  starting transfers between devices: 28.5 us -> 17.2 us
  Pallas kernels: 24.9 us -> 14.4 us
  waiting for transfers between devices: 23.8 us -> 16.5 us
  local copies, waits for them, and re-layouts: 5.53 us -> 4.02 us
    all_to_all x0 -> x1, blocking collectives: none -> 19.7 us  [per_device(): lax.all_to_all(outgoing, AXES, split_axis=0, concat_axis=0, tiled=True)]
    all_to_all x1 -> x0, waiting for transfers between devices: 11.3 us -> none  [per_device(): lax.all_to_all(outgoing, AXES, split_axis=0, concat_axis=0, tiled=True)]
    pallas_call x1, Pallas kernels: 13.4 us -> 3.5 us  [per_device(): call(final_state, [SM] * 2 + [VM] * 7, [(6, 8, elems), (8, elems), (24, 1...]
    all_to_all x1 -> x0, starting transfers between devices: 9.39 us -> none  [per_device(): lax.all_to_all(outgoing, AXES, split_axis=0, concat_axis=0, tiled=True)]
    ppermute x1, starting transfers between devices: 6.03 us -> 2.65 us  [per_device(): east = lax.ppermute(low, 'crest', steps(crest, -1))]
    ppermute x1, waiting for transfers between devices: 4.1 us -> 6.39 us  [per_device(): west = lax.ppermute(high, 'crest', steps(crest, 1))]
    unnamed x45 -> x43, local copies, waits for them, and re-layouts: 5.53 us -> 4.02 us
    ppermute x1, waiting for transfers between devices: 0.01 us -> 1.49 us  [per_device(): after = lax.ppermute(backward, AXES, steps(devices, -1))]
  transfers between devices with their start and end apart: 6 -> 5, of which waited for: 5 -> 4; matrix products, arithmetic and copies ran while one was open for 1% -> 0% of each run, Pallas kernels for 1% -> 2%
where the time goes in v2:
time: 73.3 us; the launch traced here: 72.8 us
  blocking collectives  19.7 us (27%)
  starting transfers between devices  17.2 us (23%)
  waiting for transfers between devices  16.5 us (23%)
  Pallas kernels  14.4 us (20%)
  local copies, waits for them, and re-layouts  4.02 us (5%)
  between operations  0.83 us (1%)
    all_to_all x1, blocking collectives, per_device(): lax.all_to_all(outgoing, AXES, split_axis=0, concat_axis=0, tiled=True)  19.7 us
    pallas_call x1, Pallas kernels, per_device(): call(seepage, [SM] * 3 + [VM] * 5, [pressure_head.shape, (devices, 8, 128...  8.24 us
    ppermute x1, starting transfers between devices, per_device(): after = lax.ppermute(backward, AXES, steps(devices, -1))  7.36 us
    ppermute x1, waiting for transfers between devices, per_device(): returned = lax.ppermute(ghost, AXES, steps(devices, 1))  7.26 us
    ppermute x1, waiting for transfers between devices, per_device(): west = lax.ppermute(high, 'crest', steps(crest, 1))  6.39 us
    unnamed x43, local copies, waits for them, and re-layouts  4.02 us
    pallas_call x1, Pallas kernels, per_device(): call(final_state, [SM] * 2 + [VM] * 7, [(6, 8, elems), (8, elems), (24, 1...  3.5 us
    ppermute x1, starting transfers between devices, per_device(): west = lax.ppermute(high, 'crest', steps(crest, 1))  3.32 us
  transfers between devices with their start and end apart: 5, of which 4 were waited for; matrix products, arithmetic and copies ran while one was open for 0% of the time, Pallas kernels for 2%

profile of v2, /device:TPU:2, one launch (start us, length us, event | category | flops | bytes accessed | tf_op | source)
XLA Modules:
  0.0 72.8 jit_solution(17415745825328384399)
XLA Ops:
  0.6 0.0 copy-start
  0.6 0.9 %copy-done = f32[4,32,256]{2,1,0:T(8,128)S(1)} copy-done((f32[4,32,256]{2,1,0:T(8,128)S(1)}, f32[4,32,256]{2,1,0:T(8,128)}, u32[]{:S(2)}) %copy-start) | copy-done | bytes 131096
  1.5 0.0 copy-start.2
  1.5 0.9 %copy-done.2 = s32[4,32,256]{2,1,0:T(8,128)S(1)} copy-done((s32[4,32,256]{2,1,0:T(8,128)S(1)}, s32[4,32,256]{2,1,0:T(8,128)}, u32[]{:S(2)}) %copy-start.2) | copy-done | bytes 131096
  2.4 0.7 copy-done.6
  3.2 0.7 copy-done.10
  3.8 0.1 pack_section.1
  3.9 1.9 %collective-permute-start.1 = (f32[24,256]{1,0:T(8,128)S(1)}, f32[24,256]{1,0:T(8,128)S(1)}, u32[]{:S(2)}, u32[]{:S(2)}) collective-permute-start(f32[24,256]{1,0:T(8,128)S(1)} %get-tuple-element.17), channel_id=1, source_target_pairs={{0,1},{1,2},{2,3},{3,4},{4,5},{5,6},{6,7},{8,9},{9,10},{10,11},{11... | collective-permute-start | bytes 73736 | tf_op jit(solution)/shard_map/ppermute | solution.py:431
  5.8 7.4 %collective-permute-start = (f32[32,256]{1,0:T(8,128)S(1)}, f32[32,256]{1,0:T(8,128)S(1)}, u32[]{:S(2)}, u32[]{:S(2)}) collective-permute-start(f32[32,256]{1,0:T(8,128)S(1)} %get-tuple-element.16), channel_id=1, source_target_pairs={{1,0},{2,1},{3,2},{4,3},{5,4},{6,5},{7,6},{8,7},{9,8},{10,9},{11,1... | collective-permute-start | bytes 98312 | tf_op jit(solution)/shard_map/ppermute | solution.py:432
  13.2 0.1 pad_add_fusion.place_ref
  13.3 0.0 collective-permute-done.1.before_ref
  13.3 1.5 %collective-permute-done.ghost_ref.after_ref = f32[32,256]{1,0:T(8,128)S(1)} collective-permute-done((f32[32,256]{1,0:T(8,128)S(1)}, f32[32,256]{1,0:T(8,128)S(1)}, u32[]{:S(2)}, u32[]{:S(2)}) %collective-permute-start) | collective-permute-done | bytes 32800 | tf_op jit(solution)/shard_map/ppermute | solution.py:432
  14.8 0.0 copy-done.1
  14.8 0.0 copy-done.3
  14.8 0.6 pack_crest.1
  15.4 2.7 %collective-permute-start.3 = (f32[2,3,40,256]{3,2,1,0:T(8,128)S(1)}, f32[2,3,40,256]{3,2,1,0:T(8,128)S(1)}, u32[]{:S(2)}, u32[]{:S(2)}) collective-permute-start(f32[2,3,40,256]{3,2,1,0:T(8,128)S(1)} %get-tuple-element.19.low_ref), channel_id=1, source_target_pairs={{8,0},{16,8},{24,16},{32,24},{40,32},{48,40},{56,48},{64,56},{72,6... | collective-permute-start | bytes 737288 | tf_op jit(solution)/shard_map/ppermute | solution.py:439
  18.0 0.0 copy-start.5
  18.0 0.0 copy-start.7
  18.0 0.0 copy-start.8
  18.1 3.3 %collective-permute-start.2 = (f32[2,3,40,256]{3,2,1,0:T(8,128)S(1)}, f32[2,3,40,256]{3,2,1,0:T(8,128)S(1)}, u32[]{:S(2)}, u32[]{:S(2)}) collective-permute-start(f32[2,3,40,256]{3,2,1,0:T(8,128)S(1)} %get-tuple-element.20.high_ref), channel_id=1, source_target_pairs={{0,8},{8,16},{16,24},{24,32},{32,40},{40,48},{48,56},{56,64},{64,7... | collective-permute-start | bytes 737288 | tf_op jit(solution)/shard_map/ppermute | solution.py:438
  21.4 0.0 copy-done.20
  21.4 0.1 copy.21
  21.5 0.0 copy-done.4
  21.5 0.0 copy-done.5
  21.5 0.0 copy-done.7
  21.5 0.0 copy-done.8
  21.5 1.2 %trial_state.1.trial_ref = f32[8,8,1024]{2,1,0:T(8,128)S(1)} custom-call(f32[48,24]{1,0:T(8,128)S(1)} %copy-done.8, f32[3,1024]{1,0:T(4,128)S(1)} %copy-done.7, f32[32,256]{1,0:T(8,128)S(1)} %collective-permute-done.ghost_ref.after_ref, s32[8,1024]{1,0:T(8,128)S(1)} %copy-done.5, f32[6,8,1024]{2,1,0:T(8,128)S(1)} %bitcast.11), custom_call_target="tpu_custom_call" | custom-call | tf_op jit(solution)/shard_map/trial_state/pallas_call | solution.py:442
  22.8 0.0 copy-start.15
  22.8 0.0 copy-start.16
  22.8 0.0 copy-start.17
  22.8 1.3 %collective-permute-done.3.after_ref = f32[2,3,40,256]{3,2,1,0:T(8,128)S(1)} collective-permute-done((f32[2,3,40,256]{3,2,1,0:T(8,128)S(1)}, f32[2,3,40,256]{3,2,1,0:T(8,128)S(1)}, u32[]{:S(2)}, u32[]{:S(2)}) %collective-permute-start.3) | collective-permute-done | bytes 245792 | tf_op jit(solution)/shard_map/ppermute | solution.py:439
  24.1 6.4 %collective-permute-done.2.before_ref = f32[2,3,40,256]{3,2,1,0:T(8,128)S(1)} collective-permute-done((f32[2,3,40,256]{3,2,1,0:T(8,128)S(1)}, f32[2,3,40,256]{3,2,1,0:T(8,128)S(1)}, u32[]{:S(2)}, u32[]{:S(2)}) %collective-permute-start.2) | collective-permute-done | bytes 245792 | tf_op jit(solution)/shard_map/ppermute | solution.py:438
  30.5 0.0 copy-done.15
  30.5 0.0 copy-done.16
  30.5 0.0 copy-done.17
  30.5 8.2 %seepage.1 = (f32[4,32,256]{2,1,0:T(8,128)}, f32[128,8,128]{2,1,0:T(8,128)S(1)}) custom-call(f32[8]{0:T(128)S(1)} %copy-done.15, f32[8]{0:T(128)S(1)} %copy-done.16, f32[8]{0:T(128)S(1)} %copy-done.17, f32[2,3,40,256]{3,2,1,0:T(8,128)S(1)} %get-tuple-element.19.low_ref, f32[2,3,40,256]{3,2,1,0:T(8,128)S(1)} %get-tuple-element.20.high_ref, ...), custom_call_target="tpu_custom_call" | custom-call | tf_op jit(solution)/shard_map/seepage/pallas_call | solution.py:453
  38.8 19.7 %all_to_all.5 = f32[128,8,128]{2,1,0:T(8,128)S(1)} all-to-all(f32[128,8,128]{2,1,0:T(8,128)S(1)} %get-tuple-element.22), channel_id=1, replica_groups=mesh['crest'=16,'section'=8] {'crest','section'}, dimensions={0} | all-to-all | bytes 1048576 | tf_op jit(solution)/shard_map/all_to_all | solution.py:465
  58.5 0.0 copy-done.9
  58.5 0.0 copy-done.13
  58.5 0.0 copy-done.14
  58.5 0.7 copy-done.12
  59.2 0.0 copy-done.18
  59.2 0.0 copy-done.19
  59.2 3.5 %final_state.1 = (f32[6,8,1024]{2,1,0:T(8,128)}, f32[8,1024]{1,0:T(8,128)}, f32[24,128]{1,0:T(8,128)S(1)}, f32[12,128]{1,0:T(8,128)S(1)}) custom-call(f32[8]{0:T(128)S(1)} %copy-done.18, f32[8]{0:T(128)S(1)} %copy-done.19, f32[24,48]{1,0:T(8,128)S(1)} %copy-done.9, f32[1024,128]{1,0:T(8,128)S(1)} %bitcast.9, s32[8,128]{1,0:T(8,128)S(1)} %bitcast.14, ...), custom_call_target="tpu_custom_call" | custom-call | tf_op jit(solution)/shard_map/final_state/pallas_call | solution.py:467
  62.7 2.0 %collective-permute-start.4 = (f32[12,128]{1,0:T(8,128)S(1)}, f32[12,128]{1,0:T(8,128)S(1)}, u32[]{:S(2)}, u32[]{:S(2)}) collective-permute-start(f32[12,128]{1,0:T(8,128)S(1)} %get-tuple-element.27), channel_id=1, source_target_pairs={{0,1},{1,2},{2,3},{3,4},{4,5},{5,6},{6,7},{7,8},{8,9},{9,10},{10,1... | collective-permute-start | bytes 18440 | tf_op jit(solution)/shard_map/ppermute | solution.py:484
  64.7 7.3 %collective-permute-done.4.ghost_ref = f32[12,128]{1,0:T(8,128)S(1)} collective-permute-done((f32[12,128]{1,0:T(8,128)S(1)}, f32[12,128]{1,0:T(8,128)S(1)}, u32[]{:S(2)}, u32[]{:S(2)}) %collective-permute-start.4) | collective-permute-done | bytes 6176 | tf_op jit(solution)/shard_map/ppermute | solution.py:484
  72.0 0.0 copy-done.11
  72.0 0.8 %add_returned.1 = f32[3,1024]{1,0:T(4,128)} custom-call(f32[24,128]{1,0:T(8,128)S(1)} %get-tuple-element.26.own_ref, f32[12,128]{1,0:T(8,128)S(1)} %collective-permute-done.4.ghost_ref, s32[4,128]{1,0:T(4,128)S(1)} %bitcast.13), custom_call_target="tpu_custom_call" | custom-call | tf_op jit(solution)/shard_map/add_returned/pallas_call | solution.py:485
  (13 shorter events, 0.0 us)
Async XLA Ops:
  0.6 0.9 %copy-start = (f32[4,32,256]{2,1,0:T(8,128)S(1)}, f32[4,32,256]{2,1,0:T(8,128)}, u32[]{:S(2)}) copy-start(f32[4,32,256]{2,1,0:T(8,128)} %head_ref.3) | copy-start | bytes 393220
  1.5 0.9 %copy-start.2 = (s32[4,32,256]{2,1,0:T(8,128)S(1)}, s32[4,32,256]{2,1,0:T(8,128)}, u32[]{:S(2)}) copy-start(s32[4,32,256]{2,1,0:T(8,128)} %zone_ref.3) | copy-start | bytes 393220
  2.4 0.7 copy-start.6
  3.2 0.7 copy-start.10
  3.8 10.9 %copy-start.1 = (f32[4,32,256]{2,1,0:T(8,128)S(1)}, f32[4,32,256]{2,1,0:T(8,128)}, u32[]{:S(2)}) copy-start(f32[4,32,256]{2,1,0:T(8,128)} %head_ref.3) | copy-start | bytes 393220
  3.8 10.9 %copy-start.3 = (s32[4,32,256]{2,1,0:T(8,128)S(1)}, s32[4,32,256]{2,1,0:T(8,128)}, u32[]{:S(2)}) copy-start(s32[4,32,256]{2,1,0:T(8,128)} %zone_ref.3) | copy-start | bytes 393220
  3.9 9.3 %collective-permute-start.1 = (f32[24,256]{1,0:T(8,128)S(1)}, f32[24,256]{1,0:T(8,128)S(1)}, u32[]{:S(2)}, u32[]{:S(2)}) collective-permute-start(f32[24,256]{1,0:T(8,128)S(1)} %get-tuple-element.17), channel_id=1, source_target_pairs={{0,1},{1,2},{2,3},{3,4},{4,5},{5,6},{6,7},{8,9},{9,10},{10,11},{11... | collective-permute-start | bytes 73736 | tf_op jit(solution)/shard_map/ppermute | solution.py:431
  5.8 8.9 %collective-permute-start = (f32[32,256]{1,0:T(8,128)S(1)}, f32[32,256]{1,0:T(8,128)S(1)}, u32[]{:S(2)}, u32[]{:S(2)}) collective-permute-start(f32[32,256]{1,0:T(8,128)S(1)} %get-tuple-element.16), channel_id=1, source_target_pairs={{1,0},{2,1},{3,2},{4,3},{5,4},{6,5},{7,6},{8,7},{9,8},{10,9},{11,1... | collective-permute-start | bytes 98312 | tf_op jit(solution)/shard_map/ppermute | solution.py:432
  13.3 8.1 %copy-start.20 = (s32[1,128,64]{1,2,0:T(8,128)S(1)}, s32[1,128,64]{1,2,0:T(8,128)}, u32[]{:S(2)}) copy-start(s32[1,128,64]{1,2,0:T(8,128)} %param.22) | copy-start | bytes 98308
  13.3 8.2 %copy-start.4 = (f32[8,6,1024]{2,0,1:T(8,128)S(1)}, f32[8,6,1024]{2,0,1:T(8,128)}, u32[]{:S(2)}) copy-start(f32[8,6,1024]{2,0,1:T(8,128)} %param.24) | copy-start | bytes 589828
  15.4 8.8 %collective-permute-start.3 = (f32[2,3,40,256]{3,2,1,0:T(8,128)S(1)}, f32[2,3,40,256]{3,2,1,0:T(8,128)S(1)}, u32[]{:S(2)}, u32[]{:S(2)}) collective-permute-start(f32[2,3,40,256]{3,2,1,0:T(8,128)S(1)} %get-tuple-element.19.low_ref), channel_id=1, source_target_pairs={{8,0},{16,8},{24,16},{32,24},{40,32},{48,40},{56,48},{64,56},{72,6... | collective-permute-start | bytes 737288 | tf_op jit(solution)/shard_map/ppermute | solution.py:439
  18.0 3.5 %copy-start.5 = (s32[8,1024]{1,0:T(8,128)S(1)}, s32[8,1024]{1,0:T(8,128)}, u32[]{:S(2)}) copy-start(s32[8,1024]{1,0:T(8,128)} %conn_ref.3) | copy-start | bytes 98308
  18.0 3.5 %copy-start.7 = (f32[3,1024]{1,0:T(4,128)S(1)}, f32[3,1024]{1,0:T(4,128)}, u32[]{:S(2)}) copy-start(f32[3,1024]{1,0:T(4,128)} %disp_ref.3) | copy-start | bytes 36868
  18.0 3.5 %copy-start.8 = (f32[48,24]{1,0:T(8,128)S(1)}, f32[48,24]{1,0:T(8,128)}, u32[]{:S(2)}) copy-start(f32[48,24]{1,0:T(8,128)} %constant.10.clone.matrix_ref) | copy-start | bytes 13828
  18.1 12.4 %collective-permute-start.2 = (f32[2,3,40,256]{3,2,1,0:T(8,128)S(1)}, f32[2,3,40,256]{3,2,1,0:T(8,128)S(1)}, u32[]{:S(2)}, u32[]{:S(2)}) collective-permute-start(f32[2,3,40,256]{3,2,1,0:T(8,128)S(1)} %get-tuple-element.20.high_ref), channel_id=1, source_target_pairs={{0,8},{8,16},{16,24},{24,32},{32,40},{40,48},{48,56},{56,64},{64,7... | collective-permute-start | bytes 737288 | tf_op jit(solution)/shard_map/ppermute | solution.py:438
  22.8 7.7 %copy-start.15 = (f32[8]{0:T(128)S(1)}, f32[8]{0:T(128)}, u32[]{:S(2)}) copy-start(f32[8]{0:T(128)} %alpha_ref.1) | copy-start | bytes 100
  22.8 7.7 %copy-start.16 = (f32[8]{0:T(128)S(1)}, f32[8]{0:T(128)}, u32[]{:S(2)}) copy-start(f32[8]{0:T(128)} %expo_ref.1) | copy-start | bytes 100
  22.8 7.7 %copy-start.17 = (f32[8]{0:T(128)S(1)}, f32[8]{0:T(128)}, u32[]{:S(2)}) copy-start(f32[8]{0:T(128)} %ks_ref.1) | copy-start | bytes 100
  38.8 19.8 %copy-start.9 = (f32[24,48]{1,0:T(8,128)S(1)}, f32[24,48]{1,0:T(8,128)}, u32[]{:S(2)}) copy-start(f32[24,48]{1,0:T(8,128)} %constant.11.clone.matrix_ref) | copy-start | bytes 13828
  38.8 19.8 %copy-start.13 = (s32[1024]{0:T(1024)S(1)}, s32[1024]{0:T(1024)}, u32[]{:S(2)}) copy-start(s32[1024]{0:T(1024)} %param.29) | copy-start | bytes 12292
  38.8 19.8 %copy-start.14 = (s32[1024]{0:T(1024)S(1)}, s32[1024]{0:T(1024)}, u32[]{:S(2)}) copy-start(s32[1024]{0:T(1024)} %param.27) | copy-start | bytes 12292
  58.5 0.7 copy-start.12
  58.5 0.7 copy-start.18
  58.5 0.7 copy-start.19
  62.7 9.3 %copy-start.11 = (s32[512]{0:T(512)S(1)}, s32[512]{0:T(512)}, u32[]{:S(2)}) copy-start(s32[512]{0:T(512)} %param.26) | copy-start | bytes 6148
  62.7 9.3 %collective-permute-start.4 = (f32[12,128]{1,0:T(8,128)S(1)}, f32[12,128]{1,0:T(8,128)S(1)}, u32[]{:S(2)}, u32[]{:S(2)}) collective-permute-start(f32[12,128]{1,0:T(8,128)S(1)} %get-tuple-element.27), channel_id=1, source_target_pairs={{0,1},{1,2},{2,3},{3,4},{4,5},{5,6},{6,7},{7,8},{8,9},{9,10},{10,1... | collective-permute-start | bytes 18440 | tf_op jit(solution)/shard_map/ppermute | solution.py:484

commit v3 on v2

--- a/solution.py
+++ b/solution.py
@@ -1,3 +1,5 @@
+import functools
+
 import jax
 import jax.numpy as jnp
 import numpy as np
@@ -18,7 +20,7 @@
 POISSON = 0.3
 
 AXES = ("crest", "section")
-VMEM_LIMIT = 48 * 1024 * 1024
+VMEM_LIMIT = 32 * 1024 * 1024
 
 
 def corner_signs(index):
@@ -65,16 +67,42 @@
     return table if index is None else take_lanes(table, index)
 
 
-def pack_section(head_ref, zone_ref, disp_ref, shared_ref, forward_ref, backward_ref):
-    rows = head_ref.shape[1]
-    planes = head_ref.shape[0]
+def pack_edges(
+    head_hbm,
+    zone_hbm,
+    disp_hbm,
+    shared_hbm,
+    forward_ref,
+    backward_ref,
+    low_ref,
+    high_ref,
+    head_ref,
+    zone_ref,
+    disp_ref,
+    shared_ref,
+    sems,
+):
+    copies = [
+        pltpu.make_async_copy(source, target, sems.at[i])
+        for i, (source, target) in enumerate(
+            [(head_hbm, head_ref), (zone_hbm, zone_ref), (disp_hbm, disp_ref), (shared_hbm, shared_ref)]
+        )
+    ]
+    for copy in copies:
+        copy.start()
+    for copy in copies:
+        copy.wait()
+    planes, rows = head_ref.shape[0], head_ref.shape[1]
     for x in range(planes):
-        at = WIDE * x
-        forward_ref[at : at + WIDE, :] = head_ref[x, rows - WIDE : rows, :]
-        backward_ref[at : at + WIDE, :] = head_ref[x, 0:WIDE, :]
-        at += WIDE * planes
-        forward_ref[at : at + WIDE, :] = zone_ref[x, rows - WIDE : rows, :].astype(jnp.float32) + 1.0
-        backward_ref[at : at + WIDE, :] = zone_ref[x, 0:WIDE, :].astype(jnp.float32) + 1.0
+        for field in range(2):
+            own = head_ref[x] if field == 0 else zone_ref[x].astype(jnp.float32) + 1.0
+            at = field * WIDE * planes + WIDE * x
+            forward_ref[at : at + WIDE, :] = own[rows - WIDE : rows, :]
+            backward_ref[at : at + WIDE, :] = own[0:WIDE, :]
+            if x < WIDE:
+                low_ref[field, x] = own
+            if x >= planes - WIDE:
+                high_ref[field, x - planes + WIDE] = own
     index = shared_ref[...]
     index = jnp.concatenate([index, index], axis=0)
     lanes, segment = index & 127, index >> 7
@@ -89,102 +117,121 @@
     backward_ref[30:32, :] = jnp.zeros((2, 256), jnp.float32)
 
 
-def pack_crest(place_ref, head_ref, zone_ref, before_ref, after_ref, low_ref, high_ref):
-    planes, rows = head_ref.shape[0], head_ref.shape[1]
-    inside = jnp.where(place_ref[0] < place_ref[1] - 1, 1.0, 0.0)
+def pack_corners(sections, place_ref, before_ref, after_ref, low_ref, high_ref):
+    planes = low_ref.shape[1] + high_ref.shape[1]
+    behind = jnp.where(place_ref[0] > 0, 1.0, 0.0)
+    ahead = jnp.where(place_ref[0] < sections - 1, 1.0, 0.0)
     for x in range(planes):
         for field in range(2):
             at = field * WIDE * planes + WIDE * x
-            own = head_ref[x] if field == 0 else zone_ref[x].astype(jnp.float32) + 1.0
             tail = jnp.concatenate(
                 [
-                    after_ref[at : at + WIDE, :] * inside,
-                    jnp.zeros((2, own.shape[1]), jnp.float32),
-                    before_ref[at : at + WIDE, :],
+                    after_ref[at : at + WIDE, :] * ahead,
+                    jnp.zeros((2, after_ref.shape[1]), jnp.float32),
+                    before_ref[at : at + WIDE, :] * behind,
                 ],
                 axis=0,
             )
-            if x < WIDE:
-                low_ref[field, x, 0:rows, :] = own
-                low_ref[field, x, rows : rows + 8, :] = tail
-            if x >= planes - WIDE:
-                high_ref[field, x - planes + WIDE, 0:rows, :] = own
-                high_ref[field, x - planes + WIDE, rows : rows + 8, :] = tail
+            if x < 2:
+                low_ref[field, x] = tail
+            else:
+                high_ref[field, x - 2] = tail
 
 
 def seepage(
-    alpha_ref,
-    expo_ref,
-    ks_ref,
+    crests,
+    place_ref,
+    tables_ref,
+    index,
     low_ref,
     high_ref,
+    low_tail_ref,
+    high_tail_ref,
     before_ref,
     after_ref,
-    wanted_ref,
+    before_tail_ref,
+    after_tail_ref,
     head_ref,
     out_ref,
     h,
     alpha_f,
-    expo_f,
+    less_f,
     m_f,
     root_f,
+    gain_f,
     r_f,
     cap_f,
     table,
     deep,
-    index,
 ):
     planes = head_ref.shape[0]
     rows = head_ref.shape[1]
     total = planes + 2 * WIDE
     height, depth = h.shape[1], h.shape[2]
     lane8 = lax.broadcasted_iota(jnp.int32, (8, 128), 1)
-    zones = alpha_ref.shape[0]
-    alpha_t = [jnp.full((8, depth), alpha_ref[z], jnp.float32) for z in range(zones)]
-    expo_t = [jnp.full((8, depth), expo_ref[z], jnp.float32) for z in range(zones)]
-    expo_t = [jnp.where(value > 0, value, 2.0) for value in expo_t]
-    m_t = [1.0 - 1.0 / value for value in expo_t]
-    root_t = [jnp.sqrt(jnp.full((8, depth), ks_ref[z], jnp.float32)) for z in range(zones)]
-
-    def fields(x, source, plane):
-        h[x] = source[0, plane]
-        for row in range(0, height, 8):
-            zone = source[1, plane, row : row + 8, :].astype(jnp.int32) - 1
-            bits = [(zone & (1 << bit)) != 0 for bit in range(3)]
-
-            def choose(values):
-                for bit in bits:
-                    values = [jnp.where(bit, values[i + 1], values[i]) for i in range(0, len(values), 2)]
-                return values[0]
-
-            alpha_f[x, row : row + 8, :] = choose(alpha_t)
-            expo_f[x, row : row + 8, :] = choose(expo_t)
-            m_f[x, row : row + 8, :] = choose(m_t)
-            root_f[x, row : row + 8, :] = jnp.where(zone >= 0, choose(root_t), 0.0)
+    zones = tables_ref.shape[0] // 4
+    alpha_t, less_t, m_t, root_t = (
+        [jnp.broadcast_to(tables_ref[f * zones + z : f * zones + z + 1, :], (8, depth)) for z in range(zones)]
+        for f in range(4)
+    )
+    behind = jnp.where(place_ref[1] > 0, 1.0, 0.0)
+    ahead = jnp.where(place_ref[1] < crests - 1, 1.0, 0.0)
+
+    def fields(x, row, head, zone):
+        at = slice(row, row + 8)
+        h[x, at, :] = head
+        zone = zone.astype(jnp.int32) - 1
+        bits = [(zone & (1 << bit)) != 0 for bit in range(3)]
+
+        def choose(values):
+            for bit in bits:
+                values = [jnp.where(bit, values[i + 1], values[i]) for i in range(0, len(values), 2)]
+            return values[0]
+
+        alpha, less = choose(alpha_t), choose(less_t)
+        alpha_f[x, at, :] = alpha
+        less_f[x, at, :] = less
+        m_f[x, at, :] = choose(m_t)
+        root_f[x, at, :] = jnp.where(zone >= 0, choose(root_t), 0.0)
+        gain_f[x, at, :] = THETA_GAP * alpha * less
+
+    def body_rows(x, source, plane, inside=None):
+        for row in range(0, rows, 8):
+            zone = source[1, plane, row : row + 8, :]
+            fields(x, row, source[0, plane, row : row + 8, :], zone if inside is None else zone * inside)
 
     @pl.loop(0, WIDE)
     def _(x):
-        fields(x, before_ref, x)
-        fields(WIDE + x, low_ref, x)
-        fields(WIDE + planes + x, after_ref, x)
-
-    fields(2 * WIDE, high_ref, WIDE - 1)
-
-    def log_terms(x):
+        body_rows(x, before_ref, x, behind)
+        body_rows(WIDE + x, low_ref, x)
+        body_rows(WIDE + planes + x, after_ref, x, ahead)
+
+    body_rows(2 * WIDE, high_ref, WIDE - 1)
+
+    @pl.loop(0, 2)
+    def _(x):
+        fields(1 + x, rows, before_tail_ref[0, x], before_tail_ref[1, x] * behind)
+        fields(3 + x, rows, low_tail_ref[0, x], low_tail_ref[1, x])
+        fields(5 + x, rows, high_tail_ref[0, x], high_tail_ref[1, x])
+        fields(7 + x, rows, after_tail_ref[0, x], after_tail_ref[1, x] * ahead)
+
+    for x in (0, total - 1):
+        for field in (h, alpha_f, less_f, m_f, root_f, gain_f):
+            field[x, rows:height, :] = jnp.zeros((height - rows, depth), jnp.float32)
+
+    def base(x):
         scaled = alpha_f[x] * jnp.maximum(-h[x], 0.0)
-        expo = expo_f[x]
-        log_a = jnp.log(jnp.maximum(scaled, 1e-30))
-        log_p = expo * log_a
-        log_1p = jnp.log(1.0 + jnp.exp(log_p))
-        return expo, log_a, log_p, log_1p
+        power = jnp.exp(less_f[x] * jnp.log(jnp.maximum(scaled, 1e-30)))
+        plus = 1.0 + power * scaled
+        return power, plus, jnp.log(plus)
 
     def retention(x):
-        expo, log_a, log_p, log_1p = log_terms(x)
-        m = m_f[x]
-        inner = 1.0 - jnp.exp(m * (log_p - log_1p))
-        r_f[x] = root_f[x] * jnp.exp(-0.25 * m * log_1p) * inner
-        power = jnp.exp(log_p - log_a - (m + 1.0) * log_1p)
-        cap_f[x] = TIME_STEP / (STORAGE + THETA_GAP * alpha_f[x] * (expo - 1.0) * power)
+        power, plus, log_plus = base(x)
+        fourth = jnp.exp(m_f[x] * log_plus)
+        square = fourth * fourth
+        part = power * (square * square)
+        r_f[x] = root_f[x] * fourth * (1.0 - part)
+        cap_f[x] = TIME_STEP * plus / (STORAGE * plus + gain_f[x] * part)
 
     inner_z = lax.broadcasted_iota(jnp.int32, (height, depth), 1) < depth - 1
 
@@ -210,23 +257,121 @@
         lax.fori_loop(sweep + 1, total - sweep - 1, update, face(sweep))
 
     for x in range(planes):
-        _, _, _, log_1p = log_terms(WIDE + x)
+        _, _, log_plus = base(WIDE + x)
         here = h[WIDE + x][0:rows]
         head_ref[x] = here
-        table[x * rows : (x + 1) * rows, :] = jnp.exp(-m_f[WIDE + x] * log_1p)[0:rows] * here
+        table[x * rows : (x + 1) * rows, :] = jnp.exp(4.0 * m_f[WIDE + x] * log_plus)[0:rows] * here
     deep[...] = table[...].T
-    index[:, 0:64] = wanted_ref[...]
-    index[:, 64:128] = wanted_ref[...]
     bands = depth // BAND
 
     @pl.loop(0, bands)
     def _(b):
         upper = deep[pl.ds(pl.multiple_of(b * BAND, 8), 8), :]
         lower = deep[pl.ds(pl.multiple_of(b * BAND + 8, 8), 8), :]
-        for group in range(wanted_ref.shape[0] // bands):
+        for group in range(out_ref.shape[0] // bands):
             d = group * bands + b
             columns = jnp.broadcast_to(index[pl.ds(d, 1), :], (8, 128))
             out_ref[d] = jnp.where(lane8 < 64, take_lanes(upper, columns), take_lanes(lower, columns))
+
+
+def element_rows(value):
+    return jnp.concatenate([value[r : r + 1] for r in range(8)], axis=1)
+
+
+def selectors(
+    order_ref,
+    disp_hbm,
+    stress_hbm,
+    conn_hbm,
+    strain_hbm,
+    force_hbm,
+    slot_hbm,
+    depth_hbm,
+    zone_hbm,
+    wanted_hbm,
+    alpha_hbm,
+    expo_hbm,
+    ks_hbm,
+    cohesion_hbm,
+    friction_hbm,
+    disp_ref,
+    stress_ref,
+    conn_ref,
+    strain_ref,
+    force_ref,
+    row_ref,
+    node_ref,
+    strength_ref,
+    lane_ref,
+    tables_ref,
+    index_ref,
+    slot_ref,
+    depth_ref,
+    zone_ref,
+    wanted_ref,
+    alpha_ref,
+    expo_ref,
+    ks_ref,
+    cohesion_ref,
+    friction_ref,
+    sems,
+):
+    del order_ref
+    pairs = [
+        (conn_hbm, conn_ref),
+        (slot_hbm, slot_ref),
+        (depth_hbm, depth_ref),
+        (zone_hbm, zone_ref),
+        (wanted_hbm, wanted_ref),
+        (alpha_hbm, alpha_ref),
+        (expo_hbm, expo_ref),
+        (ks_hbm, ks_ref),
+        (cohesion_hbm, cohesion_ref),
+        (friction_hbm, friction_ref),
+        (disp_hbm, disp_ref),
+        (stress_hbm, stress_ref),
+        (strain_hbm, strain_ref),
+        (force_hbm, force_ref),
+    ]
+    copies = [pltpu.make_async_copy(source, target, sems.at[i]) for i, (source, target) in enumerate(pairs)]
+    for copy in copies:
+        copy.start()
+    for copy in copies:
+        copy.wait()
+    elems = conn_ref.shape[1]
+    slot, depth = slot_ref[...], depth_ref[...]
+    row = element_rows((slot >> 6) * 8 + (depth & 7))
+    lane_ref[...] = element_rows((depth >> 3) * 64 + (slot & 63))
+    in_lane = lax.broadcasted_iota(jnp.int32, (128, elems), 0)
+
+    @pl.loop(0, row_ref.shape[0] // 128)
+    def _(part):
+        first = pl.multiple_of(part * 128, 128)
+        row_ref[pl.ds(first, 128), :] = jnp.where(in_lane == row - first, 1.0, 0.0).astype(jnp.bfloat16)
+
+    @pl.loop(0, 8)
+    def _(corner):
+        node = conn_ref[pl.ds(corner, 1), :] & 127
+        node_ref[corner] = jnp.where(in_lane == node, 1.0, 0.0).astype(jnp.bfloat16)
+
+    zone = zone_ref[...]
+    tan_red = pick(friction_ref, zone) * (1.0 / REDUCTION)
+    cos_red = 1.0 / jnp.sqrt(1.0 + tan_red * tan_red)
+    sin_red = tan_red * cos_red
+    common = 6.0 / (np.sqrt(3.0).astype(np.float32) * (3.0 - sin_red))
+    strength_ref[0:1, :] = element_rows(common * (pick(cohesion_ref, zone) * (1.0 / REDUCTION)) * cos_red)
+    strength_ref[1:2, :] = element_rows(common * sin_red)
+
+    zones, width = alpha_ref.shape[0], tables_ref.shape[1]
+    for z in range(zones):
+        expo = jnp.full((1, width), expo_ref[z], jnp.float32)
+        expo = jnp.where(expo > 0, expo, 2.0)
+        tables_ref[z : z + 1, :] = jnp.full((1, width), alpha_ref[z], jnp.float32)
+        tables_ref[zones + z : zones + z + 1, :] = expo - 1.0
+        tables_ref[2 * zones + z : 2 * zones + z + 1, :] = -0.25 * (1.0 - 1.0 / expo)
+        tables_ref[3 * zones + z : 3 * zones + z + 1, :] = jnp.sqrt(jnp.full((1, width), ks_ref[z], jnp.float32))
+    wanted = wanted_ref[...]
+    index_ref[...] = jnp.concatenate([wanted, wanted], axis=0).T
 
 
 def trial_state(matrix_ref, disp_ref, ghost_ref, conn_ref, stress_ref, trial_ref, nodes, corners):
@@ -278,48 +423,20 @@
 
 
 def final_state(
-    cohesion_ref,
-    friction_ref,
-    matrix_ref,
-    band_ref,
-    slot_ref,
-    depth_ref,
-    zone_ref,
-    trial_ref,
-    conn_ref,
-    stress_ref,
-    release_ref,
-    own_ref,
-    ghost_ref,
+    matrix_ref, band_ref, row_ref, lane_ref, node_ref, strength_ref, trial_ref, conn_ref, stress_ref, release_ref, own_ref, ghost_ref
 ):
-    slot, depth = slot_ref[...], depth_ref[...]
-    wanted_row = (slot >> 6) * 8 + (depth & 7)
-    wanted_lane = (depth >> 3) * 64 + (slot & 63)
-
-    def spread(value):
-        return jnp.concatenate([value[r : r + 1] for r in range(8)], axis=1)
-
     elems = conn_ref.shape[1]
-    found_row = lax.broadcasted_iota(jnp.int32, (band_ref.shape[0], elems), 0) == spread(wanted_row)
     high, low = halves(band_ref[...])
     found = lax.dot_general(
         jnp.concatenate([high, low], axis=1).astype(jnp.bfloat16),
-        jnp.where(found_row, 1.0, 0.0).astype(jnp.bfloat16),
+        row_ref[...],
         (((0,), (0,)), ((), ())),
         preferred_element_type=jnp.float32,
     )
     found = found[0:128] + found[128:256]
     in_lane = lax.broadcasted_iota(jnp.int32, (128, elems), 0)
-    pore = jnp.sum(jnp.where(in_lane == spread(wanted_lane), found, 0.0), axis=0, keepdims=True)
-    zone = zone_ref[...]
-    tan_red = pick(friction_ref, zone) * (1.0 / REDUCTION)
-    cos_red = 1.0 / jnp.sqrt(1.0 + tan_red * tan_red)
-    sin_red = tan_red * cos_red
-    common = 6.0 / (np.sqrt(3.0).astype(np.float32) * (3.0 - sin_red))
-    slope = common * sin_red
-    bound = common * (pick(cohesion_ref, zone) * (1.0 / REDUCTION)) * cos_red
-
-    allow = jnp.maximum(spread(bound) - spread(slope) * (trial_ref[6] + pore), 0.0)
+    pore = jnp.sum(jnp.where(in_lane == lane_ref[...], found, 0.0), axis=0, keepdims=True)
+    allow = jnp.maximum(strength_ref[0:1, :] - strength_ref[1:2, :] * (trial_ref[6] + pore), 0.0)
     deviator = trial_ref[7]
     yielded = deviator > allow
     scale = jnp.where(yielded, allow / jnp.where(yielded, deviator, 1.0), 1.0)
@@ -346,8 +463,7 @@
                 value = source[comp * 8 + corner : comp * 8 + corner + 1, :]
                 rows.append(jnp.where(here, jnp.broadcast_to(value, in_segment.shape), 0.0))
         left = jnp.concatenate(rows, axis=0).astype(jnp.bfloat16)
-        right = jnp.where(jnp.broadcast_to(node & 127, in_lane.shape) == in_lane, 1.0, 0.0).astype(jnp.bfloat16)
-        total += lax.dot_general(left, right, (((1,), (1,)), ((), ())), preferred_element_type=jnp.float32)
+        total += lax.dot_general(left, node_ref[corner], (((1,), (1,)), ((), ())), preferred_element_type=jnp.float32)
     total = total[0:48] + total[48:96]
     for comp in range(3):
         own_ref[comp * 8 : comp * 8 + 8, :] = total[comp * 16 : comp * 16 + 8]
@@ -383,20 +499,28 @@
 SM = pl.BlockSpec(memory_space=pltpu.SMEM)
 
 
-def call(body, specs, outs, scratch, name):
+HBM = pl.BlockSpec(memory_space=pltpu.HBM)
+
+
+def call(body, specs, outs, scratch, name, types=None):
+    types = types or [jnp.float32] * len(outs)
     return pl.pallas_call(
         body,
         in_specs=specs,
         out_specs=tuple(VM for _ in outs),
-        out_shape=tuple(jax.ShapeDtypeStruct(shape, jnp.float32) for shape in outs),
+        out_shape=tuple(jax.ShapeDtypeStruct(shape, kind) for shape, kind in zip(outs, types)),
         scratch_shapes=scratch,
         compiler_params=pltpu.CompilerParams(vmem_limit_bytes=VMEM_LIMIT),
         name=name,
     )
 
 
+def in_hbm(value):
+    return pltpu.with_memory_space_constraint(value, pltpu.HBM)
+
+
 def steps(count, by):
-    return [(i, i + by) for i in range(count) if 0 <= i + by < count]
+    return [(i, (i + by) % count) for i in range(count)]
 
 
 def per_device(
@@ -423,64 +547,112 @@
     elems = connectivity.shape[1]
     nodes = displacement.shape[1]
     shared = shared_nodes.reshape(4, 128)
-    place = jnp.stack([lax.axis_index("section"), jnp.int32(section)])
-
-    forward, backward = call(
-        pack_section, [VM] * 4, [(2 * WIDE * planes, depth), (32, depth)], [], "pack_section"
-    )(pressure_head, zone_ids, displacement, shared)
+    place = jnp.stack([lax.axis_index("section"), lax.axis_index("crest")])
+
+    own = (2, WIDE, rows, depth)
+    forward, backward, low, high = call(
+        pack_edges,
+        [HBM] * 4,
+        [(2 * WIDE * planes, depth), (32, depth), own, own],
+        [
+            pltpu.VMEM(pressure_head.shape, jnp.float32),
+            pltpu.VMEM(zone_ids.shape, jnp.int32),
+            pltpu.VMEM(displacement.shape, jnp.float32),
+            pltpu.VMEM(shared.shape, jnp.int32),
+            pltpu.SemaphoreType.DMA((4,)),
+        ],
+        "pack_edges",
+    )(*(in_hbm(x) for x in (pressure_head, zone_ids, displacement, shared)))
     before = lax.ppermute(forward, "section", steps(section, 1))
     after = lax.ppermute(backward, AXES, steps(devices, -1))
-
-    edge = (2, WIDE, height, depth)
-    low, high = call(pack_crest, [SM] + [VM] * 4, [edge, edge], [], "pack_crest")(
-        place, pressure_head, zone_ids, before, after
-    )
     west = lax.ppermute(high, "crest", steps(crest, 1))
     east = lax.ppermute(low, "crest", steps(crest, -1))
 
+    tails = (2, 2, 8, depth)
+    low_tail, high_tail = call(
+        functools.partial(pack_corners, section), [SM] + [VM] * 2, [tails, tails], [], "pack_corners"
+    )(place, before, after)
+    west_tail = lax.ppermute(high_tail, "crest", steps(crest, 1))
+    east_tail = lax.ppermute(low_tail, "crest", steps(crest, -1))
+
+    zones = retention_alpha.shape[0]
     matrix = component_major()
+    disp, stress, conn, strain_matrix_v, force_matrix, row_hot, node_hot, strength, lane, tables, index = call(
+        selectors,
+        [VM] + [HBM] * 14,
+        [
+            displacement.shape,
+            (6, 8, elems),
+            connectivity.shape,
+            (48, 24),
+            (24, 48),
+            (devices * 8, elems),
+            (8, 128, elems),
+            (2, elems),
+            (1, elems),
+            (4 * zones, depth),
+            (devices, 128),
+        ],
+        [pltpu.VMEM((8, 128), jnp.int32)] * 3
+        + [pltpu.VMEM((64, devices), jnp.int32)]
+        + [pltpu.SMEM((zones,), jnp.float32)] * 5
+        + [pltpu.SemaphoreType.DMA((14,))],
+        "selectors",
+        [jnp.float32] * 2
+        + [jnp.int32]
+        + [jnp.float32] * 2
+        + [jnp.bfloat16] * 2
+        + [jnp.float32, jnp.int32, jnp.float32, jnp.int32],
+    )(
+        forward,
+        *(
+            in_hbm(x)
+            for x in (
+                displacement,
+                stress_old.transpose(1, 0, 2),
+                connectivity,
+                jnp.asarray(matrix, jnp.float32),
+                jnp.asarray(matrix.T * 0.125, jnp.float32),
+                element_slot.reshape(8, 128),
+                element_depth.reshape(8, 128),
+                element_zone.reshape(8, 128),
+                sent_columns[0].T,
+                retention_alpha,
+                retention_exponent,
+                conductivity,
+                cohesion,
+                friction,
+            )
+        ),
+    )
     (trial,) = call(
         trial_state,
         [VM] * 5,
         [(8, 8, elems)],
         [pltpu.VMEM((40, 128), jnp.float32), pltpu.VMEM((24, elems), jnp.float32)],
         "trial_state",
-    )(jnp.asarray(matrix, jnp.float32), displacement, after, connectivity, stress_old.transpose(1, 0, 2))
-
-    trial, low = lax.optimization_barrier((trial, low))
+    )(strain_matrix_v, disp, after, conn, stress)
+
+    trial, tables = lax.optimization_barrier((trial, tables))
     total = planes + 2 * WIDE
     field = pltpu.VMEM((total, height, depth), jnp.float32)
     head_out, outgoing = call(
-        seepage,
-        [SM] * 3 + [VM] * 5,
+        functools.partial(seepage, crest),
+        [SM] + [VM] * 10,
         [pressure_head.shape, (devices, 8, 128)],
-        [field] * 7
-        + [
-            pltpu.VMEM((planes * rows, depth), jnp.float32),
-            pltpu.VMEM((depth, planes * rows), jnp.float32),
-            pltpu.VMEM((devices, 128), jnp.int32),
-        ],
+        [field] * 8
+        + [pltpu.VMEM((planes * rows, depth), jnp.float32), pltpu.VMEM((depth, planes * rows), jnp.float32)],
         "seepage",
-    )(retention_alpha, retention_exponent, conductivity, low, high, west, east, sent_columns[0])
+    )(place, tables, index, low, high, low_tail, high_tail, west, east, west_tail, east_tail)
     incoming = lax.all_to_all(outgoing, AXES, split_axis=0, concat_axis=0, tiled=True)
 
     stress_new, release, own, ghost = call(
         final_state,
-        [SM] * 2 + [VM] * 7,
+        [VM] * 8,
         [(6, 8, elems), (8, elems), (24, 128), (12, 128)],
         [],
         "final_state",
-    )(
-        cohesion,
-        friction,
-        jnp.asarray(matrix.T * 0.125, jnp.float32),
-        incoming.reshape(devices * 8, 128),
-        element_slot.reshape(8, 128),
-        element_depth.reshape(8, 128),
-        element_zone.reshape(8, 128),
-        trial,
-        connectivity,
-    )
+    )(force_matrix, incoming.reshape(devices * 8, 128), row_hot, lane, node_hot, strength, trial, conn)
     returned = lax.ppermute(ghost, AXES, steps(devices, 1))
     (node_forces,) = call(add_returned, [VM] * 3, [(3, nodes)], [], "add_returned")(own, returned, shared)
     return (head_out, stress_new.transpose(1, 0, 2), release, node_forces)

time: 73.3 us -> 68.7 us (0.937)
  the two profiles are of different devices: /device:TPU:2 before, /device:TPU:0 now
where the time goes in v3:
time: 68.7 us; the launch traced here: 68.5 us
  blocking collectives  23.1 us (34%)
  Pallas kernels  17.1 us (25%)
  starting transfers between devices  15.2 us (22%)
  waiting for transfers between devices  12.4 us (18%)
    all_to_all x1, blocking collectives, per_device(): lax.all_to_all(outgoing, AXES, split_axis=0, concat_axis=0, tiled=True)  23.1 us
    ppermute x1, waiting for transfers between devices, per_device(): returned = lax.ppermute(ghost, AXES, steps(devices, 1))  8.5 us
    pallas_call x1, Pallas kernels, per_device(): call(functools.partial(seepage, crest), [SM] + [VM] * 10, [pressure_head....  8.24 us
    ppermute x1, starting transfers between devices, per_device(): after = lax.ppermute(backward, AXES, steps(devices, -1))  7.73 us
    ppermute x1, starting transfers between devices, per_device(): east = lax.ppermute(low, 'crest', steps(crest, -1))  5.36 us
    pallas_call x1, Pallas kernels, per_device(): call(final_state, [VM] * 8, [(6, 8, elems), (8, elems), (24, 128), (12, 1...  3.06 us
    ppermute x1, waiting for transfers between devices, per_device(): west_tail = lax.ppermute(high_tail, 'crest', steps(crest, 1))  2.36 us
    pallas_call x1, Pallas kernels, per_device(): call(selectors, [VM] + [HBM] * 14, [displacement.shape, (6, 8, elems), co...  2.08 us
  transfers between devices with their start and end apart: 7, of which 3 were waited for; matrix products, arithmetic and copies ran while one was open for 0% of the time, Pallas kernels for 6%

profile of v3, /device:TPU:0, one launch (start us, length us, event | category | flops | bytes accessed | tf_op | source)
XLA Modules:
  0.0 68.5 jit_solution(2477900641128729962)
XLA Ops:
  0.6 1.1 %pack_edges.1 = (f32[24,256]{1,0:T(8,128)S(1)}, f32[32,256]{1,0:T(8,128)S(1)}, f32[2,3,32,256]{3,2,1,0:T(8,128)S(1)}, f32[2,3,32,256]{3,2,1,0:T(8,128)S(1)}) custom-call(f32[4,32,256]{2,1,0:T(8,128)} %head_hbm.1, s32[4,32,256]{2,1,0:T(8,128)} %zone_hbm.1, f32[3,1024]{1,0:T(4,128)} %disp_hbm.3, s32[4,128]{1,0:T(4,128)} %bitcast.13), custom_call_target="tpu_custom_call" | custom-call | tf_op jit(solution)/shard_map/pack_edges/pallas_call | solution.py:553
  1.8 5.4 %collective-permute-start.3 = (f32[2,3,32,256]{3,2,1,0:T(8,128)S(1)}, f32[2,3,32,256]{3,2,1,0:T(8,128)S(1)}, u32[]{:S(2)}, u32[]{:S(2)}) collective-permute-start(f32[2,3,32,256]{3,2,1,0:T(8,128)S(1)} %get-tuple-element.38.low_ref), channel_id=1, source_target_pairs={{0,120},{8,0},{16,8},{24,16},{32,24},{40,32},{48,40},{56,48},{64,5... | collective-permute-start | bytes 589832 | tf_op jit(solution)/shard_map/ppermute | solution.py:569
  7.1 0.0 collective-permute-start.2
  7.1 0.0 collective-permute-start.1
  7.1 7.7 %collective-permute-start = (f32[32,256]{1,0:T(8,128)S(1)}, f32[32,256]{1,0:T(8,128)S(1)}, u32[]{:S(2)}, u32[]{:S(2)}) collective-permute-start(f32[32,256]{1,0:T(8,128)S(1)} %get-tuple-element.32), channel_id=1, source_target_pairs={{0,127},{1,0},{2,1},{3,2},{4,3},{5,4},{6,5},{7,6},{8,7},{9,8},{10,... | collective-permute-start | bytes 98312 | tf_op jit(solution)/shard_map/ppermute | solution.py:567
  14.9 0.1 pad_add_fusion.place_ref
  14.9 0.0 collective-permute-done.1.before_ref
  14.9 1.5 %collective-permute-done.ghost_ref.after_ref = f32[32,256]{1,0:T(8,128)S(1)} collective-permute-done((f32[32,256]{1,0:T(8,128)S(1)}, f32[32,256]{1,0:T(8,128)S(1)}, u32[]{:S(2)}, u32[]{:S(2)}) %collective-permute-start) | collective-permute-done | bytes 32800 | tf_op jit(solution)/shard_map/ppermute | solution.py:567
  16.5 0.6 pack_corners.1
  17.0 0.5 collective-permute-start.5
  17.6 1.6 %collective-permute-start.4 = (f32[2,2,8,256]{3,2,1,0:T(8,128)S(1)}, f32[2,2,8,256]{3,2,1,0:T(8,128)S(1)}, u32[]{:S(2)}, u32[]{:S(2)}) collective-permute-start(f32[2,2,8,256]{3,2,1,0:T(8,128)S(1)} %get-tuple-element.41.high_tail_ref), channel_id=1, source_target_pairs={{0,8},{8,16},{16,24},{24,32},{32,40},{40,48},{48,56},{56,64},{64,7... | collective-permute-start | bytes 98312 | tf_op jit(solution)/shard_map/ppermute | solution.py:575
  19.1 2.1 %selectors.1 = (f32[3,1024]{1,0:T(4,128)S(1)}, f32[6,8,1024]{2,1,0:T(8,128)S(1)}, s32[8,1024]{1,0:T(8,128)S(1)}, f32[48,24]{1,0:T(8,128)S(1)}, f32[24,48]{1,0:T(...) custom-call(f32[24,256]{1,0:T(8,128)S(1)} %get-tuple-element.29.orde, ...), custom_call_target="tpu_custom_call" | custom-call | tf_op jit(solution)/shard_map/selectors/pallas_call | solution.py:580
  21.2 1.2 %trial_state.1.trial_ref = f32[8,8,1024]{2,1,0:T(8,128)S(1)} custom-call(f32[48,24]{1,0:T(8,128)S(1)} %get-tuple-element.30.matrix_ref, f32[3,1024]{1,0:T(4,128)S(1)} %get-tuple-element.31.disp_ref, f32[32,256]{1,0:T(8,128)S(1)} %collective-permute-done.ghost_ref.after_ref, s32[8,1024]{1,0:T(8,128)S(1)} %get-tuple-element.33.conn_ref, ...), custom_call_target="tpu_custom_call" | custom-call | tf_op jit(solution)/shard_map/trial_state/pallas_call | solution.py:628
  22.5 0.0 collective-permute-done.5.after_tail_ref
  22.5 2.4 %collective-permute-done.4.before_tail_ref = f32[2,2,8,256]{3,2,1,0:T(8,128)S(1)} collective-permute-done((f32[2,2,8,256]{3,2,1,0:T(8,128)S(1)}, f32[2,2,8,256]{3,2,1,0:T(8,128)S(1)}, u32[]{:S(2)}, u32[]{:S(2)}) %collective-permute-start.4) | collective-permute-done | bytes 32800 | tf_op jit(solution)/shard_map/ppermute | solution.py:575
  24.8 0.0 collective-permute-done.3.after_ref
  24.8 0.0 collective-permute-done.2.before_ref
  24.8 8.2 %seepage.1 = (f32[4,32,256]{2,1,0:T(8,128)}, f32[128,8,128]{2,1,0:T(8,128)S(1)}) custom-call(s32[2]{0:T(128)S(1)} %pad_add_fusion.place_ref, f32[32,256]{1,0:T(8,128)S(1)} %get-tuple-element.36.tables_ref, s32[128,128]{1,0:T(8,128)S(1)} %get-tuple-element.37.index, f32[2,3,32,256]{3,2,1,0:T(8,128)S(1)} %get-tuple-element.38.low_ref, ...), custom_call_target="tpu_custom_call" | custom-call | tf_op jit(solution)/shard_map/seepage/pallas_call | solution.py:639
  33.1 23.1 %all_to_all.5 = f32[128,8,128]{2,1,0:T(8,128)S(1)} all-to-all(f32[128,8,128]{2,1,0:T(8,128)S(1)} %get-tuple-element.44), channel_id=1, replica_groups=mesh['crest'=16,'section'=8] {'crest','section'}, dimensions={0} | all-to-all | bytes 1048576 | tf_op jit(solution)/shard_map/all_to_all | solution.py:647
  56.2 0.0 copy-start
  56.2 3.1 %final_state.1 = (f32[6,8,1024]{2,1,0:T(8,128)}, f32[8,1024]{1,0:T(8,128)}, f32[24,128]{1,0:T(8,128)S(1)}, f32[12,128]{1,0:T(8,128)S(1)}) custom-call(f32[24,48]{1,0:T(8,128)S(1)} %get-tuple-element.43.matrix_ref, f32[1024,128]{1,0:T(8,128)S(1)} %bitcast.12, bf16[1024,1024]{1,0:T(8,128)(2,1)S(1)} %get-tuple-element.45.row_ref, ...), custom_call_target="tpu_custom_call" | custom-call | tf_op jit(solution)/shard_map/final_state/pallas_call | solution.py:649
  59.2 0.0 collective-permute-start.6
  59.2 8.5 %collective-permute-done.6.ghost_ref = f32[12,128]{1,0:T(8,128)S(1)} collective-permute-done((f32[12,128]{1,0:T(8,128)S(1)}, f32[12,128]{1,0:T(8,128)S(1)}, u32[]{:S(2)}, u32[]{:S(2)}) %collective-permute-start.6) | collective-permute-done | bytes 6176 | tf_op jit(solution)/shard_map/ppermute | solution.py:656
  67.7 0.0 copy-done
  67.7 0.8 %add_returned.1 = f32[3,1024]{1,0:T(4,128)} custom-call(f32[24,128]{1,0:T(8,128)S(1)} %get-tuple-element.52.own_ref, f32[12,128]{1,0:T(8,128)S(1)} %collective-permute-done.6.ghost_ref, s32[4,128]{1,0:T(4,128)S(1)} %bitcast.14), custom_call_target="tpu_custom_call" | custom-call | tf_op jit(solution)/shard_map/add_returned/pallas_call | solution.py:657
Async XLA Ops:
  1.8 23.1 %collective-permute-start.3 = (f32[2,3,32,256]{3,2,1,0:T(8,128)S(1)}, f32[2,3,32,256]{3,2,1,0:T(8,128)S(1)}, u32[]{:S(2)}, u32[]{:S(2)}) collective-permute-start(f32[2,3,32,256]{3,2,1,0:T(8,128)S(1)} %get-tuple-element.38.low_ref), channel_id=1, source_target_pairs={{0,120},{8,0},{16,8},{24,16},{32,24},{40,32},{48,40},{56,48},{64,5... | collective-permute-start | bytes 589832 | tf_op jit(solution)/shard_map/ppermute | solution.py:569
  7.1 17.7 %collective-permute-start.2 = (f32[2,3,32,256]{3,2,1,0:T(8,128)S(1)}, f32[2,3,32,256]{3,2,1,0:T(8,128)S(1)}, u32[]{:S(2)}, u32[]{:S(2)}) collective-permute-start(f32[2,3,32,256]{3,2,1,0:T(8,128)S(1)} %get-tuple-element.39.high_ref), channel_id=1, source_target_pairs={{0,8},{8,16},{16,24},{24,32},{32,40},{40,48},{48,56},{56,64},{64,7... | collective-permute-start | bytes 589832 | tf_op jit(solution)/shard_map/ppermute | solution.py:568
  7.1 7.8 %collective-permute-start.1 = (f32[24,256]{1,0:T(8,128)S(1)}, f32[24,256]{1,0:T(8,128)S(1)}, u32[]{:S(2)}, u32[]{:S(2)}) collective-permute-start(f32[24,256]{1,0:T(8,128)S(1)} %get-tuple-element.29.order_ref), channel_id=1, source_target_pairs={{0,1},{1,2},{2,3},{3,4},{4,5},{5,6},{6,7},{7,0},{8,9},{9,10},{10,1... | collective-permute-start | bytes 73736 | tf_op jit(solution)/shard_map/ppermute | solution.py:566
  7.1 9.3 %collective-permute-start = (f32[32,256]{1,0:T(8,128)S(1)}, f32[32,256]{1,0:T(8,128)S(1)}, u32[]{:S(2)}, u32[]{:S(2)}) collective-permute-start(f32[32,256]{1,0:T(8,128)S(1)} %get-tuple-element.32), channel_id=1, source_target_pairs={{0,127},{1,0},{2,1},{3,2},{4,3},{5,4},{6,5},{7,6},{8,7},{9,8},{10,... | collective-permute-start | bytes 98312 | tf_op jit(solution)/shard_map/ppermute | solution.py:567
  17.0 5.4 %collective-permute-start.5 = (f32[2,2,8,256]{3,2,1,0:T(8,128)S(1)}, f32[2,2,8,256]{3,2,1,0:T(8,128)S(1)}, u32[]{:S(2)}, u32[]{:S(2)}) collective-permute-start(f32[2,2,8,256]{3,2,1,0:T(8,128)S(1)} %get-tuple-element.40.low_tail_ref), channel_id=1, source_target_pairs={{0,120},{8,0},{16,8},{24,16},{32,24},{40,32},{48,40},{56,48},{64,5... | collective-permute-start | bytes 98312 | tf_op jit(solution)/shard_map/ppermute | solution.py:576
  17.6 7.2 %collective-permute-start.4 = (f32[2,2,8,256]{3,2,1,0:T(8,128)S(1)}, f32[2,2,8,256]{3,2,1,0:T(8,128)S(1)}, u32[]{:S(2)}, u32[]{:S(2)}) collective-permute-start(f32[2,2,8,256]{3,2,1,0:T(8,128)S(1)} %get-tuple-element.41.high_tail_ref), channel_id=1, source_target_pairs={{0,8},{8,16},{16,24},{24,32},{32,40},{40,48},{48,56},{56,64},{64,7... | collective-permute-start | bytes 98312 | tf_op jit(solution)/shard_map/ppermute | solution.py:575
  56.2 11.6 %copy-start = (s32[512]{0:T(512)S(1)}, s32[512]{0:T(512)}, u32[]{:S(2)}) copy-start(s32[512]{0:T(512)} %param.26) | copy-start | bytes 6148
  59.2 8.5 %collective-permute-start.6 = (f32[12,128]{1,0:T(8,128)S(1)}, f32[12,128]{1,0:T(8,128)S(1)}, u32[]{:S(2)}, u32[]{:S(2)}) collective-permute-start(f32[12,128]{1,0:T(8,128)S(1)} %get-tuple-element.53), channel_id=1, source_target_pairs={{0,1},{1,2},{2,3},{3,4},{4,5},{5,6},{6,7},{7,8},{8,9},{9,10},{10,1... | collective-permute-start | bytes 18440 | tf_op jit(solution)/shard_map/ppermute | solution.py:656

commit v4 on v3

--- a/solution.py
+++ b/solution.py
@@ -67,42 +67,29 @@
     return table if index is None else take_lanes(table, index)
 
 
-def pack_edges(
-    head_hbm,
-    zone_hbm,
-    disp_hbm,
-    shared_hbm,
-    forward_ref,
-    backward_ref,
-    low_ref,
-    high_ref,
-    head_ref,
-    zone_ref,
-    disp_ref,
-    shared_ref,
-    sems,
-):
-    copies = [
-        pltpu.make_async_copy(source, target, sems.at[i])
-        for i, (source, target) in enumerate(
-            [(head_hbm, head_ref), (zone_hbm, zone_ref), (disp_hbm, disp_ref), (shared_hbm, shared_ref)]
-        )
-    ]
+def fetch(pairs, sems):
+    copies = [pltpu.make_async_copy(source, target, sems.at[i]) for i, (source, target) in enumerate(pairs)]
     for copy in copies:
         copy.start()
     for copy in copies:
         copy.wait()
+
+
+def pack_section(
+    head_hbm, zone_hbm, disp_hbm, shared_hbm, forward_ref, backward_ref, head_ref, zone_ref, disp_ref, shared_ref, sems
+):
+    fetch([(head_hbm, head_ref), (zone_hbm, zone_ref), (disp_hbm, disp_ref), (shared_hbm, shared_ref)], sems)
     planes, rows = head_ref.shape[0], head_ref.shape[1]
     for x in range(planes):
         for field in range(2):
-            own = head_ref[x] if field == 0 else zone_ref[x].astype(jnp.float32) + 1.0
+            first, last = slice(0, WIDE), slice(rows - WIDE, rows)
             at = field * WIDE * planes + WIDE * x
-            forward_ref[at : at + WIDE, :] = own[rows - WIDE : rows, :]
-            backward_ref[at : at + WIDE, :] = own[0:WIDE, :]
-            if x < WIDE:
-                low_ref[field, x] = own
-            if x >= planes - WIDE:
-                high_ref[field, x - planes + WIDE] = own
+            if field == 0:
+                forward_ref[at : at + WIDE, :] = head_ref[x, last, :]
+                backward_ref[at : at + WIDE, :] = head_ref[x, first, :]
+            else:
+                forward_ref[at : at + WIDE, :] = zone_ref[x, last, :].astype(jnp.float32) + 1.0
+                backward_ref[at : at + WIDE, :] = zone_ref[x, first, :].astype(jnp.float32) + 1.0
     index = shared_ref[...]
     index = jnp.concatenate([index, index], axis=0)
     lanes, segment = index & 127, index >> 7
@@ -117,8 +104,51 @@
     backward_ref[30:32, :] = jnp.zeros((2, 256), jnp.float32)
 
 
+def pack_crest(
+    head_ref,
+    zone_ref,
+    wanted_hbm,
+    alpha_hbm,
+    expo_hbm,
+    ks_hbm,
+    low_ref,
+    high_ref,
+    tables_ref,
+    index_ref,
+    wanted_ref,
+    alpha_ref,
+    expo_ref,
+    ks_ref,
+    sems,
+):
+    pairs = [(wanted_hbm, wanted_ref), (alpha_hbm, alpha_ref), (expo_hbm, expo_ref), (ks_hbm, ks_ref)]
+    copies = [pltpu.make_async_copy(source, target, sems.at[i]) for i, (source, target) in enumerate(pairs)]
+    for copy in copies:
+        copy.start()
+    planes = head_ref.shape[0]
+    for x in range(planes):
+        own = [head_ref[x], zone_ref[x].astype(jnp.float32) + 1.0]
+        for field in range(2):
+            if x < WIDE:
+                low_ref[field, x] = own[field]
+            if x >= planes - WIDE:
+                high_ref[field, x - planes + WIDE] = own[field]
+    for copy in copies:
+        copy.wait()
+    zones, width = alpha_ref.shape[0], tables_ref.shape[1]
+    for z in range(zones):
+        expo = jnp.full((1, width), expo_ref[z], jnp.float32)
+        expo = jnp.where(expo > 0, expo, 2.0)
+        tables_ref[z : z + 1, :] = jnp.full((1, width), alpha_ref[z], jnp.float32)
+        tables_ref[zones + z : zones + z + 1, :] = expo - 1.0
+        tables_ref[2 * zones + z : 2 * zones + z + 1, :] = -0.25 * (1.0 - 1.0 / expo)
+        tables_ref[3 * zones + z : 3 * zones + z + 1, :] = jnp.sqrt(jnp.full((1, width), ks_ref[z], jnp.float32))
+    wanted = wanted_ref[...]
+    index_ref[...] = jnp.concatenate([wanted, pltpu.roll(wanted, wanted.shape[1] // 2, 1)], axis=0).T
+
+
 def pack_corners(sections, place_ref, before_ref, after_ref, low_ref, high_ref):
-    planes = low_ref.shape[1] + high_ref.shape[1]
+    planes = high_ref.shape[0]
     behind = jnp.where(place_ref[0] > 0, 1.0, 0.0)
     ahead = jnp.where(place_ref[0] < sections - 1, 1.0, 0.0)
     for x in range(planes):
@@ -133,9 +163,10 @@
                 axis=0,
             )
             if x < 2:
-                low_ref[field, x] = tail
+                low_ref[2 * field + x] = tail
             else:
-                high_ref[field, x - 2] = tail
+                high_ref[2 * field + x - 2] = tail
+    low_ref[4] = after_ref[24:32, :]
 
 
 def seepage(
@@ -153,6 +184,7 @@
     after_tail_ref,
     head_ref,
     out_ref,
+    order_ref,
     h,
     alpha_f,
     less_f,
@@ -210,10 +242,10 @@
 
     @pl.loop(0, 2)
     def _(x):
-        fields(1 + x, rows, before_tail_ref[0, x], before_tail_ref[1, x] * behind)
-        fields(3 + x, rows, low_tail_ref[0, x], low_tail_ref[1, x])
-        fields(5 + x, rows, high_tail_ref[0, x], high_tail_ref[1, x])
-        fields(7 + x, rows, after_tail_ref[0, x], after_tail_ref[1, x] * ahead)
+        fields(1 + x, rows, before_tail_ref[x], before_tail_ref[2 + x] * behind)
+        fields(3 + x, rows, low_tail_ref[x], low_tail_ref[2 + x])
+        fields(5 + x, rows, high_tail_ref[x], high_tail_ref[2 + x])
+        fields(7 + x, rows, after_tail_ref[x], after_tail_ref[2 + x] * ahead)
 
     for x in (0, total - 1):
         for field in (h, alpha_f, less_f, m_f, root_f, gain_f):
@@ -264,14 +296,19 @@
     deep[...] = table[...].T
     bands = depth // BAND
 
+    order_ref[...] = deep[0:8, :]
+    half = out_ref.shape[0] // 2
+
     @pl.loop(0, bands)
     def _(b):
         upper = deep[pl.ds(pl.multiple_of(b * BAND, 8), 8), :]
         lower = deep[pl.ds(pl.multiple_of(b * BAND + 8, 8), 8), :]
-        for group in range(out_ref.shape[0] // bands):
+        for group in range(half // bands):
             d = group * bands + b
             columns = jnp.broadcast_to(index[pl.ds(d, 1), :], (8, 128))
-            out_ref[d] = jnp.where(lane8 < 64, take_lanes(upper, columns), take_lanes(lower, columns))
+            first, second = take_lanes(upper, columns), pltpu.roll(take_lanes(lower, columns), 64, 1)
+            out_ref[d] = jnp.where(lane8 < 64, first, second)
+            out_ref[half + d] = jnp.where(lane8 < 64, second, first)
 
 
 def element_rows(value):
@@ -279,6 +316,8 @@
 
 
 def selectors(
+    partitions,
+    place_ref,
     order_ref,
     disp_hbm,
     stress_hbm,
@@ -288,10 +327,6 @@
     slot_hbm,
     depth_hbm,
     zone_hbm,
-    wanted_hbm,
-    alpha_hbm,
-    expo_hbm,
-    ks_hbm,
     cohesion_hbm,
     friction_hbm,
     disp_ref,
@@ -299,61 +334,36 @@
     conn_ref,
     strain_ref,
     force_ref,
-    row_ref,
-    node_ref,
     strength_ref,
-    lane_ref,
-    tables_ref,
-    index_ref,
+    at_ref,
     slot_ref,
     depth_ref,
     zone_ref,
-    wanted_ref,
-    alpha_ref,
-    expo_ref,
-    ks_ref,
     cohesion_ref,
     friction_ref,
     sems,
 ):
     del order_ref
-    pairs = [
-        (conn_hbm, conn_ref),
-        (slot_hbm, slot_ref),
-        (depth_hbm, depth_ref),
-        (zone_hbm, zone_ref),
-        (wanted_hbm, wanted_ref),
-        (alpha_hbm, alpha_ref),
-        (expo_hbm, expo_ref),
-        (ks_hbm, ks_ref),
-        (cohesion_hbm, cohesion_ref),
-        (friction_hbm, friction_ref),
-        (disp_hbm, disp_ref),
-        (stress_hbm, stress_ref),
-        (strain_hbm, strain_ref),
-        (force_hbm, force_ref),
-    ]
-    copies = [pltpu.make_async_copy(source, target, sems.at[i]) for i, (source, target) in enumerate(pairs)]
-    for copy in copies:
-        copy.start()
-    for copy in copies:
-        copy.wait()
+    fetch(
+        [
+            (conn_hbm, conn_ref),
+            (slot_hbm, slot_ref),
+            (depth_hbm, depth_ref),
+            (zone_hbm, zone_ref),
+            (cohesion_hbm, cohesion_ref),
+            (friction_hbm, friction_ref),
+            (disp_hbm, disp_ref),
+            (stress_hbm, stress_ref),
+            (strain_hbm, strain_ref),
+            (force_hbm, force_ref),
+        ],
+        sems,
+    )
     elems = conn_ref.shape[1]
     slot, depth = slot_ref[...], depth_ref[...]
-    row = element_rows((slot >> 6) * 8 + (depth & 7))
-    lane_ref[...] = element_rows((depth >> 3) * 64 + (slot & 63))
-    in_lane = lax.broadcasted_iota(jnp.int32, (128, elems), 0)
-
-    @pl.loop(0, row_ref.shape[0] // 128)
-    def _(part):
-        first = pl.multiple_of(part * 128, 128)
-        row_ref[pl.ds(first, 128), :] = jnp.where(in_lane == row - first, 1.0, 0.0).astype(jnp.bfloat16)
-
-    @pl.loop(0, 8)
-    def _(corner):
-        node = conn_ref[pl.ds(corner, 1), :] & 127
-        node_ref[corner] = jnp.where(in_lane == node, 1.0, 0.0).astype(jnp.bfloat16)
-
+    swap = jnp.where(place_ref[2] >= partitions // 2, 1, 0)
+    at_ref[0:1, :] = element_rows((slot >> 6) * 8 + (depth & 7))
+    at_ref[1:2, :] = element_rows(((depth >> 3) ^ swap) * 64 + (slot & 63))
     zone = zone_ref[...]
     tan_red = pick(friction_ref, zone) * (1.0 / REDUCTION)
     cos_red = 1.0 / jnp.sqrt(1.0 + tan_red * tan_red)
@@ -362,25 +372,17 @@
     strength_ref[0:1, :] = element_rows(common * (pick(cohesion_ref, zone) * (1.0 / REDUCTION)) * cos_red)
     strength_ref[1:2, :] = element_rows(common * sin_red)
 
-    zones, width = alpha_ref.shape[0], tables_ref.shape[1]
-    for z in range(zones):
-        expo = jnp.full((1, width), expo_ref[z], jnp.float32)
-        expo = jnp.where(expo > 0, expo, 2.0)
-        tables_ref[z : z + 1, :] = jnp.full((1, width), alpha_ref[z], jnp.float32)
-        tables_ref[zones + z : zones + z + 1, :] = expo - 1.0
-        tables_ref[2 * zones + z : 2 * zones + z + 1, :] = -0.25 * (1.0 - 1.0 / expo)
-        tables_ref[3 * zones + z : 3 * zones + z + 1, :] = jnp.sqrt(jnp.full((1, width), ks_ref[z], jnp.float32))
-    wanted = wanted_ref[...]
-    index_ref[...] = jnp.concatenate([wanted, wanted], axis=0).T
-
-
-def trial_state(matrix_ref, disp_ref, ghost_ref, conn_ref, stress_ref, trial_ref, nodes, corners):
+
+def trial_state(
+    sections, place_ref, matrix_ref, disp_ref, after_ref, tail_ref, conn_ref, stress_ref, trial_ref, nodes, corners
+):
+    ghost = jnp.where(place_ref[0] < sections - 1, after_ref[24:32, :], tail_ref[4])
     for comp in range(3):
         for s in range(8):
             nodes[comp * 12 + s : comp * 12 + s + 1, :] = disp_ref[comp : comp + 1, s * 128 : (s + 1) * 128]
         for s in range(4):
-            at = 24 + 2 * comp + s // 2
-            nodes[comp * 12 + 8 + s : comp * 12 + 9 + s, :] = ghost_ref[at : at + 1, (s % 2) * 128 : (s % 2 + 1) * 128]
+            at = 2 * comp + s // 2
+            nodes[comp * 12 + 8 + s : comp * 12 + 9 + s, :] = ghost[at : at + 1, (s % 2) * 128 : (s % 2 + 1) * 128]
     elems = conn_ref.shape[1]
 
     @pl.loop(0, elems, step=128)
@@ -423,19 +425,20 @@
 
 
 def final_state(
-    matrix_ref, band_ref, row_ref, lane_ref, node_ref, strength_ref, trial_ref, conn_ref, stress_ref, release_ref, own_ref, ghost_ref
+    matrix_ref, band_ref, at_ref, strength_ref, trial_ref, conn_ref, stress_ref, release_ref, own_ref, ghost_ref
 ):
     elems = conn_ref.shape[1]
     high, low = halves(band_ref[...])
+    in_row = lax.broadcasted_iota(jnp.int32, (band_ref.shape[0], elems), 0) == at_ref[0:1, :]
     found = lax.dot_general(
         jnp.concatenate([high, low], axis=1).astype(jnp.bfloat16),
-        row_ref[...],
+        jnp.where(in_row, 1.0, 0.0).astype(jnp.bfloat16),
         (((0,), (0,)), ((), ())),
         preferred_element_type=jnp.float32,
     )
     found = found[0:128] + found[128:256]
     in_lane = lax.broadcasted_iota(jnp.int32, (128, elems), 0)
-    pore = jnp.sum(jnp.where(in_lane == lane_ref[...], found, 0.0), axis=0, keepdims=True)
+    pore = jnp.sum(jnp.where(in_lane == at_ref[1:2, :], found, 0.0), axis=0, keepdims=True)
     allow = jnp.maximum(strength_ref[0:1, :] - strength_ref[1:2, :] * (trial_ref[6] + pore), 0.0)
     deviator = trial_ref[7]
     yielded = deviator > allow
@@ -463,7 +466,8 @@
                 value = source[comp * 8 + corner : comp * 8 + corner + 1, :]
                 rows.append(jnp.where(here, jnp.broadcast_to(value, in_segment.shape), 0.0))
         left = jnp.concatenate(rows, axis=0).astype(jnp.bfloat16)
-        total += lax.dot_general(left, node_ref[corner], (((1,), (1,)), ((), ())), preferred_element_type=jnp.float32)
+        right = jnp.where(jnp.broadcast_to(node & 127, in_lane.shape) == in_lane, 1.0, 0.0).astype(jnp.bfloat16)
+        total += lax.dot_general(left, right, (((1,), (1,)), ((), ())), preferred_element_type=jnp.float32)
     total = total[0:48] + total[48:96]
     for comp in range(3):
         own_ref[comp * 8 : comp * 8 + 8, :] = total[comp * 16 : comp * 16 + 8]
@@ -547,112 +551,100 @@
     elems = connectivity.shape[1]
     nodes = displacement.shape[1]
     shared = shared_nodes.reshape(4, 128)
-    place = jnp.stack([lax.axis_index("section"), lax.axis_index("crest")])
-
-    own = (2, WIDE, rows, depth)
-    forward, backward, low, high = call(
-        pack_edges,
+    zones = retention_alpha.shape[0]
+    place = jnp.stack([lax.axis_index("section"), lax.axis_index("crest"), lax.axis_index(AXES)])
+    i32, f32 = jnp.int32, jnp.float32
+
+    forward, backward, head, zone = call(
+        pack_section,
         [HBM] * 4,
-        [(2 * WIDE * planes, depth), (32, depth), own, own],
-        [
-            pltpu.VMEM(pressure_head.shape, jnp.float32),
-            pltpu.VMEM(zone_ids.shape, jnp.int32),
-            pltpu.VMEM(displacement.shape, jnp.float32),
-            pltpu.VMEM(shared.shape, jnp.int32),
-            pltpu.SemaphoreType.DMA((4,)),
-        ],
-        "pack_edges",
+        [(2 * WIDE * planes, depth), (32, depth), pressure_head.shape, zone_ids.shape],
+        [pltpu.VMEM(displacement.shape, f32), pltpu.VMEM(shared.shape, i32), pltpu.SemaphoreType.DMA((4,))],
+        "pack_section",
+        [f32, f32, f32, i32],
     )(*(in_hbm(x) for x in (pressure_head, zone_ids, displacement, shared)))
     before = lax.ppermute(forward, "section", steps(section, 1))
-    after = lax.ppermute(backward, AXES, steps(devices, -1))
+    after = lax.ppermute(backward, "section", steps(section, -1))
+
+    own = (2, WIDE, rows, depth)
+    low, high, tables, index = call(
+        pack_crest,
+        [VM] * 2 + [HBM] * 4,
+        [own, own, (4 * zones, depth), (devices, 128)],
+        [pltpu.VMEM((64, devices), i32)] + [pltpu.SMEM((zones,), f32)] * 3 + [pltpu.SemaphoreType.DMA((4,))],
+        "pack_crest",
+        [f32, f32, f32, i32],
+    )(head, zone, *(in_hbm(x) for x in (sent_columns[0].T, retention_alpha, retention_exponent, conductivity)))
     west = lax.ppermute(high, "crest", steps(crest, 1))
     east = lax.ppermute(low, "crest", steps(crest, -1))
 
-    tails = (2, 2, 8, depth)
     low_tail, high_tail = call(
-        functools.partial(pack_corners, section), [SM] + [VM] * 2, [tails, tails], [], "pack_corners"
+        functools.partial(pack_corners, section), [SM] + [VM] * 2, [(5, 8, depth), (4, 8, depth)], [], "pack_corners"
     )(place, before, after)
     west_tail = lax.ppermute(high_tail, "crest", steps(crest, 1))
     east_tail = lax.ppermute(low_tail, "crest", steps(crest, -1))
 
-    zones = retention_alpha.shape[0]
+    total = planes + 2 * WIDE
+    field = pltpu.VMEM((total, height, depth), f32)
+    head_out, outgoing, order = call(
+        functools.partial(seepage, crest),
+        [SM] + [VM] * 10,
+        [pressure_head.shape, (devices, 8, 128), (8, 128)],
+        [field] * 8 + [pltpu.VMEM((planes * rows, depth), f32), pltpu.VMEM((depth, planes * rows), f32)],
+        "seepage",
+    )(place, tables, index, low, high, low_tail, high_tail, west, east, west_tail, east_tail)
+
     matrix = component_major()
-    disp, stress, conn, strain_matrix_v, force_matrix, row_hot, node_hot, strength, lane, tables, index = call(
-        selectors,
-        [VM] + [HBM] * 14,
+    disp, stress, conn, strain_rows, force_rows, strength, places = call(
+        functools.partial(selectors, devices),
+        [SM, VM] + [HBM] * 10,
         [
             displacement.shape,
             (6, 8, elems),
             connectivity.shape,
             (48, 24),
             (24, 48),
-            (devices * 8, elems),
-            (8, 128, elems),
             (2, elems),
-            (1, elems),
-            (4 * zones, depth),
-            (devices, 128),
+            (2, elems),
         ],
-        [pltpu.VMEM((8, 128), jnp.int32)] * 3
-        + [pltpu.VMEM((64, devices), jnp.int32)]
-        + [pltpu.SMEM((zones,), jnp.float32)] * 5
-        + [pltpu.SemaphoreType.DMA((14,))],
+        [pltpu.VMEM((8, 128), i32)] * 3 + [pltpu.SMEM((zones,), f32)] * 2 + [pltpu.SemaphoreType.DMA((10,))],
         "selectors",
-        [jnp.float32] * 2
-        + [jnp.int32]
-        + [jnp.float32] * 2
-        + [jnp.bfloat16] * 2
-        + [jnp.float32, jnp.int32, jnp.float32, jnp.int32],
+        [f32, f32, i32, f32, f32, f32, i32],
     )(
-        forward,
+        place,
+        order,
         *(
             in_hbm(x)
             for x in (
                 displacement,
                 stress_old.transpose(1, 0, 2),
                 connectivity,
-                jnp.asarray(matrix, jnp.float32),
-                jnp.asarray(matrix.T * 0.125, jnp.float32),
+                jnp.asarray(matrix, f32),
+                jnp.asarray(matrix.T * 0.125, f32),
                 element_slot.reshape(8, 128),
                 element_depth.reshape(8, 128),
                 element_zone.reshape(8, 128),
-                sent_columns[0].T,
-                retention_alpha,
-                retention_exponent,
-                conductivity,
                 cohesion,
                 friction,
             )
         ),
     )
     (trial,) = call(
-        trial_state,
-        [VM] * 5,
+        functools.partial(trial_state, section),
+        [SM] + [VM] * 6,
         [(8, 8, elems)],
-        [pltpu.VMEM((40, 128), jnp.float32), pltpu.VMEM((24, elems), jnp.float32)],
+        [pltpu.VMEM((40, 128), f32), pltpu.VMEM((24, elems), f32)],
         "trial_state",
-    )(strain_matrix_v, disp, after, conn, stress)
-
-    trial, tables = lax.optimization_barrier((trial, tables))
-    total = planes + 2 * WIDE
-    field = pltpu.VMEM((total, height, depth), jnp.float32)
-    head_out, outgoing = call(
-        functools.partial(seepage, crest),
-        [SM] + [VM] * 10,
-        [pressure_head.shape, (devices, 8, 128)],
-        [field] * 8
-        + [pltpu.VMEM((planes * rows, depth), jnp.float32), pltpu.VMEM((depth, planes * rows), jnp.float32)],
-        "seepage",
-    )(place, tables, index, low, high, low_tail, high_tail, west, east, west_tail, east_tail)
+    )(place, strain_rows, disp, after, east_tail, conn, stress)
     incoming = lax.all_to_all(outgoing, AXES, split_axis=0, concat_axis=0, tiled=True)
 
     stress_new, release, own, ghost = call(
         final_state,
-        [VM] * 8,
+        [VM] * 6,
         [(6, 8, elems), (8, elems), (24, 128), (12, 128)],
         [],
         "final_state",
-    )(force_matrix, incoming.reshape(devices * 8, 128), row_hot, lane, node_hot, strength, trial, conn)
+    )(force_rows, incoming.reshape(devices * 8, 128), places, strength, trial, conn)
     returned = lax.ppermute(ghost, AXES, steps(devices, 1))
     (node_forces,) = call(add_returned, [VM] * 3, [(3, nodes)], [], "add_returned")(own, returned, shared)
     return (head_out, stress_new.transpose(1, 0, 2), release, node_forces)

time: 68.7 us -> 66.1 us (0.962)
  blocking collectives: 23.1 us -> 0 us
  waiting for transfers between devices: 12.4 us -> 27.5 us
  starting transfers between devices: 15.2 us -> 18.5 us
  Pallas kernels: 17.1 us -> 19.1 us
    all_to_all x1 -> x0, blocking collectives: 23.1 us -> none  [per_device(): lax.all_to_all(outgoing, AXES, split_axis=0, concat_axis=0, tiled=True)]
    all_to_all x0 -> x1, waiting for transfers between devices: none -> 10.2 us  [per_device(): lax.all_to_all(outgoing, AXES, split_axis=0, concat_axis=0, tiled=True)]
    ppermute x1, waiting for transfers between devices: 2.36 us -> 7.23 us  [per_device(): west_tail = lax.ppermute(high_tail, 'crest', steps(crest, 1))]
    all_to_all x0 -> x1, starting transfers between devices: none -> 4.76 us  [per_device(): lax.all_to_all(outgoing, AXES, split_axis=0, concat_axis=0, tiled=True)]
    ppermute x1, starting transfers between devices: 0.54 us -> 5.17 us  [per_device(): east_tail = lax.ppermute(low_tail, 'crest', steps(crest, -1))]
    ppermute x1, starting transfers between devices: 7.73 us -> 3.2 us  [per_device(): after = lax.ppermute(backward, 'section', steps(section, -1))]
    ppermute x1, starting transfers between devices: 1.55 us -> 0.01 us  [per_device(): west_tail = lax.ppermute(high_tail, 'crest', steps(crest, 1))]
    ppermute x1, waiting for transfers between devices: 1.52 us -> 0.09 us  [per_device(): after = lax.ppermute(backward, 'section', steps(section, -1))]
  transfers between devices with their start and end apart: 7 -> 8, of which waited for: 3 -> 5; matrix products, arithmetic and copies ran while one was open for 0% -> 0% of each run, Pallas kernels for 6% -> 6%
where the time goes in v4:
time: 66.1 us; the launch traced here: 65.9 us
  waiting for transfers between devices  27.5 us (42%)
  Pallas kernels  19.1 us (29%)
  starting transfers between devices  18.5 us (28%)
  between operations  0.69 us (1%)
    all_to_all x1, waiting for transfers between devices, per_device(): lax.all_to_all(outgoing, AXES, split_axis=0, concat_axis=0, tiled=True)  10.2 us
    pallas_call x1, Pallas kernels, per_device(): call(functools.partial(seepage, crest), [SM] + [VM] * 10, [pressure_head....  9.18 us
    ppermute x1, waiting for transfers between devices, per_device(): returned = lax.ppermute(ghost, AXES, steps(devices, 1))  8.5 us
    ppermute x1, waiting for transfers between devices, per_device(): west_tail = lax.ppermute(high_tail, 'crest', steps(crest, 1))  7.23 us
    ppermute x1, starting transfers between devices, per_device(): east = lax.ppermute(low, 'crest', steps(crest, -1))  5.36 us
    ppermute x1, starting transfers between devices, per_device(): east_tail = lax.ppermute(low_tail, 'crest', steps(crest, -1))  5.17 us
    all_to_all x1, starting transfers between devices, per_device(): lax.all_to_all(outgoing, AXES, split_axis=0, concat_axis=0, tiled=True)  4.76 us
    ppermute x1, starting transfers between devices, per_device(): after = lax.ppermute(backward, 'section', steps(section, -1))  3.2 us
  transfers between devices with their start and end apart: 8, of which 5 were waited for; matrix products, arithmetic and copies ran while one was open for 0% of the time, Pallas kernels for 6%

profile of v4, /device:TPU:0, one launch (start us, length us, event | category | flops | bytes accessed | tf_op | source)
XLA Modules:
  0.0 65.9 jit_solution(9566842974671633466)
XLA Ops:
  0.6 1.1 %pack_section.1 = (f32[24,256]{1,0:T(8,128)S(1)}, f32[32,256]{1,0:T(8,128)S(1)}, f32[4,32,256]{2,1,0:T(8,128)S(1)}, s32[4,32,256]{2,1,0:T(8,128)S(1)}) custom-call(f32[4,32,256]{2,1,0:T(8,128)} %head_hbm.1, s32[4,32,256]{2,1,0:T(8,128)} %zone_hbm.1, f32[3,1024]{1,0:T(4,128)} %disp_hbm.3, s32[4,128]{1,0:T(4,128)} %bitcast.14), custom_call_target="tpu_custom_call" | custom-call | tf_op jit(solution)/shard_map/pack_section/pallas_call | solution.py:558
  1.8 1.0 %pack_crest.1 = (f32[2,3,32,256]{3,2,1,0:T(8,128)S(1)}, f32[2,3,32,256]{3,2,1,0:T(8,128)S(1)}, f32[32,256]{1,0:T(8,128)S(1)}, s32[128,128]{1,0:T(8,128)S(1)}) custom-call(f32[4,32,256]{2,1,0:T(8,128)S(1)} %get-tuple-element.28.head_ref, s32[4,32,256]{2,1,0:T(8,128)S(1)} %get-tuple-element.29.zone_ref, s32[64,128]{1,0:T(8,128)} %bitcast.17, f32[8]{0:T(128)} %alpha_hbm.1, ...), custom_call_target="tpu_custom_call" | custom-call | tf_op jit(solution)/shard_map/pack_crest/pallas_call | solution.py:570
  2.8 5.4 %collective-permute-start.3 = (f32[2,3,32,256]{3,2,1,0:T(8,128)S(1)}, f32[2,3,32,256]{3,2,1,0:T(8,128)S(1)}, u32[]{:S(2)}, u32[]{:S(2)}) collective-permute-start(f32[2,3,32,256]{3,2,1,0:T(8,128)S(1)} %get-tuple-element.32.low_ref), channel_id=1, source_target_pairs={{0,120},{8,0},{16,8},{24,16},{32,24},{40,32},{48,40},{56,48},{64,5... | collective-permute-start | bytes 589832 | tf_op jit(solution)/shard_map/ppermute | solution.py:579
  8.1 0.0 collective-permute-start.2
  8.1 0.0 collective-permute-start
  8.1 3.2 %collective-permute-start.1 = (f32[32,256]{1,0:T(8,128)S(1)}, f32[32,256]{1,0:T(8,128)S(1)}, u32[]{:S(2)}, u32[]{:S(2)}) collective-permute-start(f32[32,256]{1,0:T(8,128)S(1)} %get-tuple-element.35), channel_id=1, source_target_pairs={{0,7},{1,0},{2,1},{3,2},{4,3},{5,4},{6,5},{7,6},{8,15},{9,8},{10,9... | collective-permute-start | bytes 98312 | tf_op jit(solution)/shard_map/ppermute | solution.py:567
  11.3 0.1 pad_add_fusion.place_ref
  11.4 1.4 %collective-permute-done.before_ref = f32[24,256]{1,0:T(8,128)S(1)} collective-permute-done((f32[24,256]{1,0:T(8,128)S(1)}, f32[24,256]{1,0:T(8,128)S(1)}, u32[]{:S(2)}, u32[]{:S(2)}) %collective-permute-start) | collective-permute-done | bytes 24608 | tf_op jit(solution)/shard_map/ppermute | solution.py:566
  12.8 0.1 collective-permute-done.1.after_ref
  12.9 0.6 pack_corners.1
  13.5 5.2 %collective-permute-start.5 = (f32[5,8,256]{2,1,0:T(8,128)S(1)}, f32[5,8,256]{2,1,0:T(8,128)S(1)}, u32[]{:S(2)}, u32[]{:S(2)}) collective-permute-start(f32[5,8,256]{2,1,0:T(8,128)S(1)} %get-tuple-element.36.low_tail_ref), channel_id=1, source_target_pairs={{0,120},{8,0},{16,8},{24,16},{32,24},{40,32},{48,40},{56,48},{64,5... | collective-permute-start | bytes 122888 | tf_op jit(solution)/shard_map/ppermute | solution.py:585
  18.7 0.0 collective-permute-start.4
  18.7 7.2 %collective-permute-done.4.before_tail_ref = f32[4,8,256]{2,1,0:T(8,128)S(1)} collective-permute-done((f32[4,8,256]{2,1,0:T(8,128)S(1)}, f32[4,8,256]{2,1,0:T(8,128)S(1)}, u32[]{:S(2)}, u32[]{:S(2)}) %collective-permute-start.4) | collective-permute-done | bytes 32800 | tf_op jit(solution)/shard_map/ppermute | solution.py:584
  25.9 0.0 collective-permute-done.5.after_tail_ref.tail_ref
  25.9 0.0 collective-permute-done.3.after_ref
  25.9 0.0 collective-permute-done.2.before_ref
  25.9 9.2 %seepage.1 = (f32[4,32,256]{2,1,0:T(8,128)}, f32[128,8,128]{2,1,0:T(8,128)}, f32[8,128]{1,0:T(8,128)S(1)}) custom-call(s32[3]{0:T(128)S(1)} %pad_add_fusion.place_ref, f32[32,256]{1,0:T(8,128)S(1)} %get-tuple-element.30.tables_ref, s32[128,128]{1,0:T(8,128)S(1)} %get-tuple-element.31.index, f32[2,3,32,256]{3,2,1,0:T(8,128)S(1)} %get-tuple-element.32.low_ref, ...), custom_call_target="tpu_custom_call" | custom-call | tf_op jit(solution)/shard_map/seepage/pallas_call | solution.py:589
  35.1 4.8 %all-to-all-start = ((f32[128,8,128]{2,1,0:T(8,128)}), f32[128,8,128]{2,1,0:T(8,128)S(1)}, u32[]{:S(2)}, u32[]{:S(2)}) async-start(f32[128,8,128]{2,1,0:T(8,128)} %get-tuple-element.41), calls=%async_computation | async-start | bytes 1048576 | tf_op jit(solution)/shard_map/all_to_all | solution.py:639
  39.9 1.8 %selectors.1 = (f32[3,1024]{1,0:T(4,128)S(1)}, f32[6,8,1024]{2,1,0:T(8,128)S(1)}, s32[8,1024]{1,0:T(8,128)S(1)}, f32[48,24]{1,0:T(8,128)S(1)}, f32[24,48]{1,0:T(...) custom-call(s32[3]{0:T(128)S(1)} %pad_add_fusion.place_ref, f32[8,128]{1,0:T(8,128)S(1)} %get-tuple-element.39.order_ref, ...), custom_call_target="tpu_custom_call" | custom-call | tf_op jit(solution)/shard_map/selectors/pallas_call | solution.py:598
  41.6 1.8 %trial_state.1.trial_ref = f32[8,8,1024]{2,1,0:T(8,128)S(1)} custom-call(s32[3]{0:T(128)S(1)} %pad_add_fusion.place_ref, f32[48,24]{1,0:T(8,128)S(1)} %get-tuple-element.44.matrix_ref, f32[3,1024]{1,0:T(4,128)S(1)} %get-tuple-element.45.disp_ref, f32[32,256]{1,0:T(8,128)S(1)} %collective-permute-done.1.after_ref, ...), custom_call_target="tpu_custom_call" | custom-call | tf_op jit(solution)/shard_map/trial_state/pallas_call | solution.py:632
  43.4 10.2 %all-to-all-done = f32[128,8,128]{2,1,0:T(8,128)S(1)} async-done(((f32[128,8,128]{2,1,0:T(8,128)}), f32[128,8,128]{2,1,0:T(8,128)S(1)}, u32[]{:S(2)}, u32[]{:S(2)}) %all-to-all-start) | async-done | bytes 524320 | tf_op jit(solution)/shard_map/all_to_all | solution.py:639
  53.6 2.9 %final_state.1 = (f32[6,8,1024]{2,1,0:T(8,128)}, f32[8,1024]{1,0:T(8,128)}, f32[24,128]{1,0:T(8,128)S(1)}, f32[12,128]{1,0:T(8,128)S(1)}) custom-call(f32[24,48]{1,0:T(8,128)S(1)} %get-tuple-element.40.matrix_ref, f32[1024,128]{1,0:T(8,128)S(1)} %bitcast.13, s32[2,1024]{1,0:T(2,128)S(1)} %get-tuple-element.42.at_ref, ...), custom_call_target="tpu_custom_call" | custom-call | tf_op jit(solution)/shard_map/final_state/pallas_call | solution.py:641
  56.6 0.0 copy-start
  56.6 0.0 collective-permute-start.6
  56.6 8.5 %collective-permute-done.6.ghost_ref = f32[12,128]{1,0:T(8,128)S(1)} collective-permute-done((f32[12,128]{1,0:T(8,128)S(1)}, f32[12,128]{1,0:T(8,128)S(1)}, u32[]{:S(2)}, u32[]{:S(2)}) %collective-permute-start.6) | collective-permute-done | bytes 6176 | tf_op jit(solution)/shard_map/ppermute | solution.py:648
  65.1 0.0 copy-done
  65.1 0.8 %add_returned.1 = f32[3,1024]{1,0:T(4,128)} custom-call(f32[24,128]{1,0:T(8,128)S(1)} %get-tuple-element.50.own_ref, f32[12,128]{1,0:T(8,128)S(1)} %collective-permute-done.6.ghost_ref, s32[4,128]{1,0:T(4,128)S(1)} %bitcast.15), custom_call_target="tpu_custom_call" | custom-call | tf_op jit(solution)/shard_map/add_returned/pallas_call | solution.py:649
Async XLA Ops:
  2.8 23.1 %collective-permute-start.3 = (f32[2,3,32,256]{3,2,1,0:T(8,128)S(1)}, f32[2,3,32,256]{3,2,1,0:T(8,128)S(1)}, u32[]{:S(2)}, u32[]{:S(2)}) collective-permute-start(f32[2,3,32,256]{3,2,1,0:T(8,128)S(1)} %get-tuple-element.32.low_ref), channel_id=1, source_target_pairs={{0,120},{8,0},{16,8},{24,16},{32,24},{40,32},{48,40},{56,48},{64,5... | collective-permute-start | bytes 589832 | tf_op jit(solution)/shard_map/ppermute | solution.py:579
  8.1 17.8 %collective-permute-start.2 = (f32[2,3,32,256]{3,2,1,0:T(8,128)S(1)}, f32[2,3,32,256]{3,2,1,0:T(8,128)S(1)}, u32[]{:S(2)}, u32[]{:S(2)}) collective-permute-start(f32[2,3,32,256]{3,2,1,0:T(8,128)S(1)} %get-tuple-element.33.high_ref), channel_id=1, source_target_pairs={{0,8},{8,16},{16,24},{24,32},{32,40},{40,48},{48,56},{56,64},{64,7... | collective-permute-start | bytes 589832 | tf_op jit(solution)/shard_map/ppermute | solution.py:578
  8.1 4.7 %collective-permute-start = (f32[24,256]{1,0:T(8,128)S(1)}, f32[24,256]{1,0:T(8,128)S(1)}, u32[]{:S(2)}, u32[]{:S(2)}) collective-permute-start(f32[24,256]{1,0:T(8,128)S(1)} %get-tuple-element.34), channel_id=1, source_target_pairs={{0,1},{1,2},{2,3},{3,4},{4,5},{5,6},{6,7},{7,0},{8,9},{9,10},{10,1... | collective-permute-start | bytes 73736 | tf_op jit(solution)/shard_map/ppermute | solution.py:566
  8.1 4.8 %collective-permute-start.1 = (f32[32,256]{1,0:T(8,128)S(1)}, f32[32,256]{1,0:T(8,128)S(1)}, u32[]{:S(2)}, u32[]{:S(2)}) collective-permute-start(f32[32,256]{1,0:T(8,128)S(1)} %get-tuple-element.35), channel_id=1, source_target_pairs={{0,7},{1,0},{2,1},{3,2},{4,3},{5,4},{6,5},{7,6},{8,15},{9,8},{10,9... | collective-permute-start | bytes 98312 | tf_op jit(solution)/shard_map/ppermute | solution.py:567
  13.5 12.4 %collective-permute-start.5 = (f32[5,8,256]{2,1,0:T(8,128)S(1)}, f32[5,8,256]{2,1,0:T(8,128)S(1)}, u32[]{:S(2)}, u32[]{:S(2)}) collective-permute-start(f32[5,8,256]{2,1,0:T(8,128)S(1)} %get-tuple-element.36.low_tail_ref), channel_id=1, source_target_pairs={{0,120},{8,0},{16,8},{24,16},{32,24},{40,32},{48,40},{56,48},{64,5... | collective-permute-start | bytes 122888 | tf_op jit(solution)/shard_map/ppermute | solution.py:585
  18.7 7.2 %collective-permute-start.4 = (f32[4,8,256]{2,1,0:T(8,128)S(1)}, f32[4,8,256]{2,1,0:T(8,128)S(1)}, u32[]{:S(2)}, u32[]{:S(2)}) collective-permute-start(f32[4,8,256]{2,1,0:T(8,128)S(1)} %get-tuple-element.37.high_tail_ref), channel_id=1, source_target_pairs={{0,8},{8,16},{16,24},{24,32},{32,40},{40,48},{48,56},{56,64},{64,7... | collective-permute-start | bytes 98312 | tf_op jit(solution)/shard_map/ppermute | solution.py:584
  35.1 18.5 %all-to-all-start = ((f32[128,8,128]{2,1,0:T(8,128)}), f32[128,8,128]{2,1,0:T(8,128)S(1)}, u32[]{:S(2)}, u32[]{:S(2)}) async-start(f32[128,8,128]{2,1,0:T(8,128)} %get-tuple-element.41), calls=%async_computation | async-start | bytes 1048576 | tf_op jit(solution)/shard_map/all_to_all | solution.py:639
  56.6 8.5 %copy-start = (s32[512]{0:T(512)S(1)}, s32[512]{0:T(512)}, u32[]{:S(2)}) copy-start(s32[512]{0:T(512)} %param.26) | copy-start | bytes 6148
  56.6 8.5 %collective-permute-start.6 = (f32[12,128]{1,0:T(8,128)S(1)}, f32[12,128]{1,0:T(8,128)S(1)}, u32[]{:S(2)}, u32[]{:S(2)}) collective-permute-start(f32[12,128]{1,0:T(8,128)S(1)} %get-tuple-element.51), channel_id=1, source_target_pairs={{0,1},{1,2},{2,3},{3,4},{4,5},{5,6},{6,7},{7,8},{8,9},{9,10},{10,1... | collective-permute-start | bytes 18440 | tf_op jit(solution)/shard_map/ppermute | solution.py:648

commit v5 on v4

--- a/solution.py
+++ b/solution.py
@@ -232,16 +232,14 @@
             zone = source[1, plane, row : row + 8, :]
             fields(x, row, source[0, plane, row : row + 8, :], zone if inside is None else zone * inside)
 
-    @pl.loop(0, WIDE)
-    def _(x):
+    for x in range(WIDE):
         body_rows(x, before_ref, x, behind)
         body_rows(WIDE + x, low_ref, x)
         body_rows(WIDE + planes + x, after_ref, x, ahead)
 
     body_rows(2 * WIDE, high_ref, WIDE - 1)
 
-    @pl.loop(0, 2)
-    def _(x):
+    for x in range(2):
         fields(1 + x, rows, before_tail_ref[x], before_tail_ref[2 + x] * behind)
         fields(3 + x, rows, low_tail_ref[x], low_tail_ref[2 + x])
         fields(5 + x, rows, high_tail_ref[x], high_tail_ref[2 + x])
@@ -272,8 +270,7 @@
 
     for sweep in range(SWEEPS):
 
-        @pl.loop(sweep, total - sweep)
-        def _(x):
+        for x in range(sweep, total - sweep):
             retention(x)
 
         def update(x, came):
@@ -286,7 +283,9 @@
             h[x] = here + cap_f[x] * inflow
             return goes
 
-        lax.fori_loop(sweep + 1, total - sweep - 1, update, face(sweep))
+        came = face(sweep)
+        for x in range(sweep + 1, total - sweep - 1):
+            came = update(x, came)
 
     for x in range(planes):
         _, _, log_plus = base(WIDE + x)
@@ -299,13 +298,11 @@
     order_ref[...] = deep[0:8, :]
     half = out_ref.shape[0] // 2
 
-    @pl.loop(0, bands)
-    def _(b):
-        upper = deep[pl.ds(pl.multiple_of(b * BAND, 8), 8), :]
-        lower = deep[pl.ds(pl.multiple_of(b * BAND + 8, 8), 8), :]
-        for group in range(half // bands):
-            d = group * bands + b
-            columns = jnp.broadcast_to(index[pl.ds(d, 1), :], (8, 128))
+    for b in range(bands):
+        upper = deep[b * BAND : b * BAND + 8, :]
+        lower = deep[b * BAND + 8 : b * BAND + 16, :]
+        for d in range(b, half, bands):
+            columns = jnp.broadcast_to(index[d : d + 1, :], (8, 128))
             first, second = take_lanes(upper, columns), pltpu.roll(take_lanes(lower, columns), 64, 1)
             out_ref[d] = jnp.where(lane8 < 64, first, second)
             out_ref[half + d] = jnp.where(lane8 < 64, second, first)

time: 66.1 us -> 61.1 us (0.924)
  Pallas kernels: 19.1 us -> 14.1 us
    pallas_call x1, Pallas kernels: 9.18 us -> 4.19 us  [per_device(): call(functools.partial(seepage, crest), [SM] + [VM] * 10, [pressure_head....]
  transfers between devices with their start and end apart: 8 -> 8, of which waited for: 5 -> 5; matrix products, arithmetic and copies ran while one was open for 0% -> 0% of each run, Pallas kernels for 6% -> 7%
where the time goes in v5:
time: 61.1 us; the launch traced here: 60.9 us
  waiting for transfers between devices  27.5 us (45%)
  starting transfers between devices  18.5 us (30%)
  Pallas kernels  14.1 us (23%)
  between operations  0.69 us (1%)
    all_to_all x1, waiting for transfers between devices, per_device(): lax.all_to_all(outgoing, AXES, split_axis=0, concat_axis=0, tiled=True)  10.2 us
    ppermute x1, waiting for transfers between devices, per_device(): returned = lax.ppermute(ghost, AXES, steps(devices, 1))  8.5 us
    ppermute x1, waiting for transfers between devices, per_device(): west_tail = lax.ppermute(high_tail, 'crest', steps(crest, 1))  7.23 us
    ppermute x1, starting transfers between devices, per_device(): east = lax.ppermute(low, 'crest', steps(crest, -1))  5.36 us
    ppermute x1, starting transfers between devices, per_device(): east_tail = lax.ppermute(low_tail, 'crest', steps(crest, -1))  5.17 us
    all_to_all x1, starting transfers between devices, per_device(): lax.all_to_all(outgoing, AXES, split_axis=0, concat_axis=0, tiled=True)  4.76 us
    pallas_call x1, Pallas kernels, per_device(): call(functools.partial(seepage, crest), [SM] + [VM] * 10, [pressure_head....  4.19 us
    ppermute x1, starting transfers between devices, per_device(): after = lax.ppermute(backward, 'section', steps(section, -1))  3.2 us
  transfers between devices with their start and end apart: 8, of which 5 were waited for; matrix products, arithmetic and copies ran while one was open for 0% of the time, Pallas kernels for 7%

profile of v5, /device:TPU:0, one launch (start us, length us, event | category | flops | bytes accessed | tf_op | source)
XLA Modules:
  0.0 60.9 jit_solution(4883974454750615965)
XLA Ops:
  0.6 1.1 %pack_section.1 = (f32[24,256]{1,0:T(8,128)S(1)}, f32[32,256]{1,0:T(8,128)S(1)}, f32[4,32,256]{2,1,0:T(8,128)S(1)}, s32[4,32,256]{2,1,0:T(8,128)S(1)}) custom-call(f32[4,32,256]{2,1,0:T(8,128)} %head_hbm.1, s32[4,32,256]{2,1,0:T(8,128)} %zone_hbm.1, f32[3,1024]{1,0:T(4,128)} %disp_hbm.3, s32[4,128]{1,0:T(4,128)} %bitcast.14), custom_call_target="tpu_custom_call" | custom-call | tf_op jit(solution)/shard_map/pack_section/pallas_call | solution.py:555
  1.8 1.0 %pack_crest.1 = (f32[2,3,32,256]{3,2,1,0:T(8,128)S(1)}, f32[2,3,32,256]{3,2,1,0:T(8,128)S(1)}, f32[32,256]{1,0:T(8,128)S(1)}, s32[128,128]{1,0:T(8,128)S(1)}) custom-call(f32[4,32,256]{2,1,0:T(8,128)S(1)} %get-tuple-element.28.head_ref, s32[4,32,256]{2,1,0:T(8,128)S(1)} %get-tuple-element.29.zone_ref, s32[64,128]{1,0:T(8,128)} %bitcast.17, f32[8]{0:T(128)} %alpha_hbm.1, ...), custom_call_target="tpu_custom_call" | custom-call | tf_op jit(solution)/shard_map/pack_crest/pallas_call | solution.py:567
  2.8 5.4 %collective-permute-start.3 = (f32[2,3,32,256]{3,2,1,0:T(8,128)S(1)}, f32[2,3,32,256]{3,2,1,0:T(8,128)S(1)}, u32[]{:S(2)}, u32[]{:S(2)}) collective-permute-start(f32[2,3,32,256]{3,2,1,0:T(8,128)S(1)} %get-tuple-element.32.low_ref), channel_id=1, source_target_pairs={{0,120},{8,0},{16,8},{24,16},{32,24},{40,32},{48,40},{56,48},{64,5... | collective-permute-start | bytes 589832 | tf_op jit(solution)/shard_map/ppermute | solution.py:576
  8.1 0.0 collective-permute-start.2
  8.1 0.0 collective-permute-start
  8.1 3.2 %collective-permute-start.1 = (f32[32,256]{1,0:T(8,128)S(1)}, f32[32,256]{1,0:T(8,128)S(1)}, u32[]{:S(2)}, u32[]{:S(2)}) collective-permute-start(f32[32,256]{1,0:T(8,128)S(1)} %get-tuple-element.35), channel_id=1, source_target_pairs={{0,7},{1,0},{2,1},{3,2},{4,3},{5,4},{6,5},{7,6},{8,15},{9,8},{10,9... | collective-permute-start | bytes 98312 | tf_op jit(solution)/shard_map/ppermute | solution.py:564
  11.3 0.1 pad_add_fusion.place_ref
  11.4 1.4 %collective-permute-done.before_ref = f32[24,256]{1,0:T(8,128)S(1)} collective-permute-done((f32[24,256]{1,0:T(8,128)S(1)}, f32[24,256]{1,0:T(8,128)S(1)}, u32[]{:S(2)}, u32[]{:S(2)}) %collective-permute-start) | collective-permute-done | bytes 24608 | tf_op jit(solution)/shard_map/ppermute | solution.py:563
  12.8 0.1 collective-permute-done.1.after_ref
  12.9 0.6 pack_corners.1
  13.5 5.2 %collective-permute-start.5 = (f32[5,8,256]{2,1,0:T(8,128)S(1)}, f32[5,8,256]{2,1,0:T(8,128)S(1)}, u32[]{:S(2)}, u32[]{:S(2)}) collective-permute-start(f32[5,8,256]{2,1,0:T(8,128)S(1)} %get-tuple-element.36.low_tail_ref), channel_id=1, source_target_pairs={{0,120},{8,0},{16,8},{24,16},{32,24},{40,32},{48,40},{56,48},{64,5... | collective-permute-start | bytes 122888 | tf_op jit(solution)/shard_map/ppermute | solution.py:582
  18.7 0.0 collective-permute-start.4
  18.7 7.2 %collective-permute-done.4.before_tail_ref = f32[4,8,256]{2,1,0:T(8,128)S(1)} collective-permute-done((f32[4,8,256]{2,1,0:T(8,128)S(1)}, f32[4,8,256]{2,1,0:T(8,128)S(1)}, u32[]{:S(2)}, u32[]{:S(2)}) %collective-permute-start.4) | collective-permute-done | bytes 32800 | tf_op jit(solution)/shard_map/ppermute | solution.py:581
  25.9 0.0 collective-permute-done.5.after_tail_ref.tail_ref
  25.9 0.0 collective-permute-done.3.after_ref
  25.9 0.0 collective-permute-done.2.before_ref
  25.9 4.2 %seepage.1 = (f32[4,32,256]{2,1,0:T(8,128)}, f32[128,8,128]{2,1,0:T(8,128)}, f32[8,128]{1,0:T(8,128)S(1)}) custom-call(s32[3]{0:T(128)S(1)} %pad_add_fusion.place_ref, f32[32,256]{1,0:T(8,128)S(1)} %get-tuple-element.30.tables_ref, s32[128,128]{1,0:T(8,128)S(1)} %get-tuple-element.31.index, f32[2,3,32,256]{3,2,1,0:T(8,128)S(1)} %get-tuple-element.32.low_ref, ...), custom_call_target="tpu_custom_call" | custom-call | tf_op jit(solution)/shard_map/seepage/pallas_call | solution.py:586
  30.1 4.8 %all-to-all-start = ((f32[128,8,128]{2,1,0:T(8,128)}), f32[128,8,128]{2,1,0:T(8,128)S(1)}, u32[]{:S(2)}, u32[]{:S(2)}) async-start(f32[128,8,128]{2,1,0:T(8,128)} %get-tuple-element.41), calls=%async_computation | async-start | bytes 1048576 | tf_op jit(solution)/shard_map/all_to_all | solution.py:636
  34.9 1.8 %selectors.1 = (f32[3,1024]{1,0:T(4,128)S(1)}, f32[6,8,1024]{2,1,0:T(8,128)S(1)}, s32[8,1024]{1,0:T(8,128)S(1)}, f32[48,24]{1,0:T(8,128)S(1)}, f32[24,48]{1,0:T(...) custom-call(s32[3]{0:T(128)S(1)} %pad_add_fusion.place_ref, f32[8,128]{1,0:T(8,128)S(1)} %get-tuple-element.39.order_ref, ...), custom_call_target="tpu_custom_call" | custom-call | tf_op jit(solution)/shard_map/selectors/pallas_call | solution.py:595
  36.7 1.8 %trial_state.1.trial_ref = f32[8,8,1024]{2,1,0:T(8,128)S(1)} custom-call(s32[3]{0:T(128)S(1)} %pad_add_fusion.place_ref, f32[48,24]{1,0:T(8,128)S(1)} %get-tuple-element.44.matrix_ref, f32[3,1024]{1,0:T(4,128)S(1)} %get-tuple-element.45.disp_ref, f32[32,256]{1,0:T(8,128)S(1)} %collective-permute-done.1.after_ref, ...), custom_call_target="tpu_custom_call" | custom-call | tf_op jit(solution)/shard_map/trial_state/pallas_call | solution.py:629
  38.4 10.2 %all-to-all-done = f32[128,8,128]{2,1,0:T(8,128)S(1)} async-done(((f32[128,8,128]{2,1,0:T(8,128)}), f32[128,8,128]{2,1,0:T(8,128)S(1)}, u32[]{:S(2)}, u32[]{:S(2)}) %all-to-all-start) | async-done | bytes 524320 | tf_op jit(solution)/shard_map/all_to_all | solution.py:636
  48.6 2.9 %final_state.1 = (f32[6,8,1024]{2,1,0:T(8,128)}, f32[8,1024]{1,0:T(8,128)}, f32[24,128]{1,0:T(8,128)S(1)}, f32[12,128]{1,0:T(8,128)S(1)}) custom-call(f32[24,48]{1,0:T(8,128)S(1)} %get-tuple-element.40.matrix_ref, f32[1024,128]{1,0:T(8,128)S(1)} %bitcast.13, s32[2,1024]{1,0:T(2,128)S(1)} %get-tuple-element.42.at_ref, ...), custom_call_target="tpu_custom_call" | custom-call | tf_op jit(solution)/shard_map/final_state/pallas_call | solution.py:638
  51.6 0.0 copy-start
  51.6 0.0 collective-permute-start.6
  51.6 8.5 %collective-permute-done.6.ghost_ref = f32[12,128]{1,0:T(8,128)S(1)} collective-permute-done((f32[12,128]{1,0:T(8,128)S(1)}, f32[12,128]{1,0:T(8,128)S(1)}, u32[]{:S(2)}, u32[]{:S(2)}) %collective-permute-start.6) | collective-permute-done | bytes 6176 | tf_op jit(solution)/shard_map/ppermute | solution.py:645
  60.1 0.0 copy-done
  60.1 0.8 %add_returned.1 = f32[3,1024]{1,0:T(4,128)} custom-call(f32[24,128]{1,0:T(8,128)S(1)} %get-tuple-element.50.own_ref, f32[12,128]{1,0:T(8,128)S(1)} %collective-permute-done.6.ghost_ref, s32[4,128]{1,0:T(4,128)S(1)} %bitcast.15), custom_call_target="tpu_custom_call" | custom-call | tf_op jit(solution)/shard_map/add_returned/pallas_call | solution.py:646
Async XLA Ops:
  2.8 23.1 %collective-permute-start.3 = (f32[2,3,32,256]{3,2,1,0:T(8,128)S(1)}, f32[2,3,32,256]{3,2,1,0:T(8,128)S(1)}, u32[]{:S(2)}, u32[]{:S(2)}) collective-permute-start(f32[2,3,32,256]{3,2,1,0:T(8,128)S(1)} %get-tuple-element.32.low_ref), channel_id=1, source_target_pairs={{0,120},{8,0},{16,8},{24,16},{32,24},{40,32},{48,40},{56,48},{64,5... | collective-permute-start | bytes 589832 | tf_op jit(solution)/shard_map/ppermute | solution.py:576
  8.1 17.8 %collective-permute-start.2 = (f32[2,3,32,256]{3,2,1,0:T(8,128)S(1)}, f32[2,3,32,256]{3,2,1,0:T(8,128)S(1)}, u32[]{:S(2)}, u32[]{:S(2)}) collective-permute-start(f32[2,3,32,256]{3,2,1,0:T(8,128)S(1)} %get-tuple-element.33.high_ref), channel_id=1, source_target_pairs={{0,8},{8,16},{16,24},{24,32},{32,40},{40,48},{48,56},{56,64},{64,7... | collective-permute-start | bytes 589832 | tf_op jit(solution)/shard_map/ppermute | solution.py:575
  8.1 4.7 %collective-permute-start = (f32[24,256]{1,0:T(8,128)S(1)}, f32[24,256]{1,0:T(8,128)S(1)}, u32[]{:S(2)}, u32[]{:S(2)}) collective-permute-start(f32[24,256]{1,0:T(8,128)S(1)} %get-tuple-element.34), channel_id=1, source_target_pairs={{0,1},{1,2},{2,3},{3,4},{4,5},{5,6},{6,7},{7,0},{8,9},{9,10},{10,1... | collective-permute-start | bytes 73736 | tf_op jit(solution)/shard_map/ppermute | solution.py:563
  8.1 4.8 %collective-permute-start.1 = (f32[32,256]{1,0:T(8,128)S(1)}, f32[32,256]{1,0:T(8,128)S(1)}, u32[]{:S(2)}, u32[]{:S(2)}) collective-permute-start(f32[32,256]{1,0:T(8,128)S(1)} %get-tuple-element.35), channel_id=1, source_target_pairs={{0,7},{1,0},{2,1},{3,2},{4,3},{5,4},{6,5},{7,6},{8,15},{9,8},{10,9... | collective-permute-start | bytes 98312 | tf_op jit(solution)/shard_map/ppermute | solution.py:564
  13.5 12.4 %collective-permute-start.5 = (f32[5,8,256]{2,1,0:T(8,128)S(1)}, f32[5,8,256]{2,1,0:T(8,128)S(1)}, u32[]{:S(2)}, u32[]{:S(2)}) collective-permute-start(f32[5,8,256]{2,1,0:T(8,128)S(1)} %get-tuple-element.36.low_tail_ref), channel_id=1, source_target_pairs={{0,120},{8,0},{16,8},{24,16},{32,24},{40,32},{48,40},{56,48},{64,5... | collective-permute-start | bytes 122888 | tf_op jit(solution)/shard_map/ppermute | solution.py:582
  18.7 7.2 %collective-permute-start.4 = (f32[4,8,256]{2,1,0:T(8,128)S(1)}, f32[4,8,256]{2,1,0:T(8,128)S(1)}, u32[]{:S(2)}, u32[]{:S(2)}) collective-permute-start(f32[4,8,256]{2,1,0:T(8,128)S(1)} %get-tuple-element.37.high_tail_ref), channel_id=1, source_target_pairs={{0,8},{8,16},{16,24},{24,32},{32,40},{40,48},{48,56},{56,64},{64,7... | collective-permute-start | bytes 98312 | tf_op jit(solution)/shard_map/ppermute | solution.py:581
  30.1 18.5 %all-to-all-start = ((f32[128,8,128]{2,1,0:T(8,128)}), f32[128,8,128]{2,1,0:T(8,128)S(1)}, u32[]{:S(2)}, u32[]{:S(2)}) async-start(f32[128,8,128]{2,1,0:T(8,128)} %get-tuple-element.41), calls=%async_computation | async-start | bytes 1048576 | tf_op jit(solution)/shard_map/all_to_all | solution.py:636
  51.6 8.5 %copy-start = (s32[512]{0:T(512)S(1)}, s32[512]{0:T(512)}, u32[]{:S(2)}) copy-start(s32[512]{0:T(512)} %param.26) | copy-start | bytes 6148
  51.6 8.5 %collective-permute-start.6 = (f32[12,128]{1,0:T(8,128)S(1)}, f32[12,128]{1,0:T(8,128)S(1)}, u32[]{:S(2)}, u32[]{:S(2)}) collective-permute-start(f32[12,128]{1,0:T(8,128)S(1)} %get-tuple-element.51), channel_id=1, source_target_pairs={{0,1},{1,2},{2,3},{3,4},{4,5},{5,6},{6,7},{7,8},{8,9},{9,10},{10,1... | collective-permute-start | bytes 18440 | tf_op jit(solution)/shard_map/ppermute | solution.py:645

commit v6 on v5

--- a/solution.py
+++ b/solution.py
@@ -104,37 +104,96 @@
     backward_ref[30:32, :] = jnp.zeros((2, 256), jnp.float32)
 
 
-def pack_crest(
-    head_ref,
-    zone_ref,
+def pack_crest(sections, place_ref, head_ref, zone_ref, before_ref, after_ref, low_ref, high_ref):
+    planes, rows = head_ref.shape[0], head_ref.shape[1]
+    groups = rows // 8
+    behind = jnp.where(place_ref[0] > 0, 1.0, 0.0)
+    ahead = jnp.where(place_ref[0] < sections - 1, 1.0, 0.0)
+    for field in range(2):
+        first = field * (WIDE * groups + 2)
+        for x in range(planes):
+            for group in range(groups):
+                at = slice(8 * group, 8 * group + 8)
+                own = head_ref[x, at, :] if field == 0 else zone_ref[x, at, :].astype(jnp.float32) + 1.0
+                if x < WIDE:
+                    low_ref[first + x * groups + group] = own
+                if x >= planes - WIDE:
+                    high_ref[first + (x - planes + WIDE) * groups + group] = own
+            at = field * WIDE * planes + WIDE * x
+            tail = jnp.concatenate(
+                [
+                    after_ref[at : at + WIDE, :] * ahead,
+                    jnp.zeros((2, after_ref.shape[1]), jnp.float32),
+                    before_ref[at : at + WIDE, :] * behind,
+                ],
+                axis=0,
+            )
+            if x < 2:
+                low_ref[first + WIDE * groups + x] = tail
+            else:
+                high_ref[first + WIDE * groups + x - 2] = tail
+    low_ref[2 * (WIDE * groups + 2)] = after_ref[24:32, :]
+
+
+def choose(values, bits):
+    for bit in bits:
+        values = [jnp.where(bit, values[i + 1], values[i]) for i in range(0, len(values), 2)]
+    return values[0]
+
+
+def fields(tables_ref, out, x, row, head, zone):
+    zones = tables_ref.shape[0] // 4
+    tables = [
+        [jnp.broadcast_to(tables_ref[f * zones + z : f * zones + z + 1, :], head.shape) for z in range(zones)]
+        for f in range(4)
+    ]
+    zone = zone.astype(jnp.int32) - 1
+    bits = [(zone & (1 << bit)) != 0 for bit in range(3)]
+    alpha, less, m, root = (choose(table, bits) for table in tables)
+    values = (head, alpha, less, m, jnp.where(zone >= 0, root, 0.0), THETA_GAP * alpha * less)
+    for ref, value in zip(out, values):
+        ref[x, row : row + 8, :] = value
+
+
+def base(alpha, less, h):
+    scaled = alpha * jnp.maximum(-h, 0.0)
+    power = jnp.exp(less * jnp.log(jnp.maximum(scaled, 1e-30)))
+    plus = 1.0 + power * scaled
+    return power, plus, jnp.log(plus)
+
+
+def retention(h, alpha, less, m, root, gain):
+    power, plus, log_plus = base(alpha, less, h)
+    fourth = jnp.exp(m * log_plus)
+    square = fourth * fourth
+    part = power * (square * square)
+    return root * fourth * (1.0 - part), TIME_STEP * plus / (STORAGE * plus + gain * part)
+
+
+def prepare(
+    low_ref,
+    high_ref,
     wanted_hbm,
     alpha_hbm,
     expo_hbm,
     ks_hbm,
-    low_ref,
-    high_ref,
     tables_ref,
     index_ref,
+    h,
+    alpha_f,
+    less_f,
+    m_f,
+    root_f,
+    gain_f,
+    r_f,
+    cap_f,
     wanted_ref,
     alpha_ref,
     expo_ref,
     ks_ref,
     sems,
 ):
-    pairs = [(wanted_hbm, wanted_ref), (alpha_hbm, alpha_ref), (expo_hbm, expo_ref), (ks_hbm, ks_ref)]
-    copies = [pltpu.make_async_copy(source, target, sems.at[i]) for i, (source, target) in enumerate(pairs)]
-    for copy in copies:
-        copy.start()
-    planes = head_ref.shape[0]
-    for x in range(planes):
-        own = [head_ref[x], zone_ref[x].astype(jnp.float32) + 1.0]
-        for field in range(2):
-            if x < WIDE:
-                low_ref[field, x] = own[field]
-            if x >= planes - WIDE:
-                high_ref[field, x - planes + WIDE] = own[field]
-    for copy in copies:
-        copy.wait()
+    fetch([(wanted_hbm, wanted_ref), (alpha_hbm, alpha_ref), (expo_hbm, expo_ref), (ks_hbm, ks_ref)], sems)
     zones, width = alpha_ref.shape[0], tables_ref.shape[1]
     for z in range(zones):
         expo = jnp.full((1, width), expo_ref[z], jnp.float32)
@@ -145,28 +204,17 @@
         tables_ref[3 * zones + z : 3 * zones + z + 1, :] = jnp.sqrt(jnp.full((1, width), ks_ref[z], jnp.float32))
     wanted = wanted_ref[...]
     index_ref[...] = jnp.concatenate([wanted, pltpu.roll(wanted, wanted.shape[1] // 2, 1)], axis=0).T
-
-
-def pack_corners(sections, place_ref, before_ref, after_ref, low_ref, high_ref):
-    planes = high_ref.shape[0]
-    behind = jnp.where(place_ref[0] > 0, 1.0, 0.0)
-    ahead = jnp.where(place_ref[0] < sections - 1, 1.0, 0.0)
+    planes, groups = h.shape[0], h.shape[1] // 8 - 1
+    out = (h, alpha_f, less_f, m_f, root_f, gain_f)
     for x in range(planes):
-        for field in range(2):
-            at = field * WIDE * planes + WIDE * x
-            tail = jnp.concatenate(
-                [
-                    after_ref[at : at + WIDE, :] * ahead,
-                    jnp.zeros((2, after_ref.shape[1]), jnp.float32),
-                    before_ref[at : at + WIDE, :] * behind,
-                ],
-                axis=0,
-            )
-            if x < 2:
-                low_ref[2 * field + x] = tail
-            else:
-                high_ref[2 * field + x - 2] = tail
-    low_ref[4] = after_ref[24:32, :]
+        source, plane, tail = (low_ref, x, x) if x < 2 else (high_ref, x - planes + WIDE, x - 2)
+        zone_at = WIDE * groups + 2
+        for group in range(groups):
+            at = plane * groups + group
+            fields(tables_ref, out, x, 8 * group, source[at], source[zone_at + at])
+        at = WIDE * groups + tail
+        fields(tables_ref, out, x, 8 * groups, source[at], source[zone_at + at])
+        r_f[x], cap_f[x] = retention(*(ref[x] for ref in out))
 
 
 def seepage(
@@ -174,14 +222,16 @@
     place_ref,
     tables_ref,
     index,
-    low_ref,
-    high_ref,
-    low_tail_ref,
-    high_tail_ref,
+    own_h,
+    own_alpha,
+    own_less,
+    own_m,
+    own_root,
+    own_gain,
+    own_r,
+    own_cap,
     before_ref,
     after_ref,
-    before_tail_ref,
-    after_tail_ref,
     head_ref,
     out_ref,
     order_ref,
@@ -200,102 +250,69 @@
     rows = head_ref.shape[1]
     total = planes + 2 * WIDE
     height, depth = h.shape[1], h.shape[2]
+    groups = rows // 8
+    zone_at = WIDE * groups + 2
     lane8 = lax.broadcasted_iota(jnp.int32, (8, 128), 1)
-    zones = tables_ref.shape[0] // 4
-    alpha_t, less_t, m_t, root_t = (
-        [jnp.broadcast_to(tables_ref[f * zones + z : f * zones + z + 1, :], (8, depth)) for z in range(zones)]
-        for f in range(4)
-    )
     behind = jnp.where(place_ref[1] > 0, 1.0, 0.0)
     ahead = jnp.where(place_ref[1] < crests - 1, 1.0, 0.0)
-
-    def fields(x, row, head, zone):
-        at = slice(row, row + 8)
-        h[x, at, :] = head
-        zone = zone.astype(jnp.int32) - 1
-        bits = [(zone & (1 << bit)) != 0 for bit in range(3)]
-
-        def choose(values):
-            for bit in bits:
-                values = [jnp.where(bit, values[i + 1], values[i]) for i in range(0, len(values), 2)]
-            return values[0]
-
-        alpha, less = choose(alpha_t), choose(less_t)
-        alpha_f[x, at, :] = alpha
-        less_f[x, at, :] = less
-        m_f[x, at, :] = choose(m_t)
-        root_f[x, at, :] = jnp.where(zone >= 0, choose(root_t), 0.0)
-        gain_f[x, at, :] = THETA_GAP * alpha * less
-
-    def body_rows(x, source, plane, inside=None):
-        for row in range(0, rows, 8):
-            zone = source[1, plane, row : row + 8, :]
-            fields(x, row, source[0, plane, row : row + 8, :], zone if inside is None else zone * inside)
-
-    for x in range(WIDE):
-        body_rows(x, before_ref, x, behind)
-        body_rows(WIDE + x, low_ref, x)
-        body_rows(WIDE + planes + x, after_ref, x, ahead)
-
-    body_rows(2 * WIDE, high_ref, WIDE - 1)
-
-    for x in range(2):
-        fields(1 + x, rows, before_tail_ref[x], before_tail_ref[2 + x] * behind)
-        fields(3 + x, rows, low_tail_ref[x], low_tail_ref[2 + x])
-        fields(5 + x, rows, high_tail_ref[x], high_tail_ref[2 + x])
-        fields(7 + x, rows, after_tail_ref[x], after_tail_ref[2 + x] * ahead)
-
+    out = (h, alpha_f, less_f, m_f, root_f, gain_f)
+
+    for source, first, tail, inside in ((before_ref, 0, 1, behind), (after_ref, WIDE + planes, 0, ahead)):
+        for plane in range(WIDE):
+            for group in range(groups):
+                at = plane * groups + group
+                fields(tables_ref, out, first + plane, 8 * group, source[at], source[zone_at + at] * inside)
+        for plane in range(2):
+            at = WIDE * groups + plane
+            fields(tables_ref, out, first + tail + plane, rows, source[at], source[zone_at + at] * inside)
     for x in (0, total - 1):
-        for field in (h, alpha_f, less_f, m_f, root_f, gain_f):
-            field[x, rows:height, :] = jnp.zeros((height - rows, depth), jnp.float32)
-
-    def base(x):
-        scaled = alpha_f[x] * jnp.maximum(-h[x], 0.0)
-        power = jnp.exp(less_f[x] * jnp.log(jnp.maximum(scaled, 1e-30)))
-        plus = 1.0 + power * scaled
-        return power, plus, jnp.log(plus)
-
-    def retention(x):
-        power, plus, log_plus = base(x)
-        fourth = jnp.exp(m_f[x] * log_plus)
-        square = fourth * fourth
-        part = power * (square * square)
-        r_f[x] = root_f[x] * fourth * (1.0 - part)
-        cap_f[x] = TIME_STEP * plus / (STORAGE * plus + gain_f[x] * part)
+        for ref in out:
+            ref[x, rows:height, :] = jnp.zeros((height - rows, depth), jnp.float32)
+    for x in range(planes):
+        h[WIDE + x] = own_h[x]
+
+    own = dict(zip(map(id, (alpha_f, less_f, m_f, root_f, gain_f)), (own_alpha, own_less, own_m, own_root, own_gain)))
+
+    def param(ref, x):
+        return own[id(ref)][x - WIDE] if WIDE <= x < WIDE + planes else ref[x]
 
     inner_z = lax.broadcasted_iota(jnp.int32, (height, depth), 1) < depth - 1
 
-    def face(x):
-        return r_f[x] * r_f[x + 1] * (h[x + 1] - h[x])
-
     for sweep in range(SWEEPS):
-
+        held = {}
         for x in range(sweep, total - sweep):
-            retention(x)
-
-        def update(x, came):
-            here, r = h[x], r_f[x]
+            if sweep == 0 and WIDE <= x < WIDE + planes:
+                held[x] = (own_r, own_cap, x - WIDE)
+            else:
+                values = (param(ref, x) for ref in (alpha_f, less_f, m_f, root_f, gain_f))
+                r_f[x], cap_f[x] = retention(h[x], *values)
+                held[x] = (r_f, cap_f, x)
+
+        def r_of(x):
+            return held[x][0][held[x][2]]
+
+        def face(x):
+            return r_of(x) * r_of(x + 1) * (h[x + 1] - h[x])
+
+        came = face(sweep)
+        for x in range(sweep + 1, total - sweep - 1):
+            here, r = h[x], r_of(x)
             goes = face(x)
             flux_y = r * pltpu.roll(r, height - 1, 0) * (pltpu.roll(here, height - 1, 0) - here)
             flux_z = r * pltpu.roll(r, depth - 1, 1) * (pltpu.roll(here, depth - 1, 1) - here + 1.0)
             flux_z = jnp.where(inner_z, flux_z, 0.0)
             inflow = goes - came + (flux_y - pltpu.roll(flux_y, 1, 0)) + (flux_z - pltpu.roll(flux_z, 1, 1))
-            h[x] = here + cap_f[x] * inflow
-            return goes
-
-        came = face(sweep)
-        for x in range(sweep + 1, total - sweep - 1):
-            came = update(x, came)
+            h[x] = here + held[x][1][held[x][2]] * inflow
+            came = goes
 
     for x in range(planes):
-        _, _, log_plus = base(WIDE + x)
-        here = h[WIDE + x][0:rows]
-        head_ref[x] = here
-        table[x * rows : (x + 1) * rows, :] = jnp.exp(4.0 * m_f[WIDE + x] * log_plus)[0:rows] * here
+        here = h[WIDE + x]
+        _, _, log_plus = base(own_alpha[x], own_less[x], here)
+        head_ref[x] = here[0:rows]
+        table[x * rows : (x + 1) * rows, :] = (jnp.exp(4.0 * own_m[x] * log_plus) * here)[0:rows]
     deep[...] = table[...].T
+    order_ref[...] = deep[0:8, :]
     bands = depth // BAND
-
-    order_ref[...] = deep[0:8, :]
     half = out_ref.shape[0] // 2
 
     for b in range(bands):
@@ -373,7 +390,7 @@
 def trial_state(
     sections, place_ref, matrix_ref, disp_ref, after_ref, tail_ref, conn_ref, stress_ref, trial_ref, nodes, corners
 ):
-    ghost = jnp.where(place_ref[0] < sections - 1, after_ref[24:32, :], tail_ref[4])
+    ghost = jnp.where(place_ref[0] < sections - 1, after_ref[24:32, :], tail_ref[tail_ref.shape[0] - 1])
     for comp in range(3):
         for s in range(8):
             nodes[comp * 12 + s : comp * 12 + s + 1, :] = disp_ref[comp : comp + 1, s * 128 : (s + 1) * 128]
@@ -563,33 +580,35 @@
     before = lax.ppermute(forward, "section", steps(section, 1))
     after = lax.ppermute(backward, "section", steps(section, -1))
 
-    own = (2, WIDE, rows, depth)
-    low, high, tables, index = call(
-        pack_crest,
-        [VM] * 2 + [HBM] * 4,
-        [own, own, (4 * zones, depth), (devices, 128)],
-        [pltpu.VMEM((64, devices), i32)] + [pltpu.SMEM((zones,), f32)] * 3 + [pltpu.SemaphoreType.DMA((4,))],
+    groups = rows // 8
+    edge = (2 * (WIDE * groups + 2), 8, depth)
+    low, high = call(
+        functools.partial(pack_crest, section),
+        [SM] + [VM] * 4,
+        [(edge[0] + 1, 8, depth), edge],
+        [],
         "pack_crest",
-        [f32, f32, f32, i32],
-    )(head, zone, *(in_hbm(x) for x in (sent_columns[0].T, retention_alpha, retention_exponent, conductivity)))
+    )(place, head, zone, before, after)
     west = lax.ppermute(high, "crest", steps(crest, 1))
     east = lax.ppermute(low, "crest", steps(crest, -1))
 
-    low_tail, high_tail = call(
-        functools.partial(pack_corners, section), [SM] + [VM] * 2, [(5, 8, depth), (4, 8, depth)], [], "pack_corners"
-    )(place, before, after)
-    west_tail = lax.ppermute(high_tail, "crest", steps(crest, 1))
-    east_tail = lax.ppermute(low_tail, "crest", steps(crest, -1))
-
-    total = planes + 2 * WIDE
-    field = pltpu.VMEM((total, height, depth), f32)
+    tables, index, *own = call(
+        prepare,
+        [VM] * 2 + [HBM] * 4,
+        [(4 * zones, depth), (devices, 128)] + [(planes, height, depth)] * 8,
+        [pltpu.VMEM((64, devices), i32)] + [pltpu.SMEM((zones,), f32)] * 3 + [pltpu.SemaphoreType.DMA((4,))],
+        "prepare",
+        [f32, i32] + [f32] * 8,
+    )(low, high, *(in_hbm(x) for x in (sent_columns[0].T, retention_alpha, retention_exponent, conductivity)))
+
+    field = pltpu.VMEM((planes + 2 * WIDE, height, depth), f32)
     head_out, outgoing, order = call(
         functools.partial(seepage, crest),
-        [SM] + [VM] * 10,
+        [SM] + [VM] * 12,
         [pressure_head.shape, (devices, 8, 128), (8, 128)],
         [field] * 8 + [pltpu.VMEM((planes * rows, depth), f32), pltpu.VMEM((depth, planes * rows), f32)],
         "seepage",
-    )(place, tables, index, low, high, low_tail, high_tail, west, east, west_tail, east_tail)
+    )(place, tables, index, *own, west, east)
 
     matrix = component_major()
     disp, stress, conn, strain_rows, force_rows, strength, places = call(
@@ -632,7 +651,7 @@
         [(8, 8, elems)],
         [pltpu.VMEM((40, 128), f32), pltpu.VMEM((24, elems), f32)],
         "trial_state",
-    )(place, strain_rows, disp, after, east_tail, conn, stress)
+    )(place, strain_rows, disp, after, east, conn, stress)
     incoming = lax.all_to_all(outgoing, AXES, split_axis=0, concat_axis=0, tiled=True)
 
     stress_new, release, own, ghost = call(

time: 61.1 us -> 59 us (0.966)
  starting transfers between devices: 18.5 us -> 13.9 us
  waiting for transfers between devices: 27.5 us -> 29.7 us
    ppermute x1, waiting for transfers between devices: 0.01 us -> 9.44 us  [per_device(): west = lax.ppermute(high, 'crest', steps(crest, 1))]
    ppermute x2 -> x0, waiting for transfers between devices: 7.23 us -> none  [the longest x1 7.23 us: per_device(): west_tail = lax.ppermute(high_tail, 'crest', steps(crest, 1))]
    ppermute x2 -> x0, starting transfers between devices: 5.17 us -> none  [the longest x1 5.17 us: per_device(): east_tail = lax.ppermute(low_tail, 'crest', steps(crest, -1))]
  transfers between devices with their start and end apart: 8 -> 6, of which waited for: 5 -> 5; matrix products, arithmetic and copies ran while one was open for 0% -> 0% of each run, Pallas kernels for 7% -> 8%
where the time goes in v6:
time: 59 us; the launch traced here: 58.7 us
  waiting for transfers between devices  29.7 us (50%)
  Pallas kernels  14.4 us (24%)
  starting transfers between devices  13.9 us (24%)
  between operations  0.69 us (1%)
    all_to_all x1, waiting for transfers between devices, per_device(): lax.all_to_all(outgoing, AXES, split_axis=0, concat_axis=0, tiled=True)  10.2 us
    ppermute x1, waiting for transfers between devices, per_device(): west = lax.ppermute(high, 'crest', steps(crest, 1))  9.44 us
    ppermute x1, waiting for transfers between devices, per_device(): returned = lax.ppermute(ghost, AXES, steps(devices, 1))  8.5 us
    ppermute x1, starting transfers between devices, per_device(): east = lax.ppermute(low, 'crest', steps(crest, -1))  5.28 us
    all_to_all x1, starting transfers between devices, per_device(): lax.all_to_all(outgoing, AXES, split_axis=0, concat_axis=0, tiled=True)  5.01 us
    pallas_call x1, Pallas kernels, per_device(): call(functools.partial(seepage, crest), [SM] + [VM] * 12, [pressure_head....  4.06 us
    ppermute x1, starting transfers between devices, per_device(): after = lax.ppermute(backward, 'section', steps(section, -1))  3.57 us
    pallas_call x1, Pallas kernels, per_device(): call(final_state, [VM] * 6, [(6, 8, elems), (8, elems), (24, 128), (12, 1...  2.95 us
  transfers between devices with their start and end apart: 6, of which 5 were waited for; matrix products, arithmetic and copies ran while one was open for 0% of the time, Pallas kernels for 8%

profile of v6, /device:TPU:0, one launch (start us, length us, event | category | flops | bytes accessed | tf_op | source)
XLA Modules:
  0.0 58.7 jit_solution(11898201226270500475)
XLA Ops:
  0.6 1.1 %pack_section.1 = (f32[24,256]{1,0:T(8,128)S(1)}, f32[32,256]{1,0:T(8,128)S(1)}, f32[4,32,256]{2,1,0:T(8,128)S(1)}, s32[4,32,256]{2,1,0:T(8,128)S(1)}) custom-call(f32[4,32,256]{2,1,0:T(8,128)} %head_hbm.1, s32[4,32,256]{2,1,0:T(8,128)} %zone_hbm.1, f32[3,1024]{1,0:T(4,128)} %disp_hbm.3, s32[4,128]{1,0:T(4,128)} %bitcast.14), custom_call_target="tpu_custom_call" | custom-call | tf_op jit(solution)/shard_map/pack_section/pallas_call | solution.py:572
  1.8 0.0 collective-permute-start
  1.8 3.6 %collective-permute-start.1 = (f32[32,256]{1,0:T(8,128)S(1)}, f32[32,256]{1,0:T(8,128)S(1)}, u32[]{:S(2)}, u32[]{:S(2)}) collective-permute-start(f32[32,256]{1,0:T(8,128)S(1)} %get-tuple-element.37), channel_id=1, source_target_pairs={{0,7},{1,0},{2,1},{3,2},{4,3},{5,4},{6,5},{7,6},{8,15},{9,8},{10,9... | collective-permute-start | bytes 98312 | tf_op jit(solution)/shard_map/ppermute | solution.py:581
  5.4 0.1 pad_add_fusion.place_ref
  5.4 1.4 %collective-permute-done.before_ref = f32[24,256]{1,0:T(8,128)S(1)} collective-permute-done((f32[24,256]{1,0:T(8,128)S(1)}, f32[24,256]{1,0:T(8,128)S(1)}, u32[]{:S(2)}, u32[]{:S(2)}) %collective-permute-start) | collective-permute-done | bytes 24608 | tf_op jit(solution)/shard_map/ppermute | solution.py:580
  6.8 0.1 collective-permute-done.1.after_ref
  7.0 0.6 pack_crest.1
  7.5 5.3 %collective-permute-start.3 = (f32[29,8,256]{2,1,0:T(8,128)S(1)}, f32[29,8,256]{2,1,0:T(8,128)S(1)}, u32[]{:S(2)}, u32[]{:S(2)}) collective-permute-start(f32[29,8,256]{2,1,0:T(8,128)S(1)} %get-tuple-element.38.low_ref), channel_id=1, source_target_pairs={{0,120},{8,0},{16,8},{24,16},{32,24},{40,32},{48,40},{56,48},{64,5... | collective-permute-start | bytes 712712 | tf_op jit(solution)/shard_map/ppermute | solution.py:593
  12.8 0.0 collective-permute-start.2
  12.8 1.4 %prepare.1 = (f32[32,256]{1,0:T(8,128)S(1)}, s32[128,128]{1,0:T(8,128)S(1)}, f32[4,40,256]{2,1,0:T(8,128)S(1)}, f32[4,40,256]{2,1,0:T(8,128)S(1)}, f32[4,40,256]...) custom-call(f32[29,8,256]{2,1,0:T(8,128)S(1)} %get-tuple-element.38., ...), custom_call_target="tpu_custom_call" | custom-call | tf_op jit(solution)/shard_map/prepare/pallas_call | solution.py:595
  14.2 9.4 %collective-permute-done.2.before_ref = f32[28,8,256]{2,1,0:T(8,128)S(1)} collective-permute-done((f32[28,8,256]{2,1,0:T(8,128)S(1)}, f32[28,8,256]{2,1,0:T(8,128)S(1)}, u32[]{:S(2)}, u32[]{:S(2)}) %collective-permute-start.2) | collective-permute-done | bytes 229408 | tf_op jit(solution)/shard_map/ppermute | solution.py:592
  23.6 0.0 collective-permute-done.3.after_ref.tail_ref
  23.6 4.1 %seepage.1 = (f32[4,32,256]{2,1,0:T(8,128)}, f32[128,8,128]{2,1,0:T(8,128)}, f32[8,128]{1,0:T(8,128)S(1)}) custom-call(s32[3]{0:T(128)S(1)} %pad_add_fusion.place_ref, f32[32,256]{1,0:T(8,128)S(1)} %get-tuple-element.40.tables_ref, s32[128,128]{1,0:T(8,128)S(1)} %get-tuple-element.41.index, f32[4,40,256]{2,1,0:T(8,128)S(1)} %get-tuple-element.42.own_h, ...), custom_call_target="tpu_custom_call" | custom-call | tf_op jit(solution)/shard_map/seepage/pallas_call | solution.py:605
  27.7 5.0 %all-to-all-start = ((f32[128,8,128]{2,1,0:T(8,128)}), f32[128,8,128]{2,1,0:T(8,128)S(1)}, u32[]{:S(2)}, u32[]{:S(2)}) async-start(f32[128,8,128]{2,1,0:T(8,128)} %get-tuple-element.53), calls=%async_computation | async-start | bytes 1048576 | tf_op jit(solution)/shard_map/all_to_all | solution.py:655
  32.7 1.8 %selectors.1 = (f32[3,1024]{1,0:T(4,128)S(1)}, f32[6,8,1024]{2,1,0:T(8,128)S(1)}, s32[8,1024]{1,0:T(8,128)S(1)}, f32[48,24]{1,0:T(8,128)S(1)}, f32[24,48]{1,0:T(...) custom-call(s32[3]{0:T(128)S(1)} %pad_add_fusion.place_ref, f32[8,128]{1,0:T(8,128)S(1)} %get-tuple-element.51.order_ref, ...), custom_call_target="tpu_custom_call" | custom-call | tf_op jit(solution)/shard_map/selectors/pallas_call | solution.py:614
  34.5 1.8 %trial_state.1.trial_ref = f32[8,8,1024]{2,1,0:T(8,128)S(1)} custom-call(s32[3]{0:T(128)S(1)} %pad_add_fusion.place_ref, f32[48,24]{1,0:T(8,128)S(1)} %get-tuple-element.56.matrix_ref, f32[3,1024]{1,0:T(4,128)S(1)} %get-tuple-element.57.disp_ref, f32[32,256]{1,0:T(8,128)S(1)} %collective-permute-done.1.after_ref, ...), custom_call_target="tpu_custom_call" | custom-call | tf_op jit(solution)/shard_map/trial_state/pallas_call | solution.py:648
  36.3 10.2 %all-to-all-done = f32[128,8,128]{2,1,0:T(8,128)S(1)} async-done(((f32[128,8,128]{2,1,0:T(8,128)}), f32[128,8,128]{2,1,0:T(8,128)S(1)}, u32[]{:S(2)}, u32[]{:S(2)}) %all-to-all-start) | async-done | bytes 524320 | tf_op jit(solution)/shard_map/all_to_all | solution.py:655
  46.5 2.9 %final_state.1 = (f32[6,8,1024]{2,1,0:T(8,128)}, f32[8,1024]{1,0:T(8,128)}, f32[24,128]{1,0:T(8,128)S(1)}, f32[12,128]{1,0:T(8,128)S(1)}) custom-call(f32[24,48]{1,0:T(8,128)S(1)} %get-tuple-element.52.matrix_ref, f32[1024,128]{1,0:T(8,128)S(1)} %bitcast.13, s32[2,1024]{1,0:T(2,128)S(1)} %get-tuple-element.54.at_ref, ...), custom_call_target="tpu_custom_call" | custom-call | tf_op jit(solution)/shard_map/final_state/pallas_call | solution.py:657
  49.4 0.0 copy-start
  49.4 0.0 collective-permute-start.4
  49.4 8.5 %collective-permute-done.4.ghost_ref = f32[12,128]{1,0:T(8,128)S(1)} collective-permute-done((f32[12,128]{1,0:T(8,128)S(1)}, f32[12,128]{1,0:T(8,128)S(1)}, u32[]{:S(2)}, u32[]{:S(2)}) %collective-permute-start.4) | collective-permute-done | bytes 6176 | tf_op jit(solution)/shard_map/ppermute | solution.py:664
  57.9 0.0 copy-done
  57.9 0.8 %add_returned.1 = f32[3,1024]{1,0:T(4,128)} custom-call(f32[24,128]{1,0:T(8,128)S(1)} %get-tuple-element.62.own_ref, f32[12,128]{1,0:T(8,128)S(1)} %collective-permute-done.4.ghost_ref, s32[4,128]{1,0:T(4,128)S(1)} %bitcast.15), custom_call_target="tpu_custom_call" | custom-call | tf_op jit(solution)/shard_map/add_returned/pallas_call | solution.py:665
Async XLA Ops:
  1.8 5.1 %collective-permute-start = (f32[24,256]{1,0:T(8,128)S(1)}, f32[24,256]{1,0:T(8,128)S(1)}, u32[]{:S(2)}, u32[]{:S(2)}) collective-permute-start(f32[24,256]{1,0:T(8,128)S(1)} %get-tuple-element.36), channel_id=1, source_target_pairs={{0,1},{1,2},{2,3},{3,4},{4,5},{5,6},{6,7},{7,0},{8,9},{9,10},{10,1... | collective-permute-start | bytes 73736 | tf_op jit(solution)/shard_map/ppermute | solution.py:580
  1.8 5.2 %collective-permute-start.1 = (f32[32,256]{1,0:T(8,128)S(1)}, f32[32,256]{1,0:T(8,128)S(1)}, u32[]{:S(2)}, u32[]{:S(2)}) collective-permute-start(f32[32,256]{1,0:T(8,128)S(1)} %get-tuple-element.37), channel_id=1, source_target_pairs={{0,7},{1,0},{2,1},{3,2},{4,3},{5,4},{6,5},{7,6},{8,15},{9,8},{10,9... | collective-permute-start | bytes 98312 | tf_op jit(solution)/shard_map/ppermute | solution.py:581
  7.5 16.1 %collective-permute-start.3 = (f32[29,8,256]{2,1,0:T(8,128)S(1)}, f32[29,8,256]{2,1,0:T(8,128)S(1)}, u32[]{:S(2)}, u32[]{:S(2)}) collective-permute-start(f32[29,8,256]{2,1,0:T(8,128)S(1)} %get-tuple-element.38.low_ref), channel_id=1, source_target_pairs={{0,120},{8,0},{16,8},{24,16},{32,24},{40,32},{48,40},{56,48},{64,5... | collective-permute-start | bytes 712712 | tf_op jit(solution)/shard_map/ppermute | solution.py:593
  12.8 10.8 %collective-permute-start.2 = (f32[28,8,256]{2,1,0:T(8,128)S(1)}, f32[28,8,256]{2,1,0:T(8,128)S(1)}, u32[]{:S(2)}, u32[]{:S(2)}) collective-permute-start(f32[28,8,256]{2,1,0:T(8,128)S(1)} %get-tuple-element.39.high_ref), channel_id=1, source_target_pairs={{0,8},{8,16},{16,24},{24,32},{32,40},{40,48},{48,56},{56,64},{64,7... | collective-permute-start | bytes 688136 | tf_op jit(solution)/shard_map/ppermute | solution.py:592
  27.7 18.8 %all-to-all-start = ((f32[128,8,128]{2,1,0:T(8,128)}), f32[128,8,128]{2,1,0:T(8,128)S(1)}, u32[]{:S(2)}, u32[]{:S(2)}) async-start(f32[128,8,128]{2,1,0:T(8,128)} %get-tuple-element.53), calls=%async_computation | async-start | bytes 1048576 | tf_op jit(solution)/shard_map/all_to_all | solution.py:655
  49.4 8.5 %copy-start = (s32[512]{0:T(512)S(1)}, s32[512]{0:T(512)}, u32[]{:S(2)}) copy-start(s32[512]{0:T(512)} %param.26) | copy-start | bytes 6148
  49.4 8.5 %collective-permute-start.4 = (f32[12,128]{1,0:T(8,128)S(1)}, f32[12,128]{1,0:T(8,128)S(1)}, u32[]{:S(2)}, u32[]{:S(2)}) collective-permute-start(f32[12,128]{1,0:T(8,128)S(1)} %get-tuple-element.63), channel_id=1, source_target_pairs={{0,1},{1,2},{2,3},{3,4},{4,5},{5,6},{6,7},{7,8},{8,9},{9,10},{10,1... | collective-permute-start | bytes 18440 | tf_op jit(solution)/shard_map/ppermute | solution.py:664

commit v7 on v6

--- a/solution.py
+++ b/solution.py
@@ -438,12 +438,19 @@
     return high, value - high
 
 
+def node_lanes(node, elems):
+    in_lane = lax.broadcasted_iota(jnp.int32, (128, elems), 0)
+    return jnp.where(jnp.broadcast_to(node & 127, in_lane.shape) == in_lane, 1.0, 0.0).astype(jnp.bfloat16)
+
+
 def final_state(
-    matrix_ref, band_ref, at_ref, strength_ref, trial_ref, conn_ref, stress_ref, release_ref, own_ref, ghost_ref
+    matrix_ref, band_ref, at_ref, strength_ref, trial_ref, conn_ref, stress_ref, release_ref, force_ref, ghost_ref
 ):
     elems = conn_ref.shape[1]
-    high, low = halves(band_ref[...])
-    in_row = lax.broadcasted_iota(jnp.int32, (band_ref.shape[0], elems), 0) == at_ref[0:1, :]
+    count = band_ref.shape[0]
+    split = count // 2
+    high, low = halves(band_ref[0:split, :])
+    in_row = lax.broadcasted_iota(jnp.int32, (split, elems), 0) == at_ref[0:1, :]
     found = lax.dot_general(
         jnp.concatenate([high, low], axis=1).astype(jnp.bfloat16),
         jnp.where(in_row, 1.0, 0.0).astype(jnp.bfloat16),
@@ -453,6 +460,13 @@
     found = found[0:128] + found[128:256]
     in_lane = lax.broadcasted_iota(jnp.int32, (128, elems), 0)
     pore = jnp.sum(jnp.where(in_lane == at_ref[1:2, :], found, 0.0), axis=0, keepdims=True)
+    row8, lane8 = (
+        jnp.concatenate([at_ref[i : i + 1, r * 128 : (r + 1) * 128] for r in range(8)], axis=0) for i in range(2)
+    )
+    parts = [jnp.zeros((8, 128), jnp.float32) for _ in range(4)]
+    for r in range(split, count):
+        parts[r % 4] = jnp.where(row8 == r, take_lanes(band_ref[r : r + 1, :], lane8), parts[r % 4])
+    pore = pore + element_rows((parts[0] + parts[1]) + (parts[2] + parts[3]))
     allow = jnp.maximum(strength_ref[0:1, :] - strength_ref[1:2, :] * (trial_ref[6] + pore), 0.0)
     deviator = trial_ref[7]
     yielded = deviator > allow
@@ -468,24 +482,46 @@
         precision=lax.Precision.HIGHEST,
         preferred_element_type=jnp.float32,
     )
-    in_segment = lax.broadcasted_iota(jnp.int32, (16, elems), 0)
+    force_ref[...] = force
     high, low = halves(force)
-    total = jnp.zeros((96, 128), jnp.float32)
+    tile = lax.broadcasted_iota(jnp.int32, (8, elems), 0)
+    total = jnp.zeros((32, 128), jnp.float32)
     for corner in range(8):
         node = conn_ref[corner : corner + 1, :]
-        here = jnp.broadcast_to(node >> 7, in_segment.shape) == in_segment
+        here = jnp.broadcast_to(node >> 7, tile.shape) == 8 + (tile & 3)
         rows = []
-        for source in (high, low):
-            for comp in range(3):
-                value = source[comp * 8 + corner : comp * 8 + corner + 1, :]
-                rows.append(jnp.where(here, jnp.broadcast_to(value, in_segment.shape), 0.0))
+        for comp in range(3):
+            at = slice(comp * 8 + corner, comp * 8 + corner + 1)
+            value = jnp.where(tile < 4, jnp.broadcast_to(high[at], tile.shape), jnp.broadcast_to(low[at], tile.shape))
+            rows.append(jnp.where(here, value, 0.0))
+        rows.append(jnp.zeros(tile.shape, jnp.float32))
         left = jnp.concatenate(rows, axis=0).astype(jnp.bfloat16)
-        right = jnp.where(jnp.broadcast_to(node & 127, in_lane.shape) == in_lane, 1.0, 0.0).astype(jnp.bfloat16)
-        total += lax.dot_general(left, right, (((1,), (1,)), ((), ())), preferred_element_type=jnp.float32)
-    total = total[0:48] + total[48:96]
+        total += lax.dot_general(
+            left, node_lanes(node, elems), (((1,), (1,)), ((), ())), preferred_element_type=jnp.float32
+        )
     for comp in range(3):
-        own_ref[comp * 8 : comp * 8 + 8, :] = total[comp * 16 : comp * 16 + 8]
-        ghost_ref[comp * 4 : comp * 4 + 4, :] = total[comp * 16 + 8 : comp * 16 + 12]
+        ghost_ref[comp * 4 : comp * 4 + 4, :] = total[comp * 8 : comp * 8 + 4] + total[comp * 8 + 4 : comp * 8 + 8]
+
+
+def own_forces(force_ref, conn_ref, own_ref):
+    elems = conn_ref.shape[1]
+    high, low = halves(force_ref[...])
+    tile = lax.broadcasted_iota(jnp.int32, (8, elems), 0)
+    total = jnp.zeros((48, 128), jnp.float32)
+    for corner in range(8):
+        node = conn_ref[corner : corner + 1, :]
+        here = jnp.broadcast_to(node >> 7, tile.shape) == tile
+        rows = []
+        for comp in range(3):
+            for source in (high, low):
+                value = source[comp * 8 + corner : comp * 8 + corner + 1]
+                rows.append(jnp.where(here, jnp.broadcast_to(value, tile.shape), 0.0))
+        left = jnp.concatenate(rows, axis=0).astype(jnp.bfloat16)
+        total += lax.dot_general(
+            left, node_lanes(node, elems), (((1,), (1,)), ((), ())), preferred_element_type=jnp.float32
+        )
+    for comp in range(3):
+        own_ref[comp * 8 : comp * 8 + 8, :] = total[comp * 16 : comp * 16 + 8] + total[comp * 16 + 8 : comp * 16 + 16]
 
 
 def add_returned(own_ref, ghost_ref, shared_ref, out_ref):
@@ -654,14 +690,15 @@
     )(place, strain_rows, disp, after, east, conn, stress)
     incoming = lax.all_to_all(outgoing, AXES, split_axis=0, concat_axis=0, tiled=True)
 
-    stress_new, release, own, ghost = call(
+    stress_new, release, force, ghost = call(
         final_state,
         [VM] * 6,
-        [(6, 8, elems), (8, elems), (24, 128), (12, 128)],
+        [(6, 8, elems), (8, elems), (24, elems), (12, 128)],
         [],
         "final_state",
     )(force_rows, incoming.reshape(devices * 8, 128), places, strength, trial, conn)
     returned = lax.ppermute(ghost, AXES, steps(devices, 1))
+    (own,) = call(own_forces, [VM] * 2, [(24, 128)], [], "own_forces")(force, conn)
     (node_forces,) = call(add_returned, [VM] * 3, [(3, nodes)], [], "add_returned")(own, returned, shared)
     return (head_out, stress_new.transpose(1, 0, 2), release, node_forces)
 

time: 59 us -> 58.4 us (0.990)
  waiting for transfers between devices: 29.7 us -> 28.8 us
    ppermute x1, waiting for transfers between devices: 8.5 us -> 7.65 us  [per_device(): returned = lax.ppermute(ghost, AXES, steps(devices, 1))]
    pallas_call x1 -> x2, Pallas kernels: 2.95 us -> 3.22 us  [the longest x1 2.38 us: per_device(): call(final_state, [VM] * 6, [(6, 8, elems), (8, elems), (24, elems), (12,...]
  transfers between devices with their start and end apart: 6 -> 6, of which waited for: 5 -> 5; matrix products, arithmetic and copies ran while one was open for 0% -> 0% of each run, Pallas kernels for 8% -> 10%
where the time goes in v7:
time: 58.4 us; the launch traced here: 58.1 us
  waiting for transfers between devices  28.8 us (49%)
  Pallas kernels  14.6 us (25%)
  starting transfers between devices  13.9 us (24%)
  between operations  0.7 us (1%)
    all_to_all x1, waiting for transfers between devices, per_device(): lax.all_to_all(outgoing, AXES, split_axis=0, concat_axis=0, tiled=True)  10.2 us
    ppermute x1, waiting for transfers between devices, per_device(): west = lax.ppermute(high, 'crest', steps(crest, 1))  9.44 us
    ppermute x1, waiting for transfers between devices, per_device(): returned = lax.ppermute(ghost, AXES, steps(devices, 1))  7.65 us
    ppermute x1, starting transfers between devices, per_device(): east = lax.ppermute(low, 'crest', steps(crest, -1))  5.28 us
    all_to_all x1, starting transfers between devices, per_device(): lax.all_to_all(outgoing, AXES, split_axis=0, concat_axis=0, tiled=True)  5.01 us
    pallas_call x1, Pallas kernels, per_device(): call(functools.partial(seepage, crest), [SM] + [VM] * 12, [pressure_head....  4.06 us
    ppermute x1, starting transfers between devices, per_device(): after = lax.ppermute(backward, 'section', steps(section, -1))  3.57 us
    pallas_call x1, Pallas kernels, per_device(): call(final_state, [VM] * 6, [(6, 8, elems), (8, elems), (24, elems), (12,...  2.38 us
  transfers between devices with their start and end apart: 6, of which 5 were waited for; matrix products, arithmetic and copies ran while one was open for 0% of the time, Pallas kernels for 10%

profile of v7, /device:TPU:0, one launch (start us, length us, event | category | flops | bytes accessed | tf_op | source)
XLA Modules:
  0.0 58.1 jit_solution(13136407620268642406)
XLA Ops:
  0.6 1.1 %pack_section.1 = (f32[24,256]{1,0:T(8,128)S(1)}, f32[32,256]{1,0:T(8,128)S(1)}, f32[4,32,256]{2,1,0:T(8,128)S(1)}, s32[4,32,256]{2,1,0:T(8,128)S(1)}) custom-call(f32[4,32,256]{2,1,0:T(8,128)} %head_hbm.1, s32[4,32,256]{2,1,0:T(8,128)} %zone_hbm.1, f32[3,1024]{1,0:T(4,128)} %disp_hbm.3, s32[4,128]{1,0:T(4,128)} %bitcast.14), custom_call_target="tpu_custom_call" | custom-call | tf_op jit(solution)/shard_map/pack_section/pallas_call | solution.py:608
  1.8 0.0 collective-permute-start
  1.8 3.6 %collective-permute-start.1 = (f32[32,256]{1,0:T(8,128)S(1)}, f32[32,256]{1,0:T(8,128)S(1)}, u32[]{:S(2)}, u32[]{:S(2)}) collective-permute-start(f32[32,256]{1,0:T(8,128)S(1)} %get-tuple-element.37), channel_id=1, source_target_pairs={{0,7},{1,0},{2,1},{3,2},{4,3},{5,4},{6,5},{7,6},{8,15},{9,8},{10,9... | collective-permute-start | bytes 98312 | tf_op jit(solution)/shard_map/ppermute | solution.py:617
  5.4 0.1 pad_add_fusion.place_ref
  5.4 1.4 %collective-permute-done.before_ref = f32[24,256]{1,0:T(8,128)S(1)} collective-permute-done((f32[24,256]{1,0:T(8,128)S(1)}, f32[24,256]{1,0:T(8,128)S(1)}, u32[]{:S(2)}, u32[]{:S(2)}) %collective-permute-start) | collective-permute-done | bytes 24608 | tf_op jit(solution)/shard_map/ppermute | solution.py:616
  6.8 0.1 collective-permute-done.1.after_ref
  7.0 0.6 pack_crest.1
  7.5 5.3 %collective-permute-start.3 = (f32[29,8,256]{2,1,0:T(8,128)S(1)}, f32[29,8,256]{2,1,0:T(8,128)S(1)}, u32[]{:S(2)}, u32[]{:S(2)}) collective-permute-start(f32[29,8,256]{2,1,0:T(8,128)S(1)} %get-tuple-element.38.low_ref), channel_id=1, source_target_pairs={{0,120},{8,0},{16,8},{24,16},{32,24},{40,32},{48,40},{56,48},{64,5... | collective-permute-start | bytes 712712 | tf_op jit(solution)/shard_map/ppermute | solution.py:629
  12.8 0.0 collective-permute-start.2
  12.8 1.4 %prepare.1 = (f32[32,256]{1,0:T(8,128)S(1)}, s32[128,128]{1,0:T(8,128)S(1)}, f32[4,40,256]{2,1,0:T(8,128)S(1)}, f32[4,40,256]{2,1,0:T(8,128)S(1)}, f32[4,40,256]...) custom-call(f32[29,8,256]{2,1,0:T(8,128)S(1)} %get-tuple-element.38., ...), custom_call_target="tpu_custom_call" | custom-call | tf_op jit(solution)/shard_map/prepare/pallas_call | solution.py:631
  14.2 9.4 %collective-permute-done.2.before_ref = f32[28,8,256]{2,1,0:T(8,128)S(1)} collective-permute-done((f32[28,8,256]{2,1,0:T(8,128)S(1)}, f32[28,8,256]{2,1,0:T(8,128)S(1)}, u32[]{:S(2)}, u32[]{:S(2)}) %collective-permute-start.2) | collective-permute-done | bytes 229408 | tf_op jit(solution)/shard_map/ppermute | solution.py:628
  23.6 0.0 collective-permute-done.3.after_ref.tail_ref
  23.6 4.1 %seepage.1 = (f32[4,32,256]{2,1,0:T(8,128)}, f32[128,8,128]{2,1,0:T(8,128)}, f32[8,128]{1,0:T(8,128)S(1)}) custom-call(s32[3]{0:T(128)S(1)} %pad_add_fusion.place_ref, f32[32,256]{1,0:T(8,128)S(1)} %get-tuple-element.40.tables_ref, s32[128,128]{1,0:T(8,128)S(1)} %get-tuple-element.41.index, f32[4,40,256]{2,1,0:T(8,128)S(1)} %get-tuple-element.42.own_h, ...), custom_call_target="tpu_custom_call" | custom-call | tf_op jit(solution)/shard_map/seepage/pallas_call | solution.py:641
  27.7 5.0 %all-to-all-start = ((f32[128,8,128]{2,1,0:T(8,128)}), f32[128,8,128]{2,1,0:T(8,128)S(1)}, u32[]{:S(2)}, u32[]{:S(2)}) async-start(f32[128,8,128]{2,1,0:T(8,128)} %get-tuple-element.53), calls=%async_computation | async-start | bytes 1048576 | tf_op jit(solution)/shard_map/all_to_all | solution.py:691
  32.7 1.8 %selectors.1 = (f32[3,1024]{1,0:T(4,128)S(1)}, f32[6,8,1024]{2,1,0:T(8,128)S(1)}, s32[8,1024]{1,0:T(8,128)S(1)}, f32[48,24]{1,0:T(8,128)S(1)}, f32[24,48]{1,0:T(...) custom-call(s32[3]{0:T(128)S(1)} %pad_add_fusion.place_ref, f32[8,128]{1,0:T(8,128)S(1)} %get-tuple-element.51.order_ref, ...), custom_call_target="tpu_custom_call" | custom-call | tf_op jit(solution)/shard_map/selectors/pallas_call | solution.py:650
  34.5 1.8 %trial_state.1.trial_ref = f32[8,8,1024]{2,1,0:T(8,128)S(1)} custom-call(s32[3]{0:T(128)S(1)} %pad_add_fusion.place_ref, f32[48,24]{1,0:T(8,128)S(1)} %get-tuple-element.56.matrix_ref, f32[3,1024]{1,0:T(4,128)S(1)} %get-tuple-element.57.disp_ref, f32[32,256]{1,0:T(8,128)S(1)} %collective-permute-done.1.after_ref, ...), custom_call_target="tpu_custom_call" | custom-call | tf_op jit(solution)/shard_map/trial_state/pallas_call | solution.py:684
  36.3 10.2 %all-to-all-done = f32[128,8,128]{2,1,0:T(8,128)S(1)} async-done(((f32[128,8,128]{2,1,0:T(8,128)}), f32[128,8,128]{2,1,0:T(8,128)S(1)}, u32[]{:S(2)}, u32[]{:S(2)}) %all-to-all-start) | async-done | bytes 524320 | tf_op jit(solution)/shard_map/all_to_all | solution.py:691
  46.5 2.4 %final_state.1 = (f32[6,8,1024]{2,1,0:T(8,128)}, f32[8,1024]{1,0:T(8,128)}, f32[24,1024]{1,0:T(8,128)S(1)}, f32[12,128]{1,0:T(8,128)S(1)}) custom-call(f32[24,48]{1,0:T(8,128)S(1)} %get-tuple-element.52.matrix_ref, f32[1024,128]{1,0:T(8,128)S(1)} %bitcast.13, s32[2,1024]{1,0:T(2,128)S(1)} %get-tuple-element.54.at_ref, ...), custom_call_target="tpu_custom_call" | custom-call | tf_op jit(solution)/shard_map/final_state/pallas_call | solution.py:693
  48.9 0.0 collective-permute-start.4
  48.9 0.0 copy-start
  48.9 0.8 %own_forces.1.own_ref = f32[24,128]{1,0:T(8,128)S(1)} custom-call(f32[24,1024]{1,0:T(8,128)S(1)} %get-tuple-element.62.force_ref, s32[8,1024]{1,0:T(8,128)S(1)} %get-tuple-element.58.conn_ref), custom_call_target="tpu_custom_call" | custom-call | tf_op jit(solution)/shard_map/own_forces/pallas_call | solution.py:701
  49.7 7.7 %collective-permute-done.4.ghost_ref = f32[12,128]{1,0:T(8,128)S(1)} collective-permute-done((f32[12,128]{1,0:T(8,128)S(1)}, f32[12,128]{1,0:T(8,128)S(1)}, u32[]{:S(2)}, u32[]{:S(2)}) %collective-permute-start.4) | collective-permute-done | bytes 6176 | tf_op jit(solution)/shard_map/ppermute | solution.py:700
  57.4 0.0 copy-done
  57.4 0.8 %add_returned.1 = f32[3,1024]{1,0:T(4,128)} custom-call(f32[24,128]{1,0:T(8,128)S(1)} %own_forces.1.own_ref, f32[12,128]{1,0:T(8,128)S(1)} %collective-permute-done.4.ghost_ref, s32[4,128]{1,0:T(4,128)S(1)} %bitcast.15), custom_call_target="tpu_custom_call" | custom-call | tf_op jit(solution)/shard_map/add_returned/pallas_call | solution.py:702
Async XLA Ops:
  1.8 5.1 %collective-permute-start = (f32[24,256]{1,0:T(8,128)S(1)}, f32[24,256]{1,0:T(8,128)S(1)}, u32[]{:S(2)}, u32[]{:S(2)}) collective-permute-start(f32[24,256]{1,0:T(8,128)S(1)} %get-tuple-element.36), channel_id=1, source_target_pairs={{0,1},{1,2},{2,3},{3,4},{4,5},{5,6},{6,7},{7,0},{8,9},{9,10},{10,1... | collective-permute-start | bytes 73736 | tf_op jit(solution)/shard_map/ppermute | solution.py:616
  1.8 5.2 %collective-permute-start.1 = (f32[32,256]{1,0:T(8,128)S(1)}, f32[32,256]{1,0:T(8,128)S(1)}, u32[]{:S(2)}, u32[]{:S(2)}) collective-permute-start(f32[32,256]{1,0:T(8,128)S(1)} %get-tuple-element.37), channel_id=1, source_target_pairs={{0,7},{1,0},{2,1},{3,2},{4,3},{5,4},{6,5},{7,6},{8,15},{9,8},{10,9... | collective-permute-start | bytes 98312 | tf_op jit(solution)/shard_map/ppermute | solution.py:617
  7.5 16.1 %collective-permute-start.3 = (f32[29,8,256]{2,1,0:T(8,128)S(1)}, f32[29,8,256]{2,1,0:T(8,128)S(1)}, u32[]{:S(2)}, u32[]{:S(2)}) collective-permute-start(f32[29,8,256]{2,1,0:T(8,128)S(1)} %get-tuple-element.38.low_ref), channel_id=1, source_target_pairs={{0,120},{8,0},{16,8},{24,16},{32,24},{40,32},{48,40},{56,48},{64,5... | collective-permute-start | bytes 712712 | tf_op jit(solution)/shard_map/ppermute | solution.py:629
  12.8 10.8 %collective-permute-start.2 = (f32[28,8,256]{2,1,0:T(8,128)S(1)}, f32[28,8,256]{2,1,0:T(8,128)S(1)}, u32[]{:S(2)}, u32[]{:S(2)}) collective-permute-start(f32[28,8,256]{2,1,0:T(8,128)S(1)} %get-tuple-element.39.high_ref), channel_id=1, source_target_pairs={{0,8},{8,16},{16,24},{24,32},{32,40},{40,48},{48,56},{56,64},{64,7... | collective-permute-start | bytes 688136 | tf_op jit(solution)/shard_map/ppermute | solution.py:628
  27.7 18.8 %all-to-all-start = ((f32[128,8,128]{2,1,0:T(8,128)}), f32[128,8,128]{2,1,0:T(8,128)S(1)}, u32[]{:S(2)}, u32[]{:S(2)}) async-start(f32[128,8,128]{2,1,0:T(8,128)} %get-tuple-element.53), calls=%async_computation | async-start | bytes 1048576 | tf_op jit(solution)/shard_map/all_to_all | solution.py:691
  48.9 8.5 %collective-permute-start.4 = (f32[12,128]{1,0:T(8,128)S(1)}, f32[12,128]{1,0:T(8,128)S(1)}, u32[]{:S(2)}, u32[]{:S(2)}) collective-permute-start(f32[12,128]{1,0:T(8,128)S(1)} %get-tuple-element.63), channel_id=1, source_target_pairs={{0,1},{1,2},{2,3},{3,4},{4,5},{5,6},{6,7},{7,8},{8,9},{9,10},{10,1... | collective-permute-start | bytes 18440 | tf_op jit(solution)/shard_map/ppermute | solution.py:700
  48.9 8.5 %copy-start = (s32[512]{0:T(512)S(1)}, s32[512]{0:T(512)}, u32[]{:S(2)}) copy-start(s32[512]{0:T(512)} %param.26) | copy-start | bytes 6148

commit v8 on v7

--- a/solution.py
+++ b/solution.py
@@ -104,23 +104,22 @@
     backward_ref[30:32, :] = jnp.zeros((2, 256), jnp.float32)
 
 
-def pack_crest(sections, place_ref, head_ref, zone_ref, before_ref, after_ref, low_ref, high_ref):
+def pack_crest(sections, place_ref, head_ref, zone_ref, flux_ref, before_ref, after_ref, low_ref, high_ref):
     planes, rows = head_ref.shape[0], head_ref.shape[1]
     groups = rows // 8
     behind = jnp.where(place_ref[0] > 0, 1.0, 0.0)
     ahead = jnp.where(place_ref[0] < sections - 1, 1.0, 0.0)
-    for field in range(2):
-        first = field * (WIDE * groups + 2)
-        for x in range(planes):
+    zone_at = 2 * groups + 2
+    for x in range(planes):
+        target, plane = (low_ref, x) if x < 2 else (high_ref, x - 2)
+        for field in range(2):
+            first = field * zone_at
             for group in range(groups):
                 at = slice(8 * group, 8 * group + 8)
                 own = head_ref[x, at, :] if field == 0 else zone_ref[x, at, :].astype(jnp.float32) + 1.0
-                if x < WIDE:
-                    low_ref[first + x * groups + group] = own
-                if x >= planes - WIDE:
-                    high_ref[first + (x - planes + WIDE) * groups + group] = own
+                target[first + plane * groups + group] = own
             at = field * WIDE * planes + WIDE * x
-            tail = jnp.concatenate(
+            target[first + 2 * groups + plane] = jnp.concatenate(
                 [
                     after_ref[at : at + WIDE, :] * ahead,
                     jnp.zeros((2, after_ref.shape[1]), jnp.float32),
@@ -128,11 +127,10 @@
                 ],
                 axis=0,
             )
-            if x < 2:
-                low_ref[first + WIDE * groups + x] = tail
-            else:
-                high_ref[first + WIDE * groups + x - 2] = tail
-    low_ref[2 * (WIDE * groups + 2)] = after_ref[24:32, :]
+    for group in range(groups):
+        low_ref[2 * zone_at + group] = flux_ref[group]
+        high_ref[2 * zone_at + group] = flux_ref[group]
+    low_ref[2 * zone_at + groups] = after_ref[24:32, :]
 
 
 def choose(values, bits):
@@ -141,17 +139,20 @@
     return values[0]
 
 
-def fields(tables_ref, out, x, row, head, zone):
+def params(tables_ref, zone):
     zones = tables_ref.shape[0] // 4
     tables = [
-        [jnp.broadcast_to(tables_ref[f * zones + z : f * zones + z + 1, :], head.shape) for z in range(zones)]
+        [jnp.broadcast_to(tables_ref[f * zones + z : f * zones + z + 1, :], zone.shape) for z in range(zones)]
         for f in range(4)
     ]
     zone = zone.astype(jnp.int32) - 1
     bits = [(zone & (1 << bit)) != 0 for bit in range(3)]
     alpha, less, m, root = (choose(table, bits) for table in tables)
-    values = (head, alpha, less, m, jnp.where(zone >= 0, root, 0.0), THETA_GAP * alpha * less)
-    for ref, value in zip(out, values):
+    return alpha, less, m, jnp.where(zone >= 0, root, 0.0), THETA_GAP * alpha * less
+
+
+def fields(tables_ref, out, x, row, head, zone):
+    for ref, value in zip(out, (head,) + params(tables_ref, zone)):
         ref[x, row : row + 8, :] = value
 
 
@@ -170,23 +171,16 @@
     return root * fourth * (1.0 - part), TIME_STEP * plus / (STORAGE * plus + gain * part)
 
 
-def prepare(
-    low_ref,
-    high_ref,
+def inner_flux(
+    head_ref,
+    zone_ref,
     wanted_hbm,
     alpha_hbm,
     expo_hbm,
     ks_hbm,
     tables_ref,
     index_ref,
-    h,
-    alpha_f,
-    less_f,
-    m_f,
-    root_f,
-    gain_f,
-    r_f,
-    cap_f,
+    flux_ref,
     wanted_ref,
     alpha_ref,
     expo_ref,
@@ -204,15 +198,24 @@
         tables_ref[3 * zones + z : 3 * zones + z + 1, :] = jnp.sqrt(jnp.full((1, width), ks_ref[z], jnp.float32))
     wanted = wanted_ref[...]
     index_ref[...] = jnp.concatenate([wanted, pltpu.roll(wanted, wanted.shape[1] // 2, 1)], axis=0).T
+    for group in range(flux_ref.shape[0]):
+        at = slice(8 * group, 8 * group + 8)
+        near, far = head_ref[1, at, :], head_ref[2, at, :]
+        r_near, _ = retention(near, *params(tables_ref, zone_ref[1, at, :] + 1))
+        r_far, _ = retention(far, *params(tables_ref, zone_ref[2, at, :] + 1))
+        flux_ref[group] = r_near * r_far * (far - near)
+
+
+def prepare(tables_ref, low_ref, high_ref, h, alpha_f, less_f, m_f, root_f, gain_f, r_f, cap_f):
     planes, groups = h.shape[0], h.shape[1] // 8 - 1
+    zone_at = 2 * groups + 2
     out = (h, alpha_f, less_f, m_f, root_f, gain_f)
     for x in range(planes):
-        source, plane, tail = (low_ref, x, x) if x < 2 else (high_ref, x - planes + WIDE, x - 2)
-        zone_at = WIDE * groups + 2
+        source, plane = (low_ref, x) if x < 2 else (high_ref, x - 2)
         for group in range(groups):
             at = plane * groups + group
             fields(tables_ref, out, x, 8 * group, source[at], source[zone_at + at])
-        at = WIDE * groups + tail
+        at = 2 * groups + plane
         fields(tables_ref, out, x, 8 * groups, source[at], source[zone_at + at])
         r_f[x], cap_f[x] = retention(*(ref[x] for ref in out))
 
@@ -251,23 +254,22 @@
     total = planes + 2 * WIDE
     height, depth = h.shape[1], h.shape[2]
     groups = rows // 8
-    zone_at = WIDE * groups + 2
+    zone_at = 2 * groups + 2
     lane8 = lax.broadcasted_iota(jnp.int32, (8, 128), 1)
     behind = jnp.where(place_ref[1] > 0, 1.0, 0.0)
     ahead = jnp.where(place_ref[1] < crests - 1, 1.0, 0.0)
     out = (h, alpha_f, less_f, m_f, root_f, gain_f)
 
-    for source, first, tail, inside in ((before_ref, 0, 1, behind), (after_ref, WIDE + planes, 0, ahead)):
-        for plane in range(WIDE):
+    ends = []
+    for source, first, inside in ((before_ref, 1, behind), (after_ref, WIDE + planes, ahead)):
+        for plane in range(2):
             for group in range(groups):
                 at = plane * groups + group
                 fields(tables_ref, out, first + plane, 8 * group, source[at], source[zone_at + at] * inside)
-        for plane in range(2):
-            at = WIDE * groups + plane
-            fields(tables_ref, out, first + tail + plane, rows, source[at], source[zone_at + at] * inside)
-    for x in (0, total - 1):
-        for ref in out:
-            ref[x, rows:height, :] = jnp.zeros((height - rows, depth), jnp.float32)
+            at = 2 * groups + plane
+            fields(tables_ref, out, first + plane, rows, source[at], source[zone_at + at] * inside)
+        flux = [source[2 * zone_at + group] * inside for group in range(groups)]
+        ends.append(jnp.concatenate(flux + [jnp.zeros((height - rows, depth), jnp.float32)], axis=0))
     for x in range(planes):
         h[WIDE + x] = own_h[x]
 
@@ -280,7 +282,7 @@
 
     for sweep in range(SWEEPS):
         held = {}
-        for x in range(sweep, total - sweep):
+        for x in range(max(sweep, 1), total - max(sweep, 1)):
             if sweep == 0 and WIDE <= x < WIDE + planes:
                 held[x] = (own_r, own_cap, x - WIDE)
             else:
@@ -294,10 +296,10 @@
         def face(x):
             return r_of(x) * r_of(x + 1) * (h[x + 1] - h[x])
 
-        came = face(sweep)
+        came = face(sweep) if sweep > 0 else ends[0]
         for x in range(sweep + 1, total - sweep - 1):
             here, r = h[x], r_of(x)
-            goes = face(x)
+            goes = face(x) if x < total - 2 or sweep > 0 else ends[1]
             flux_y = r * pltpu.roll(r, height - 1, 0) * (pltpu.roll(here, height - 1, 0) - here)
             flux_z = r * pltpu.roll(r, depth - 1, 1) * (pltpu.roll(here, depth - 1, 1) - here + 1.0)
             flux_z = jnp.where(inner_z, flux_z, 0.0)
@@ -617,25 +619,26 @@
     after = lax.ppermute(backward, "section", steps(section, -1))
 
     groups = rows // 8
-    edge = (2 * (WIDE * groups + 2), 8, depth)
+    tables, index, flux = call(
+        inner_flux,
+        [VM] * 2 + [HBM] * 4,
+        [(4 * zones, depth), (devices, 128), (groups, 8, depth)],
+        [pltpu.VMEM((64, devices), i32)] + [pltpu.SMEM((zones,), f32)] * 3 + [pltpu.SemaphoreType.DMA((4,))],
+        "inner_flux",
+        [f32, i32, f32],
+    )(head, zone, *(in_hbm(x) for x in (sent_columns[0].T, retention_alpha, retention_exponent, conductivity)))
+
+    edge = (2 * (2 * groups + 2) + groups, 8, depth)
     low, high = call(
         functools.partial(pack_crest, section),
-        [SM] + [VM] * 4,
+        [SM] + [VM] * 5,
         [(edge[0] + 1, 8, depth), edge],
         [],
         "pack_crest",
-    )(place, head, zone, before, after)
+    )(place, head, zone, flux, before, after)
     west = lax.ppermute(high, "crest", steps(crest, 1))
     east = lax.ppermute(low, "crest", steps(crest, -1))
-
-    tables, index, *own = call(
-        prepare,
-        [VM] * 2 + [HBM] * 4,
-        [(4 * zones, depth), (devices, 128)] + [(planes, height, depth)] * 8,
-        [pltpu.VMEM((64, devices), i32)] + [pltpu.SMEM((zones,), f32)] * 3 + [pltpu.SemaphoreType.DMA((4,))],
-        "prepare",
-        [f32, i32] + [f32] * 8,
-    )(low, high, *(in_hbm(x) for x in (sent_columns[0].T, retention_alpha, retention_exponent, conductivity)))
+    own = call(prepare, [VM] * 3, [(planes, height, depth)] * 8, [], "prepare")(tables, low, high)
 
     field = pltpu.VMEM((planes + 2 * WIDE, height, depth), f32)
     head_out, outgoing, order = call(

time: 58.4 us -> 57.5 us (0.985)
  waiting for transfers between devices: 28.8 us -> 28 us
    ppermute x1, waiting for transfers between devices: 1.41 us -> 0.32 us  [per_device(): before = lax.ppermute(forward, 'section', steps(section, 1))]
    pallas_call x2 -> x3, Pallas kernels: 1.94 us -> 2.12 us  [the longest x1 1.08 us: per_device(): call(inner_flux, [VM] * 2 + [HBM] * 4, [(4 * zones, depth), (devices, 128...]
where the time goes in v8:
time: 57.5 us; the launch traced here: 57.2 us
  waiting for transfers between devices  28 us (49%)
  Pallas kernels  14.6 us (25%)
  starting transfers between devices  13.9 us (24%)
  between operations  0.7 us (1%)
    all_to_all x1, waiting for transfers between devices, per_device(): lax.all_to_all(outgoing, AXES, split_axis=0, concat_axis=0, tiled=True)  10.2 us
    ppermute x1, waiting for transfers between devices, per_device(): west = lax.ppermute(high, 'crest', steps(crest, 1))  9.65 us
    ppermute x1, waiting for transfers between devices, per_device(): returned = lax.ppermute(ghost, AXES, steps(devices, 1))  7.65 us
    ppermute x1, starting transfers between devices, per_device(): east = lax.ppermute(low, 'crest', steps(crest, -1))  5.28 us
    all_to_all x1, starting transfers between devices, per_device(): lax.all_to_all(outgoing, AXES, split_axis=0, concat_axis=0, tiled=True)  5.01 us
    pallas_call x1, Pallas kernels, per_device(): call(functools.partial(seepage, crest), [SM] + [VM] * 12, [pressure_head....  3.86 us
    ppermute x1, starting transfers between devices, per_device(): after = lax.ppermute(backward, 'section', steps(section, -1))  3.57 us
    pallas_call x1, Pallas kernels, per_device(): call(final_state, [VM] * 6, [(6, 8, elems), (8, elems), (24, elems), (12,...  2.38 us
  transfers between devices with their start and end apart: 6, of which 5 were waited for; matrix products, arithmetic and copies ran while one was open for 0% of the time, Pallas kernels for 10%

profile of v8, /device:TPU:0, one launch (start us, length us, event | category | flops | bytes accessed | tf_op | source)
XLA Modules:
  0.0 57.2 jit_solution(4068108683009609817)
XLA Ops:
  0.6 1.1 %pack_section.1 = (f32[24,256]{1,0:T(8,128)S(1)}, f32[32,256]{1,0:T(8,128)S(1)}, f32[4,32,256]{2,1,0:T(8,128)S(1)}, s32[4,32,256]{2,1,0:T(8,128)S(1)}) custom-call(f32[4,32,256]{2,1,0:T(8,128)} %head_hbm.1, s32[4,32,256]{2,1,0:T(8,128)} %zone_hbm.1, f32[3,1024]{1,0:T(4,128)} %disp_hbm.3, s32[4,128]{1,0:T(4,128)} %bitcast.14), custom_call_target="tpu_custom_call" | custom-call | tf_op jit(solution)/shard_map/pack_section/pallas_call | solution.py:610
  1.8 0.0 collective-permute-start
  1.8 3.6 %collective-permute-start.1 = (f32[32,256]{1,0:T(8,128)S(1)}, f32[32,256]{1,0:T(8,128)S(1)}, u32[]{:S(2)}, u32[]{:S(2)}) collective-permute-start(f32[32,256]{1,0:T(8,128)S(1)} %get-tuple-element.41), channel_id=1, source_target_pairs={{0,7},{1,0},{2,1},{3,2},{4,3},{5,4},{6,5},{7,6},{8,15},{9,8},{10,9... | collective-permute-start | bytes 98312 | tf_op jit(solution)/shard_map/ppermute | solution.py:619
  5.4 0.1 pad_add_fusion.place_ref
  5.4 1.1 %inner_flux.1 = (f32[32,256]{1,0:T(8,128)S(1)}, s32[128,128]{1,0:T(8,128)S(1)}, f32[4,8,256]{2,1,0:T(8,128)S(1)}) custom-call(f32[4,32,256]{2,1,0:T(8,128)S(1)} %get-tuple-element.35.head_ref, s32[4,32,256]{2,1,0:T(8,128)S(1)} %get-tuple-element.36.zone_ref, s32[64,128]{1,0:T(8,128)} %bitcast.17, f32[8]{0:T(128)} %alpha_hbm.1, f32[8]{0:T(128)} %expo_hbm.1, ...), custom_call_target="tpu_custom_call" | custom-call | tf_op jit(solution)/shard_map/inner_flux/pallas_call | solution.py:622
  6.5 0.3 collective-permute-done.before_ref
  6.8 0.1 collective-permute-done.1.after_ref
  7.0 0.6 %pack_crest.1 = (f32[25,8,256]{2,1,0:T(8,128)S(1)}, f32[24,8,256]{2,1,0:T(8,128)S(1)}) custom-call(s32[3]{0:T(128)S(1)} %pad_add_fusion.place_ref, f32[4,32,256]{2,1,0:T(8,128)S(1)} %get-tuple-element.35.head_ref, s32[4,32,256]{2,1,0:T(8,128)S(1)} %get-tuple-element.36.zone_ref, f32[4,8,256]{2,1,0:T(8,128)S(1)} %get-tuple-element.39.flux_ref, ...), custom_call_target="tpu_custom_call" | custom-call | tf_op jit(solution)/shard_map/pack_crest/pallas_call | solution.py:632
  7.5 5.3 %collective-permute-start.3 = (f32[25,8,256]{2,1,0:T(8,128)S(1)}, f32[25,8,256]{2,1,0:T(8,128)S(1)}, u32[]{:S(2)}, u32[]{:S(2)}) collective-permute-start(f32[25,8,256]{2,1,0:T(8,128)S(1)} %get-tuple-element.42.low_ref), channel_id=1, source_target_pairs={{0,120},{8,0},{16,8},{24,16},{32,24},{40,32},{48,40},{56,48},{64,5... | collective-permute-start | bytes 614408 | tf_op jit(solution)/shard_map/ppermute | solution.py:640
  12.8 0.0 collective-permute-start.2
  12.8 0.5 prepare.1
  13.3 9.7 %collective-permute-done.2.before_ref = f32[24,8,256]{2,1,0:T(8,128)S(1)} collective-permute-done((f32[24,8,256]{2,1,0:T(8,128)S(1)}, f32[24,8,256]{2,1,0:T(8,128)S(1)}, u32[]{:S(2)}, u32[]{:S(2)}) %collective-permute-start.2) | collective-permute-done | bytes 196640 | tf_op jit(solution)/shard_map/ppermute | solution.py:639
  22.9 0.0 collective-permute-done.3.after_ref.tail_ref
  22.9 3.9 %seepage.1 = (f32[4,32,256]{2,1,0:T(8,128)}, f32[128,8,128]{2,1,0:T(8,128)}, f32[8,128]{1,0:T(8,128)S(1)}) custom-call(s32[3]{0:T(128)S(1)} %pad_add_fusion.place_ref, f32[32,256]{1,0:T(8,128)S(1)} %get-tuple-element.37.tables_ref, s32[128,128]{1,0:T(8,128)S(1)} %get-tuple-element.38.index, f32[4,40,256]{2,1,0:T(8,128)S(1)} %get-tuple-element.44.own_h, ...), custom_call_target="tpu_custom_call" | custom-call | tf_op jit(solution)/shard_map/seepage/pallas_call | solution.py:644
  26.8 5.0 %all-to-all-start = ((f32[128,8,128]{2,1,0:T(8,128)}), f32[128,8,128]{2,1,0:T(8,128)S(1)}, u32[]{:S(2)}, u32[]{:S(2)}) async-start(f32[128,8,128]{2,1,0:T(8,128)} %get-tuple-element.55), calls=%async_computation | async-start | bytes 1048576 | tf_op jit(solution)/shard_map/all_to_all | solution.py:694
  31.8 1.8 %selectors.1 = (f32[3,1024]{1,0:T(4,128)S(1)}, f32[6,8,1024]{2,1,0:T(8,128)S(1)}, s32[8,1024]{1,0:T(8,128)S(1)}, f32[48,24]{1,0:T(8,128)S(1)}, f32[24,48]{1,0:T(...) custom-call(s32[3]{0:T(128)S(1)} %pad_add_fusion.place_ref, f32[8,128]{1,0:T(8,128)S(1)} %get-tuple-element.53.order_ref, ...), custom_call_target="tpu_custom_call" | custom-call | tf_op jit(solution)/shard_map/selectors/pallas_call | solution.py:653
  33.6 1.8 %trial_state.1.trial_ref = f32[8,8,1024]{2,1,0:T(8,128)S(1)} custom-call(s32[3]{0:T(128)S(1)} %pad_add_fusion.place_ref, f32[48,24]{1,0:T(8,128)S(1)} %get-tuple-element.58.matrix_ref, f32[3,1024]{1,0:T(4,128)S(1)} %get-tuple-element.59.disp_ref, f32[32,256]{1,0:T(8,128)S(1)} %collective-permute-done.1.after_ref, ...), custom_call_target="tpu_custom_call" | custom-call | tf_op jit(solution)/shard_map/trial_state/pallas_call | solution.py:687
  35.4 10.2 %all-to-all-done = f32[128,8,128]{2,1,0:T(8,128)S(1)} async-done(((f32[128,8,128]{2,1,0:T(8,128)}), f32[128,8,128]{2,1,0:T(8,128)S(1)}, u32[]{:S(2)}, u32[]{:S(2)}) %all-to-all-start) | async-done | bytes 524320 | tf_op jit(solution)/shard_map/all_to_all | solution.py:694
  45.6 2.4 %final_state.1 = (f32[6,8,1024]{2,1,0:T(8,128)}, f32[8,1024]{1,0:T(8,128)}, f32[24,1024]{1,0:T(8,128)S(1)}, f32[12,128]{1,0:T(8,128)S(1)}) custom-call(f32[24,48]{1,0:T(8,128)S(1)} %get-tuple-element.54.matrix_ref, f32[1024,128]{1,0:T(8,128)S(1)} %bitcast.13, s32[2,1024]{1,0:T(2,128)S(1)} %get-tuple-element.56.at_ref, ...), custom_call_target="tpu_custom_call" | custom-call | tf_op jit(solution)/shard_map/final_state/pallas_call | solution.py:696
  47.9 0.0 collective-permute-start.4
  48.0 0.0 copy-start
  48.0 0.8 %own_forces.1.own_ref = f32[24,128]{1,0:T(8,128)S(1)} custom-call(f32[24,1024]{1,0:T(8,128)S(1)} %get-tuple-element.64.force_ref, s32[8,1024]{1,0:T(8,128)S(1)} %get-tuple-element.60.conn_ref), custom_call_target="tpu_custom_call" | custom-call | tf_op jit(solution)/shard_map/own_forces/pallas_call | solution.py:704
  48.8 7.7 %collective-permute-done.4.ghost_ref = f32[12,128]{1,0:T(8,128)S(1)} collective-permute-done((f32[12,128]{1,0:T(8,128)S(1)}, f32[12,128]{1,0:T(8,128)S(1)}, u32[]{:S(2)}, u32[]{:S(2)}) %collective-permute-start.4) | collective-permute-done | bytes 6176 | tf_op jit(solution)/shard_map/ppermute | solution.py:703
  56.5 0.0 copy-done
  56.5 0.8 %add_returned.1 = f32[3,1024]{1,0:T(4,128)} custom-call(f32[24,128]{1,0:T(8,128)S(1)} %own_forces.1.own_ref, f32[12,128]{1,0:T(8,128)S(1)} %collective-permute-done.4.ghost_ref, s32[4,128]{1,0:T(4,128)S(1)} %bitcast.15), custom_call_target="tpu_custom_call" | custom-call | tf_op jit(solution)/shard_map/add_returned/pallas_call | solution.py:705
Async XLA Ops:
  1.8 5.1 %collective-permute-start = (f32[24,256]{1,0:T(8,128)S(1)}, f32[24,256]{1,0:T(8,128)S(1)}, u32[]{:S(2)}, u32[]{:S(2)}) collective-permute-start(f32[24,256]{1,0:T(8,128)S(1)} %get-tuple-element.40), channel_id=1, source_target_pairs={{0,1},{1,2},{2,3},{3,4},{4,5},{5,6},{6,7},{7,0},{8,9},{9,10},{10,1... | collective-permute-start | bytes 73736 | tf_op jit(solution)/shard_map/ppermute | solution.py:618
  1.8 5.2 %collective-permute-start.1 = (f32[32,256]{1,0:T(8,128)S(1)}, f32[32,256]{1,0:T(8,128)S(1)}, u32[]{:S(2)}, u32[]{:S(2)}) collective-permute-start(f32[32,256]{1,0:T(8,128)S(1)} %get-tuple-element.41), channel_id=1, source_target_pairs={{0,7},{1,0},{2,1},{3,2},{4,3},{5,4},{6,5},{7,6},{8,15},{9,8},{10,9... | collective-permute-start | bytes 98312 | tf_op jit(solution)/shard_map/ppermute | solution.py:619
  7.5 15.4 %collective-permute-start.3 = (f32[25,8,256]{2,1,0:T(8,128)S(1)}, f32[25,8,256]{2,1,0:T(8,128)S(1)}, u32[]{:S(2)}, u32[]{:S(2)}) collective-permute-start(f32[25,8,256]{2,1,0:T(8,128)S(1)} %get-tuple-element.42.low_ref), channel_id=1, source_target_pairs={{0,120},{8,0},{16,8},{24,16},{32,24},{40,32},{48,40},{56,48},{64,5... | collective-permute-start | bytes 614408 | tf_op jit(solution)/shard_map/ppermute | solution.py:640
  12.8 10.1 %collective-permute-start.2 = (f32[24,8,256]{2,1,0:T(8,128)S(1)}, f32[24,8,256]{2,1,0:T(8,128)S(1)}, u32[]{:S(2)}, u32[]{:S(2)}) collective-permute-start(f32[24,8,256]{2,1,0:T(8,128)S(1)} %get-tuple-element.43.high_ref), channel_id=1, source_target_pairs={{0,8},{8,16},{16,24},{24,32},{32,40},{40,48},{48,56},{56,64},{64,7... | collective-permute-start | bytes 589832 | tf_op jit(solution)/shard_map/ppermute | solution.py:639
  26.8 18.8 %all-to-all-start = ((f32[128,8,128]{2,1,0:T(8,128)}), f32[128,8,128]{2,1,0:T(8,128)S(1)}, u32[]{:S(2)}, u32[]{:S(2)}) async-start(f32[128,8,128]{2,1,0:T(8,128)} %get-tuple-element.55), calls=%async_computation | async-start | bytes 1048576 | tf_op jit(solution)/shard_map/all_to_all | solution.py:694
  47.9 8.5 %collective-permute-start.4 = (f32[12,128]{1,0:T(8,128)S(1)}, f32[12,128]{1,0:T(8,128)S(1)}, u32[]{:S(2)}, u32[]{:S(2)}) collective-permute-start(f32[12,128]{1,0:T(8,128)S(1)} %get-tuple-element.65), channel_id=1, source_target_pairs={{0,1},{1,2},{2,3},{3,4},{4,5},{5,6},{6,7},{7,8},{8,9},{9,10},{10,1... | collective-permute-start | bytes 18440 | tf_op jit(solution)/shard_map/ppermute | solution.py:703
  48.0 8.5 %copy-start = (s32[512]{0:T(512)S(1)}, s32[512]{0:T(512)}, u32[]{:S(2)}) copy-start(s32[512]{0:T(512)} %param.26) | copy-start | bytes 6148

commit v9 on v8

--- a/solution.py
+++ b/solution.py
@@ -104,29 +104,38 @@
     backward_ref[30:32, :] = jnp.zeros((2, 256), jnp.float32)
 
 
-def pack_crest(sections, place_ref, head_ref, zone_ref, flux_ref, before_ref, after_ref, low_ref, high_ref):
+def pack_crest(sections, place_ref, head_ref, zone_ref, flux_ref, before_ref, after_ref, low_ref, high_ref, tail_ref):
     planes, rows = head_ref.shape[0], head_ref.shape[1]
     groups = rows // 8
     behind = jnp.where(place_ref[0] > 0, 1.0, 0.0)
     ahead = jnp.where(place_ref[0] < sections - 1, 1.0, 0.0)
-    zone_at = 2 * groups + 2
-    for x in range(planes):
-        target, plane = (low_ref, x) if x < 2 else (high_ref, x - 2)
-        for field in range(2):
+    zone_at = 2 * groups + 1
+    row = lax.broadcasted_iota(jnp.int32, (8, after_ref.shape[1]), 0)
+    for field in range(2):
+        tails = []
+        for x in range(planes):
+            target, plane = (low_ref, x) if x < 2 else (high_ref, x - 2)
             first = field * zone_at
             for group in range(groups):
                 at = slice(8 * group, 8 * group + 8)
                 own = head_ref[x, at, :] if field == 0 else zone_ref[x, at, :].astype(jnp.float32) + 1.0
                 target[first + plane * groups + group] = own
             at = field * WIDE * planes + WIDE * x
-            target[first + 2 * groups + plane] = jnp.concatenate(
-                [
-                    after_ref[at : at + WIDE, :] * ahead,
-                    jnp.zeros((2, after_ref.shape[1]), jnp.float32),
-                    before_ref[at : at + WIDE, :] * behind,
-                ],
-                axis=0,
+            tails.append(
+                jnp.concatenate(
+                    [
+                        after_ref[at : at + WIDE, :] * ahead,
+                        jnp.zeros((2, after_ref.shape[1]), jnp.float32),
+                        before_ref[at : at + WIDE, :] * behind,
+                    ],
+                    axis=0,
+                )
             )
+            tail_ref[field * planes + x] = tails[-1]
+        for target, near, next_one in ((low_ref, 0, 1), (high_ref, 3, 2)):
+            inner = jnp.where(row < 4, pltpu.roll(tails[next_one], 2, 0), pltpu.roll(tails[next_one], 6, 0))
+            shared = jnp.where((row == 2) | (row == 5), inner, tails[near])
+            target[field * zone_at + 2 * groups] = shared
     for group in range(groups):
         low_ref[2 * zone_at + group] = flux_ref[group]
         high_ref[2 * zone_at + group] = flux_ref[group]
@@ -206,17 +215,16 @@
         flux_ref[group] = r_near * r_far * (far - near)
 
 
-def prepare(tables_ref, low_ref, high_ref, h, alpha_f, less_f, m_f, root_f, gain_f, r_f, cap_f):
+def prepare(tables_ref, low_ref, high_ref, tail_ref, h, alpha_f, less_f, m_f, root_f, gain_f, r_f, cap_f):
     planes, groups = h.shape[0], h.shape[1] // 8 - 1
-    zone_at = 2 * groups + 2
+    zone_at = 2 * groups + 1
     out = (h, alpha_f, less_f, m_f, root_f, gain_f)
     for x in range(planes):
         source, plane = (low_ref, x) if x < 2 else (high_ref, x - 2)
         for group in range(groups):
             at = plane * groups + group
             fields(tables_ref, out, x, 8 * group, source[at], source[zone_at + at])
-        at = 2 * groups + plane
-        fields(tables_ref, out, x, 8 * groups, source[at], source[zone_at + at])
+        fields(tables_ref, out, x, 8 * groups, tail_ref[x], tail_ref[planes + x])
         r_f[x], cap_f[x] = retention(*(ref[x] for ref in out))
 
 
@@ -254,11 +262,18 @@
     total = planes + 2 * WIDE
     height, depth = h.shape[1], h.shape[2]
     groups = rows // 8
-    zone_at = 2 * groups + 2
+    zone_at = 2 * groups + 1
     lane8 = lax.broadcasted_iota(jnp.int32, (8, 128), 1)
     behind = jnp.where(place_ref[1] > 0, 1.0, 0.0)
     ahead = jnp.where(place_ref[1] < crests - 1, 1.0, 0.0)
     out = (h, alpha_f, less_f, m_f, root_f, gain_f)
+
+    row = lax.broadcasted_iota(jnp.int32, (8, depth), 0)
+
+    def tail_of(shared, near):
+        if near:
+            return jnp.where((row < 2) | (row > 5), shared, 0.0)
+        return jnp.where(row == 0, pltpu.roll(shared, 6, 0), jnp.where(row == 7, pltpu.roll(shared, 2, 0), 0.0))
 
     ends = []
     for source, first, inside in ((before_ref, 1, behind), (after_ref, WIDE + planes, ahead)):
@@ -266,8 +281,9 @@
             for group in range(groups):
                 at = plane * groups + group
                 fields(tables_ref, out, first + plane, 8 * group, source[at], source[zone_at + at] * inside)
-            at = 2 * groups + plane
-            fields(tables_ref, out, first + plane, rows, source[at], source[zone_at + at] * inside)
+            near = (first + plane) in (WIDE - 1, WIDE + planes)
+            head, zone = tail_of(source[2 * groups], near), tail_of(source[zone_at + 2 * groups], near)
+            fields(tables_ref, out, first + plane, rows, head, zone * inside)
         flux = [source[2 * zone_at + group] * inside for group in range(groups)]
         ends.append(jnp.concatenate(flux + [jnp.zeros((height - rows, depth), jnp.float32)], axis=0))
     for x in range(planes):
@@ -628,17 +644,17 @@
         [f32, i32, f32],
     )(head, zone, *(in_hbm(x) for x in (sent_columns[0].T, retention_alpha, retention_exponent, conductivity)))
 
-    edge = (2 * (2 * groups + 2) + groups, 8, depth)
-    low, high = call(
+    edge = (2 * (2 * groups + 1) + groups, 8, depth)
+    low, high, tails = call(
         functools.partial(pack_crest, section),
         [SM] + [VM] * 5,
-        [(edge[0] + 1, 8, depth), edge],
+        [(edge[0] + 1, 8, depth), edge, (2 * planes, 8, depth)],
         [],
         "pack_crest",
     )(place, head, zone, flux, before, after)
     west = lax.ppermute(high, "crest", steps(crest, 1))
     east = lax.ppermute(low, "crest", steps(crest, -1))
-    own = call(prepare, [VM] * 3, [(planes, height, depth)] * 8, [], "prepare")(tables, low, high)
+    own = call(prepare, [VM] * 4, [(planes, height, depth)] * 8, [], "prepare")(tables, low, high, tails)
 
     field = pltpu.VMEM((planes + 2 * WIDE, height, depth), f32)
     head_out, outgoing, order = call(

time: 57.5 us -> 57.2 us (level)
  no operation moved by 1% of the time
where the time goes in v9:
time: 57.2 us; the launch traced here: 56.9 us
  waiting for transfers between devices  27.6 us (48%)
  Pallas kernels  14.7 us (26%)
  starting transfers between devices  13.9 us (24%)
  between operations  0.7 us (1%)
    all_to_all x1, waiting for transfers between devices, per_device(): lax.all_to_all(outgoing, AXES, split_axis=0, concat_axis=0, tiled=True)  10.2 us
    ppermute x1, waiting for transfers between devices, per_device(): west = lax.ppermute(high, 'crest', steps(crest, 1))  9.3 us
    ppermute x1, waiting for transfers between devices, per_device(): returned = lax.ppermute(ghost, AXES, steps(devices, 1))  7.65 us
    ppermute x1, starting transfers between devices, per_device(): east = lax.ppermute(low, 'crest', steps(crest, -1))  5.28 us
    all_to_all x1, starting transfers between devices, per_device(): lax.all_to_all(outgoing, AXES, split_axis=0, concat_axis=0, tiled=True)  5.01 us
    pallas_call x1, Pallas kernels, per_device(): call(functools.partial(seepage, crest), [SM] + [VM] * 12, [pressure_head....  3.89 us
    ppermute x1, starting transfers between devices, per_device(): after = lax.ppermute(backward, 'section', steps(section, -1))  3.57 us
    pallas_call x1, Pallas kernels, per_device(): call(final_state, [VM] * 6, [(6, 8, elems), (8, elems), (24, elems), (12,...  2.38 us
  transfers between devices with their start and end apart: 6, of which 5 were waited for; matrix products, arithmetic and copies ran while one was open for 0% of the time, Pallas kernels for 10%

profile of v9, /device:TPU:0, one launch (start us, length us, event | category | flops | bytes accessed | tf_op | source)
XLA Modules:
  0.0 56.9 jit_solution(867417550015899702)
XLA Ops:
  0.6 1.1 %pack_section.1 = (f32[24,256]{1,0:T(8,128)S(1)}, f32[32,256]{1,0:T(8,128)S(1)}, f32[4,32,256]{2,1,0:T(8,128)S(1)}, s32[4,32,256]{2,1,0:T(8,128)S(1)}) custom-call(f32[4,32,256]{2,1,0:T(8,128)} %head_hbm.1, s32[4,32,256]{2,1,0:T(8,128)} %zone_hbm.1, f32[3,1024]{1,0:T(4,128)} %disp_hbm.3, s32[4,128]{1,0:T(4,128)} %bitcast.14), custom_call_target="tpu_custom_call" | custom-call | tf_op jit(solution)/shard_map/pack_section/pallas_call | solution.py:626
  1.8 0.0 collective-permute-start
  1.8 3.6 %collective-permute-start.1 = (f32[32,256]{1,0:T(8,128)S(1)}, f32[32,256]{1,0:T(8,128)S(1)}, u32[]{:S(2)}, u32[]{:S(2)}) collective-permute-start(f32[32,256]{1,0:T(8,128)S(1)} %get-tuple-element.42), channel_id=1, source_target_pairs={{0,7},{1,0},{2,1},{3,2},{4,3},{5,4},{6,5},{7,6},{8,15},{9,8},{10,9... | collective-permute-start | bytes 98312 | tf_op jit(solution)/shard_map/ppermute | solution.py:635
  5.4 0.1 pad_add_fusion.place_ref
  5.4 1.1 %inner_flux.1 = (f32[32,256]{1,0:T(8,128)S(1)}, s32[128,128]{1,0:T(8,128)S(1)}, f32[4,8,256]{2,1,0:T(8,128)S(1)}) custom-call(f32[4,32,256]{2,1,0:T(8,128)S(1)} %get-tuple-element.36.head_ref, s32[4,32,256]{2,1,0:T(8,128)S(1)} %get-tuple-element.37.zone_ref, s32[64,128]{1,0:T(8,128)} %bitcast.17, f32[8]{0:T(128)} %alpha_hbm.1, f32[8]{0:T(128)} %expo_hbm.1, ...), custom_call_target="tpu_custom_call" | custom-call | tf_op jit(solution)/shard_map/inner_flux/pallas_call | solution.py:638
  6.5 0.3 collective-permute-done.before_ref
  6.8 0.1 collective-permute-done.1.after_ref
  7.0 0.6 %pack_crest.1 = (f32[23,8,256]{2,1,0:T(8,128)S(1)}, f32[22,8,256]{2,1,0:T(8,128)S(1)}, f32[8,8,256]{2,1,0:T(8,128)S(1)}) custom-call(s32[3]{0:T(128)S(1)} %pad_add_fusion.place_ref, f32[4,32,256]{2,1,0:T(8,128)S(1)} %get-tuple-element.36.head_ref, s32[4,32,256]{2,1,0:T(8,128)S(1)} %get-tuple-element.37.zone_ref, ...), custom_call_target="tpu_custom_call" | custom-call | tf_op jit(solution)/shard_map/pack_crest/pallas_call | solution.py:648
  7.5 5.3 %collective-permute-start.3 = (f32[23,8,256]{2,1,0:T(8,128)S(1)}, f32[23,8,256]{2,1,0:T(8,128)S(1)}, u32[]{:S(2)}, u32[]{:S(2)}) collective-permute-start(f32[23,8,256]{2,1,0:T(8,128)S(1)} %get-tuple-element.43.low_ref), channel_id=1, source_target_pairs={{0,120},{8,0},{16,8},{24,16},{32,24},{40,32},{48,40},{56,48},{64,5... | collective-permute-start | bytes 565256 | tf_op jit(solution)/shard_map/ppermute | solution.py:656
  12.8 0.0 collective-permute-start.2
  12.8 0.5 prepare.1
  13.3 9.3 %collective-permute-done.2.before_ref = f32[22,8,256]{2,1,0:T(8,128)S(1)} collective-permute-done((f32[22,8,256]{2,1,0:T(8,128)S(1)}, f32[22,8,256]{2,1,0:T(8,128)S(1)}, u32[]{:S(2)}, u32[]{:S(2)}) %collective-permute-start.2) | collective-permute-done | bytes 180256 | tf_op jit(solution)/shard_map/ppermute | solution.py:655
  22.6 0.0 collective-permute-done.3.after_ref.tail_ref
  22.6 3.9 %seepage.1 = (f32[4,32,256]{2,1,0:T(8,128)}, f32[128,8,128]{2,1,0:T(8,128)}, f32[8,128]{1,0:T(8,128)S(1)}) custom-call(s32[3]{0:T(128)S(1)} %pad_add_fusion.place_ref, f32[32,256]{1,0:T(8,128)S(1)} %get-tuple-element.38.tables_ref, s32[128,128]{1,0:T(8,128)S(1)} %get-tuple-element.39.index, f32[4,40,256]{2,1,0:T(8,128)S(1)} %get-tuple-element.46.own_h, ...), custom_call_target="tpu_custom_call" | custom-call | tf_op jit(solution)/shard_map/seepage/pallas_call | solution.py:660
  26.5 5.0 %all-to-all-start = ((f32[128,8,128]{2,1,0:T(8,128)}), f32[128,8,128]{2,1,0:T(8,128)S(1)}, u32[]{:S(2)}, u32[]{:S(2)}) async-start(f32[128,8,128]{2,1,0:T(8,128)} %get-tuple-element.57), calls=%async_computation | async-start | bytes 1048576 | tf_op jit(solution)/shard_map/all_to_all | solution.py:710
  31.5 1.8 %selectors.1 = (f32[3,1024]{1,0:T(4,128)S(1)}, f32[6,8,1024]{2,1,0:T(8,128)S(1)}, s32[8,1024]{1,0:T(8,128)S(1)}, f32[48,24]{1,0:T(8,128)S(1)}, f32[24,48]{1,0:T(...) custom-call(s32[3]{0:T(128)S(1)} %pad_add_fusion.place_ref, f32[8,128]{1,0:T(8,128)S(1)} %get-tuple-element.55.order_ref, ...), custom_call_target="tpu_custom_call" | custom-call | tf_op jit(solution)/shard_map/selectors/pallas_call | solution.py:669
  33.3 1.8 %trial_state.1.trial_ref = f32[8,8,1024]{2,1,0:T(8,128)S(1)} custom-call(s32[3]{0:T(128)S(1)} %pad_add_fusion.place_ref, f32[48,24]{1,0:T(8,128)S(1)} %get-tuple-element.60.matrix_ref, f32[3,1024]{1,0:T(4,128)S(1)} %get-tuple-element.61.disp_ref, f32[32,256]{1,0:T(8,128)S(1)} %collective-permute-done.1.after_ref, ...), custom_call_target="tpu_custom_call" | custom-call | tf_op jit(solution)/shard_map/trial_state/pallas_call | solution.py:703
  35.0 10.2 %all-to-all-done = f32[128,8,128]{2,1,0:T(8,128)S(1)} async-done(((f32[128,8,128]{2,1,0:T(8,128)}), f32[128,8,128]{2,1,0:T(8,128)S(1)}, u32[]{:S(2)}, u32[]{:S(2)}) %all-to-all-start) | async-done | bytes 524320 | tf_op jit(solution)/shard_map/all_to_all | solution.py:710
  45.3 2.4 %final_state.1 = (f32[6,8,1024]{2,1,0:T(8,128)}, f32[8,1024]{1,0:T(8,128)}, f32[24,1024]{1,0:T(8,128)S(1)}, f32[12,128]{1,0:T(8,128)S(1)}) custom-call(f32[24,48]{1,0:T(8,128)S(1)} %get-tuple-element.56.matrix_ref, f32[1024,128]{1,0:T(8,128)S(1)} %bitcast.13, s32[2,1024]{1,0:T(2,128)S(1)} %get-tuple-element.58.at_ref, ...), custom_call_target="tpu_custom_call" | custom-call | tf_op jit(solution)/shard_map/final_state/pallas_call | solution.py:712
  47.6 0.0 collective-permute-start.4
  47.6 0.0 copy-start
  47.6 0.8 %own_forces.1.own_ref = f32[24,128]{1,0:T(8,128)S(1)} custom-call(f32[24,1024]{1,0:T(8,128)S(1)} %get-tuple-element.66.force_ref, s32[8,1024]{1,0:T(8,128)S(1)} %get-tuple-element.62.conn_ref), custom_call_target="tpu_custom_call" | custom-call | tf_op jit(solution)/shard_map/own_forces/pallas_call | solution.py:720
  48.5 7.7 %collective-permute-done.4.ghost_ref = f32[12,128]{1,0:T(8,128)S(1)} collective-permute-done((f32[12,128]{1,0:T(8,128)S(1)}, f32[12,128]{1,0:T(8,128)S(1)}, u32[]{:S(2)}, u32[]{:S(2)}) %collective-permute-start.4) | collective-permute-done | bytes 6176 | tf_op jit(solution)/shard_map/ppermute | solution.py:719
  56.1 0.0 copy-done
  56.1 0.8 %add_returned.1 = f32[3,1024]{1,0:T(4,128)} custom-call(f32[24,128]{1,0:T(8,128)S(1)} %own_forces.1.own_ref, f32[12,128]{1,0:T(8,128)S(1)} %collective-permute-done.4.ghost_ref, s32[4,128]{1,0:T(4,128)S(1)} %bitcast.15), custom_call_target="tpu_custom_call" | custom-call | tf_op jit(solution)/shard_map/add_returned/pallas_call | solution.py:721
Async XLA Ops:
  1.8 5.1 %collective-permute-start = (f32[24,256]{1,0:T(8,128)S(1)}, f32[24,256]{1,0:T(8,128)S(1)}, u32[]{:S(2)}, u32[]{:S(2)}) collective-permute-start(f32[24,256]{1,0:T(8,128)S(1)} %get-tuple-element.41), channel_id=1, source_target_pairs={{0,1},{1,2},{2,3},{3,4},{4,5},{5,6},{6,7},{7,0},{8,9},{9,10},{10,1... | collective-permute-start | bytes 73736 | tf_op jit(solution)/shard_map/ppermute | solution.py:634
  1.8 5.2 %collective-permute-start.1 = (f32[32,256]{1,0:T(8,128)S(1)}, f32[32,256]{1,0:T(8,128)S(1)}, u32[]{:S(2)}, u32[]{:S(2)}) collective-permute-start(f32[32,256]{1,0:T(8,128)S(1)} %get-tuple-element.42), channel_id=1, source_target_pairs={{0,7},{1,0},{2,1},{3,2},{4,3},{5,4},{6,5},{7,6},{8,15},{9,8},{10,9... | collective-permute-start | bytes 98312 | tf_op jit(solution)/shard_map/ppermute | solution.py:635
  7.5 15.0 %collective-permute-start.3 = (f32[23,8,256]{2,1,0:T(8,128)S(1)}, f32[23,8,256]{2,1,0:T(8,128)S(1)}, u32[]{:S(2)}, u32[]{:S(2)}) collective-permute-start(f32[23,8,256]{2,1,0:T(8,128)S(1)} %get-tuple-element.43.low_ref), channel_id=1, source_target_pairs={{0,120},{8,0},{16,8},{24,16},{32,24},{40,32},{48,40},{56,48},{64,5... | collective-permute-start | bytes 565256 | tf_op jit(solution)/shard_map/ppermute | solution.py:656
  12.8 9.8 %collective-permute-start.2 = (f32[22,8,256]{2,1,0:T(8,128)S(1)}, f32[22,8,256]{2,1,0:T(8,128)S(1)}, u32[]{:S(2)}, u32[]{:S(2)}) collective-permute-start(f32[22,8,256]{2,1,0:T(8,128)S(1)} %get-tuple-element.44.high_ref), channel_id=1, source_target_pairs={{0,8},{8,16},{16,24},{24,32},{32,40},{40,48},{48,56},{56,64},{64,7... | collective-permute-start | bytes 540680 | tf_op jit(solution)/shard_map/ppermute | solution.py:655
  26.5 18.8 %all-to-all-start = ((f32[128,8,128]{2,1,0:T(8,128)}), f32[128,8,128]{2,1,0:T(8,128)S(1)}, u32[]{:S(2)}, u32[]{:S(2)}) async-start(f32[128,8,128]{2,1,0:T(8,128)} %get-tuple-element.57), calls=%async_computation | async-start | bytes 1048576 | tf_op jit(solution)/shard_map/all_to_all | solution.py:710
  47.6 8.5 %collective-permute-start.4 = (f32[12,128]{1,0:T(8,128)S(1)}, f32[12,128]{1,0:T(8,128)S(1)}, u32[]{:S(2)}, u32[]{:S(2)}) collective-permute-start(f32[12,128]{1,0:T(8,128)S(1)} %get-tuple-element.67), channel_id=1, source_target_pairs={{0,1},{1,2},{2,3},{3,4},{4,5},{5,6},{6,7},{7,8},{8,9},{9,10},{10,1... | collective-permute-start | bytes 18440 | tf_op jit(solution)/shard_map/ppermute | solution.py:719
  47.6 8.5 %copy-start = (s32[512]{0:T(512)S(1)}, s32[512]{0:T(512)}, u32[]{:S(2)}) copy-start(s32[512]{0:T(512)} %param.26) | copy-start | bytes 6148

commit v10 on v9

--- a/solution.py
+++ b/solution.py
@@ -574,13 +574,16 @@
 HBM = pl.BlockSpec(memory_space=pltpu.HBM)
 
 
-def call(body, specs, outs, scratch, name, types=None):
+def call(body, specs, outs, scratch, name, types=None, pinned=()):
     types = types or [jnp.float32] * len(outs)
     return pl.pallas_call(
         body,
         in_specs=specs,
         out_specs=tuple(VM for _ in outs),
-        out_shape=tuple(jax.ShapeDtypeStruct(shape, kind) for shape, kind in zip(outs, types)),
+        out_shape=tuple(
+            (pltpu.VMEM if i in pinned else jax.ShapeDtypeStruct)(shape, kind)
+            for i, (shape, kind) in enumerate(zip(outs, types))
+        ),
         scratch_shapes=scratch,
         compiler_params=pltpu.CompilerParams(vmem_limit_bytes=VMEM_LIMIT),
         name=name,
@@ -663,6 +666,7 @@
         [pressure_head.shape, (devices, 8, 128), (8, 128)],
         [field] * 8 + [pltpu.VMEM((planes * rows, depth), f32), pltpu.VMEM((depth, planes * rows), f32)],
         "seepage",
+        pinned=(1,),
     )(place, tables, index, *own, west, east)
 
     matrix = component_major()

time: 57.2 us -> 57.2 us (level)
  no operation moved by 1% of the time
where the time goes in v10:
time: 57.2 us; the launch traced here: 56.9 us
  waiting for transfers between devices  27.6 us (48%)
  Pallas kernels  14.7 us (26%)
  starting transfers between devices  13.9 us (24%)
  between operations  0.7 us (1%)
    all_to_all x1, waiting for transfers between devices, per_device(): lax.all_to_all(outgoing, AXES, split_axis=0, concat_axis=0, tiled=True)  10.2 us
    ppermute x1, waiting for transfers between devices, per_device(): west = lax.ppermute(high, 'crest', steps(crest, 1))  9.3 us
    ppermute x1, waiting for transfers between devices, per_device(): returned = lax.ppermute(ghost, AXES, steps(devices, 1))  7.65 us
    ppermute x1, starting transfers between devices, per_device(): east = lax.ppermute(low, 'crest', steps(crest, -1))  5.28 us
    all_to_all x1, starting transfers between devices, per_device(): lax.all_to_all(outgoing, AXES, split_axis=0, concat_axis=0, tiled=True)  5.01 us
    pallas_call x1, Pallas kernels, per_device(): call(functools.partial(seepage, crest), [SM] + [VM] * 12, [pressure_head....  3.89 us
    ppermute x1, starting transfers between devices, per_device(): after = lax.ppermute(backward, 'section', steps(section, -1))  3.57 us
    pallas_call x1, Pallas kernels, per_device(): call(final_state, [VM] * 6, [(6, 8, elems), (8, elems), (24, elems), (12,...  2.38 us
  transfers between devices with their start and end apart: 6, of which 5 were waited for; matrix products, arithmetic and copies ran while one was open for 0% of the time, Pallas kernels for 10%

profile of v10, /device:TPU:0, one launch (start us, length us, event | category | flops | bytes accessed | tf_op | source)
XLA Modules:
  0.0 56.9 jit_solution(867417550015899702)
XLA Ops:
  0.6 1.1 %pack_section.1 = (f32[24,256]{1,0:T(8,128)S(1)}, f32[32,256]{1,0:T(8,128)S(1)}, f32[4,32,256]{2,1,0:T(8,128)S(1)}, s32[4,32,256]{2,1,0:T(8,128)S(1)}) custom-call(f32[4,32,256]{2,1,0:T(8,128)} %head_hbm.1, s32[4,32,256]{2,1,0:T(8,128)} %zone_hbm.1, f32[3,1024]{1,0:T(4,128)} %disp_hbm.3, s32[4,128]{1,0:T(4,128)} %bitcast.14), custom_call_target="tpu_custom_call" | custom-call | tf_op jit(solution)/shard_map/pack_section/pallas_call | solution.py:629
  1.8 0.0 collective-permute-start
  1.8 3.6 %collective-permute-start.1 = (f32[32,256]{1,0:T(8,128)S(1)}, f32[32,256]{1,0:T(8,128)S(1)}, u32[]{:S(2)}, u32[]{:S(2)}) collective-permute-start(f32[32,256]{1,0:T(8,128)S(1)} %get-tuple-element.42), channel_id=1, source_target_pairs={{0,7},{1,0},{2,1},{3,2},{4,3},{5,4},{6,5},{7,6},{8,15},{9,8},{10,9... | collective-permute-start | bytes 98312 | tf_op jit(solution)/shard_map/ppermute | solution.py:638
  5.4 0.1 pad_add_fusion.place_ref
  5.4 1.1 %inner_flux.1 = (f32[32,256]{1,0:T(8,128)S(1)}, s32[128,128]{1,0:T(8,128)S(1)}, f32[4,8,256]{2,1,0:T(8,128)S(1)}) custom-call(f32[4,32,256]{2,1,0:T(8,128)S(1)} %get-tuple-element.36.head_ref, s32[4,32,256]{2,1,0:T(8,128)S(1)} %get-tuple-element.37.zone_ref, s32[64,128]{1,0:T(8,128)} %bitcast.17, f32[8]{0:T(128)} %alpha_hbm.1, f32[8]{0:T(128)} %expo_hbm.1, ...), custom_call_target="tpu_custom_call" | custom-call | tf_op jit(solution)/shard_map/inner_flux/pallas_call | solution.py:641
  6.5 0.3 collective-permute-done.before_ref
  6.8 0.1 collective-permute-done.1.after_ref
  7.0 0.6 %pack_crest.1 = (f32[23,8,256]{2,1,0:T(8,128)S(1)}, f32[22,8,256]{2,1,0:T(8,128)S(1)}, f32[8,8,256]{2,1,0:T(8,128)S(1)}) custom-call(s32[3]{0:T(128)S(1)} %pad_add_fusion.place_ref, f32[4,32,256]{2,1,0:T(8,128)S(1)} %get-tuple-element.36.head_ref, s32[4,32,256]{2,1,0:T(8,128)S(1)} %get-tuple-element.37.zone_ref, ...), custom_call_target="tpu_custom_call" | custom-call | tf_op jit(solution)/shard_map/pack_crest/pallas_call | solution.py:651
  7.5 5.3 %collective-permute-start.3 = (f32[23,8,256]{2,1,0:T(8,128)S(1)}, f32[23,8,256]{2,1,0:T(8,128)S(1)}, u32[]{:S(2)}, u32[]{:S(2)}) collective-permute-start(f32[23,8,256]{2,1,0:T(8,128)S(1)} %get-tuple-element.43.low_ref), channel_id=1, source_target_pairs={{0,120},{8,0},{16,8},{24,16},{32,24},{40,32},{48,40},{56,48},{64,5... | collective-permute-start | bytes 565256 | tf_op jit(solution)/shard_map/ppermute | solution.py:659
  12.8 0.0 collective-permute-start.2
  12.8 0.5 prepare.1
  13.3 9.3 %collective-permute-done.2.before_ref = f32[22,8,256]{2,1,0:T(8,128)S(1)} collective-permute-done((f32[22,8,256]{2,1,0:T(8,128)S(1)}, f32[22,8,256]{2,1,0:T(8,128)S(1)}, u32[]{:S(2)}, u32[]{:S(2)}) %collective-permute-start.2) | collective-permute-done | bytes 180256 | tf_op jit(solution)/shard_map/ppermute | solution.py:658
  22.6 0.0 collective-permute-done.3.after_ref.tail_ref
  22.6 3.9 %seepage.1 = (f32[4,32,256]{2,1,0:T(8,128)}, f32[128,8,128]{2,1,0:T(8,128)}, f32[8,128]{1,0:T(8,128)S(1)}) custom-call(s32[3]{0:T(128)S(1)} %pad_add_fusion.place_ref, f32[32,256]{1,0:T(8,128)S(1)} %get-tuple-element.38.tables_ref, s32[128,128]{1,0:T(8,128)S(1)} %get-tuple-element.39.index, f32[4,40,256]{2,1,0:T(8,128)S(1)} %get-tuple-element.46.own_h, ...), custom_call_target="tpu_custom_call" | custom-call | tf_op jit(solution)/shard_map/seepage/pallas_call | solution.py:663
  26.5 5.0 %all-to-all-start = ((f32[128,8,128]{2,1,0:T(8,128)}), f32[128,8,128]{2,1,0:T(8,128)S(1)}, u32[]{:S(2)}, u32[]{:S(2)}) async-start(f32[128,8,128]{2,1,0:T(8,128)} %get-tuple-element.57), calls=%async_computation | async-start | bytes 1048576 | tf_op jit(solution)/shard_map/all_to_all | solution.py:714
  31.5 1.8 %selectors.1 = (f32[3,1024]{1,0:T(4,128)S(1)}, f32[6,8,1024]{2,1,0:T(8,128)S(1)}, s32[8,1024]{1,0:T(8,128)S(1)}, f32[48,24]{1,0:T(8,128)S(1)}, f32[24,48]{1,0:T(...) custom-call(s32[3]{0:T(128)S(1)} %pad_add_fusion.place_ref, f32[8,128]{1,0:T(8,128)S(1)} %get-tuple-element.55.order_ref, ...), custom_call_target="tpu_custom_call" | custom-call | tf_op jit(solution)/shard_map/selectors/pallas_call | solution.py:673
  33.3 1.8 %trial_state.1.trial_ref = f32[8,8,1024]{2,1,0:T(8,128)S(1)} custom-call(s32[3]{0:T(128)S(1)} %pad_add_fusion.place_ref, f32[48,24]{1,0:T(8,128)S(1)} %get-tuple-element.60.matrix_ref, f32[3,1024]{1,0:T(4,128)S(1)} %get-tuple-element.61.disp_ref, f32[32,256]{1,0:T(8,128)S(1)} %collective-permute-done.1.after_ref, ...), custom_call_target="tpu_custom_call" | custom-call | tf_op jit(solution)/shard_map/trial_state/pallas_call | solution.py:707
  35.0 10.2 %all-to-all-done = f32[128,8,128]{2,1,0:T(8,128)S(1)} async-done(((f32[128,8,128]{2,1,0:T(8,128)}), f32[128,8,128]{2,1,0:T(8,128)S(1)}, u32[]{:S(2)}, u32[]{:S(2)}) %all-to-all-start) | async-done | bytes 524320 | tf_op jit(solution)/shard_map/all_to_all | solution.py:714
  45.3 2.4 %final_state.1 = (f32[6,8,1024]{2,1,0:T(8,128)}, f32[8,1024]{1,0:T(8,128)}, f32[24,1024]{1,0:T(8,128)S(1)}, f32[12,128]{1,0:T(8,128)S(1)}) custom-call(f32[24,48]{1,0:T(8,128)S(1)} %get-tuple-element.56.matrix_ref, f32[1024,128]{1,0:T(8,128)S(1)} %bitcast.13, s32[2,1024]{1,0:T(2,128)S(1)} %get-tuple-element.58.at_ref, ...), custom_call_target="tpu_custom_call" | custom-call | tf_op jit(solution)/shard_map/final_state/pallas_call | solution.py:716
  47.6 0.0 collective-permute-start.4
  47.6 0.0 copy-start
  47.6 0.8 %own_forces.1.own_ref = f32[24,128]{1,0:T(8,128)S(1)} custom-call(f32[24,1024]{1,0:T(8,128)S(1)} %get-tuple-element.66.force_ref, s32[8,1024]{1,0:T(8,128)S(1)} %get-tuple-element.62.conn_ref), custom_call_target="tpu_custom_call" | custom-call | tf_op jit(solution)/shard_map/own_forces/pallas_call | solution.py:724
  48.5 7.7 %collective-permute-done.4.ghost_ref = f32[12,128]{1,0:T(8,128)S(1)} collective-permute-done((f32[12,128]{1,0:T(8,128)S(1)}, f32[12,128]{1,0:T(8,128)S(1)}, u32[]{:S(2)}, u32[]{:S(2)}) %collective-permute-start.4) | collective-permute-done | bytes 6176 | tf_op jit(solution)/shard_map/ppermute | solution.py:723
  56.1 0.0 copy-done
  56.1 0.8 %add_returned.1 = f32[3,1024]{1,0:T(4,128)} custom-call(f32[24,128]{1,0:T(8,128)S(1)} %own_forces.1.own_ref, f32[12,128]{1,0:T(8,128)S(1)} %collective-permute-done.4.ghost_ref, s32[4,128]{1,0:T(4,128)S(1)} %bitcast.15), custom_call_target="tpu_custom_call" | custom-call | tf_op jit(solution)/shard_map/add_returned/pallas_call | solution.py:725
Async XLA Ops:
  1.8 5.1 %collective-permute-start = (f32[24,256]{1,0:T(8,128)S(1)}, f32[24,256]{1,0:T(8,128)S(1)}, u32[]{:S(2)}, u32[]{:S(2)}) collective-permute-start(f32[24,256]{1,0:T(8,128)S(1)} %get-tuple-element.41), channel_id=1, source_target_pairs={{0,1},{1,2},{2,3},{3,4},{4,5},{5,6},{6,7},{7,0},{8,9},{9,10},{10,1... | collective-permute-start | bytes 73736 | tf_op jit(solution)/shard_map/ppermute | solution.py:637
  1.8 5.2 %collective-permute-start.1 = (f32[32,256]{1,0:T(8,128)S(1)}, f32[32,256]{1,0:T(8,128)S(1)}, u32[]{:S(2)}, u32[]{:S(2)}) collective-permute-start(f32[32,256]{1,0:T(8,128)S(1)} %get-tuple-element.42), channel_id=1, source_target_pairs={{0,7},{1,0},{2,1},{3,2},{4,3},{5,4},{6,5},{7,6},{8,15},{9,8},{10,9... | collective-permute-start | bytes 98312 | tf_op jit(solution)/shard_map/ppermute | solution.py:638
  7.5 15.0 %collective-permute-start.3 = (f32[23,8,256]{2,1,0:T(8,128)S(1)}, f32[23,8,256]{2,1,0:T(8,128)S(1)}, u32[]{:S(2)}, u32[]{:S(2)}) collective-permute-start(f32[23,8,256]{2,1,0:T(8,128)S(1)} %get-tuple-element.43.low_ref), channel_id=1, source_target_pairs={{0,120},{8,0},{16,8},{24,16},{32,24},{40,32},{48,40},{56,48},{64,5... | collective-permute-start | bytes 565256 | tf_op jit(solution)/shard_map/ppermute | solution.py:659
  12.8 9.8 %collective-permute-start.2 = (f32[22,8,256]{2,1,0:T(8,128)S(1)}, f32[22,8,256]{2,1,0:T(8,128)S(1)}, u32[]{:S(2)}, u32[]{:S(2)}) collective-permute-start(f32[22,8,256]{2,1,0:T(8,128)S(1)} %get-tuple-element.44.high_ref), channel_id=1, source_target_pairs={{0,8},{8,16},{16,24},{24,32},{32,40},{40,48},{48,56},{56,64},{64,7... | collective-permute-start | bytes 540680 | tf_op jit(solution)/shard_map/ppermute | solution.py:658
  26.5 18.8 %all-to-all-start = ((f32[128,8,128]{2,1,0:T(8,128)}), f32[128,8,128]{2,1,0:T(8,128)S(1)}, u32[]{:S(2)}, u32[]{:S(2)}) async-start(f32[128,8,128]{2,1,0:T(8,128)} %get-tuple-element.57), calls=%async_computation | async-start | bytes 1048576 | tf_op jit(solution)/shard_map/all_to_all | solution.py:714
  47.6 8.5 %collective-permute-start.4 = (f32[12,128]{1,0:T(8,128)S(1)}, f32[12,128]{1,0:T(8,128)S(1)}, u32[]{:S(2)}, u32[]{:S(2)}) collective-permute-start(f32[12,128]{1,0:T(8,128)S(1)} %get-tuple-element.67), channel_id=1, source_target_pairs={{0,1},{1,2},{2,3},{3,4},{4,5},{5,6},{6,7},{7,8},{8,9},{9,10},{10,1... | collective-permute-start | bytes 18440 | tf_op jit(solution)/shard_map/ppermute | solution.py:723
  47.6 8.5 %copy-start = (s32[512]{0:T(512)S(1)}, s32[512]{0:T(512)}, u32[]{:S(2)}) copy-start(s32[512]{0:T(512)} %param.26) | copy-start | bytes 6148
